TPU v7x, 256 devices: a whole 4x4x8 slice. The times are simulated.
256 devices in a mesh: row: 64 (over y, z, core), node: 4 (over x).
Axes of the slice: x: 4, y: 4, z: 8, core: 2. Of those that a mesh axis runs over, the one named last changes fastest.
Arguments:
- probes: float32 [32, 65536], P(None, 'row'), may hold values from -6 to 6
- diag_blocks: float32 [512, 128, 128], P('row'), may hold values from -0.1875 to 0.1875
- couplings: float32 [512, 3, 128, 128], P('row'), may hold values from -0.1875 to 0.1875
- neighbours: int32 [512, 3], P('row'), may hold values from 0 to 511, as said below
Outputs:
- moments: float32 [16, 32, 65536], P('node', None, 'row')
- projected: float32 [16, 32, 32], P('node')
Inputs may be any that keep to these rules, and one draw needn't show every extreme that they name: (neighbours[i, f] - i) modulo 512 lies in 1 to 4, and equals 4 for some entry.
All inputs are finite; a program needn't handle non-finite values.
Results may differ from a plain program's by a relative error of at most 0.0002.
Values sent between devices are 32-bit elements; how exact they have to be, the bound alone decides.
No kernel may reach another device: no remote copies, remote signals or barrier semaphores. Data moves between devices by JAX's collectives and lax.ppermute only.
A program may use at most 64 MiB of HBM per device.

v0:
```python
import jax
import jax.numpy as jnp
from jax import lax
from jax.sharding import PartitionSpec as P

NODES = 8
MOMENTS = 16
REACH = 4
ITERS = 4


highest = lax.Precision.HIGHEST


def from_behind(value, axis, steps):
    count = lax.axis_size(axis)
    pairs = [(source, (source + steps) % count) for source in range(count)]
    return lax.ppermute(value, axis, pairs)


def node_gram(left, right):
    return jnp.einsum("bnlr,bnmr->nlm", left, right, precision=highest)


def combine_cols(vectors, coeffs):
    return jnp.einsum("bnlr,nlm->bnmr", vectors, coeffs, precision=highest)


def single_solve(matrix, target):
    return jax.scipy.linalg.cho_solve((jnp.linalg.cholesky(matrix), True), target)


def system_solve(matrices, targets):
    return jax.vmap(single_solve)(matrices, targets)


def shards(probes, diag_blocks, couplings, neighbours):
    block_count = diag_blocks.shape[0]
    block_size = diag_blocks.shape[1]
    probe_count = probes.shape[0]
    row_devices = lax.axis_size("row")
    node_devices = lax.axis_size("node")
    node_share = NODES // node_devices
    moment_share = MOMENTS // node_devices
    node_ids = lax.axis_index("node") * node_share + jnp.arange(node_share, dtype=jnp.int32)
    angles = jnp.pi * (node_ids.astype(jnp.float32) + 0.5) / NODES
    shift_real = jnp.cos(angles)
    shift_imag = jnp.sin(angles)
    imag_square = shift_imag * shift_imag
    symmetric = 0.5 * (diag_blocks + jnp.swapaxes(diag_blocks, 1, 2))
    first_block = lax.axis_index("row") * block_count + jnp.arange(block_count, dtype=jnp.int32)
    offsets = (neighbours - first_block[:, None]) % (block_count * row_devices)
    local_cols = jnp.arange(block_count, dtype=jnp.int32)[:, None] + offsets
    targets_all = jnp.arange(block_count + REACH, dtype=jnp.int32)
    selector = (local_cols[:, :, None] == targets_all[None, None, :]).astype(jnp.float32)
    width = node_share * probe_count

    def apply_hamiltonian(vectors):
        flat = vectors.reshape(block_count, width, block_size)
        ahead = from_behind(flat[:REACH], "row", -1)
        pushed = jnp.einsum("bcr,bfrs->bfcs", flat, couplings, precision=highest)
        spilled = jnp.einsum("bfk,bfcs->kcs", selector, pushed, precision=highest)
        arrived = from_behind(spilled[block_count:], "row", 1)
        extended = jnp.concatenate([flat, ahead], axis=0)
        gathered = jnp.take(extended, local_cols, axis=0)
        result = jnp.einsum("bcs,brs->bcr", flat, symmetric, precision=highest)
        result = result + jnp.einsum("bfcs,bfrs->bcr", gathered, couplings, precision=highest)
        result = result + spilled[:block_count]
        result = jnp.concatenate([result[:REACH] + arrived, result[REACH:]], axis=0)
        return result.reshape(vectors.shape)

    def shifted(vectors):
        return apply_hamiltonian(vectors) - shift_real[None, :, None, None] * vectors

    def residual_gram(vectors):
        return lax.psum(node_gram(vectors, vectors), "row")

    seeds = probes.reshape(probe_count, block_count, block_size).transpose(1, 0, 2)
    residual = jnp.broadcast_to(seeds[:, None], (block_count, node_share, probe_count, block_size))
    direction = residual
    solution = jnp.zeros_like(residual)
    gram_now = residual_gram(residual)
    for iteration in range(ITERS):
        once = shifted(direction)
        image = shifted(once) + imag_square[None, :, None, None] * direction
        curvature = lax.psum(node_gram(direction, image), "row")
        alpha = system_solve(curvature, gram_now)
        solution = solution + combine_cols(direction, alpha)
        if iteration + 1 < ITERS:
            residual = residual - combine_cols(image, alpha)
            gram_next = residual_gram(residual)
            beta = system_solve(gram_now, gram_next)
            direction = residual + combine_cols(direction, beta)
            gram_now = gram_next
    applied = shifted(solution)
    orders = jnp.arange(MOMENTS, dtype=jnp.float32)[:, None] + 1.0
    weight_real = jnp.cos(orders * angles[None, :]) / 8.0
    weight_imag = jnp.sin(orders * angles[None, :]) * shift_imag[None, :] / 8.0
    terms = jnp.einsum("kn,bnlr->klbr", weight_imag, solution, precision=highest)
    terms = terms - jnp.einsum("kn,bnlr->klbr", weight_real, applied, precision=highest)
    summed = lax.psum(terms.reshape(MOMENTS, probe_count, block_count * block_size), "node")
    moments = lax.dynamic_slice_in_dim(
        summed, lax.axis_index("node") * moment_share, moment_share, 0
    )
    order_total = block_count * block_size * row_devices
    local_projection = jnp.einsum("lr,kmr->klm", probes, moments, precision=highest) / order_total
    projected = lax.psum(local_projection, "row")
    return (moments, projected)


def solution(mesh):
    placed = (P(None, "row"), P("row", None, None), P("row", None, None, None), P("row", None))
    return jax.shard_map(
        shards,
        mesh=mesh,
        in_specs=placed,
        out_specs=(P("node", None, "row"), P("node", None, None)),
        check_vma=False,
    )
```

profile of v0, /device:TPU:1, one launch (start us, length us, event | category | flops | bytes accessed | tf_op | source)
XLA Modules:
  0.0 2306.4 jit_solution(6871018585321540976)
XLA Ops:
  27.5 6.1 collective-permute-start.2
  43.1 250.4 %all-reduce = (f32[2,32,32]{1,2,0:T(8,128)S(1)}, f32[2,32,32]{1,2,0:T(8,128)S(1)}) all-reduce(f32[2,32,32]{1,2,0:T(8,128)S(1)} %convolution_bitcast_fusion.47, f32[2,32,32]{1,2,0:T(8,128)S(1)} %convolution_bitcast_fusion.48), channel_id=1, replica_groups=mesh['row'=64,'node'=4] {'row'}, use_global_device_ids=true, to_apply=%region_3.6 | all-reduce | flops 4096 | bytes 32768 | tf_op jit(solution)/shard_map/psum | solution.py:76
  293.5 5.9 custom-call.20
  299.5 5.9 custom-call.22
  305.7 4.9 custom-call.23
  310.6 4.9 custom-call.21
  317.0 246.1 %psum.72 = f32[2,32,32]{1,2,0:T(8,128)S(1)} all-reduce(f32[2,32,32]{1,2,0:T(8,128)S(1)} %convolution_bitcast_fusion.46), channel_id=1, replica_groups=mesh['row'=64,'node'=4] {'row'}, use_global_device_ids=true, to_apply=%region_4.8 | all-reduce | flops 2048 | bytes 16384 | tf_op jit(solution)/shard_map/psum | solution.py:76
  566.9 6.5 custom-call.26
  573.4 5.7 collective-permute-start.4
  584.4 3.4 fusion.14
  598.0 3.4 fusion.12
  602.8 248.8 %psum.73 = f32[2,32,32]{1,2,0:T(8,128)S(1)} all-reduce(f32[2,32,32]{1,2,0:T(8,128)S(1)} %convolution_bitcast_fusion.45), channel_id=1, replica_groups=mesh['row'=64,'node'=4] {'row'}, use_global_device_ids=true, to_apply=%region_5.9 | all-reduce | flops 2048 | bytes 16384 | tf_op jit(solution)/shard_map/psum | solution.py:86
  851.7 5.9 custom-call.24
  858.0 4.9 custom-call.27
  862.9 4.9 custom-call.25
  869.9 246.5 %psum.74 = f32[2,32,32]{1,2,0:T(8,128)S(1)} all-reduce(f32[2,32,32]{1,2,0:T(8,128)S(1)} %convolution_bitcast_fusion.44), channel_id=1, replica_groups=mesh['row'=64,'node'=4] {'row'}, use_global_device_ids=true, to_apply=%region_6.10 | all-reduce | flops 2048 | bytes 16384 | tf_op jit(solution)/shard_map/psum | solution.py:76
  1121.4 6.5 custom-call.30
  1128.9 5.7 collective-permute-start.8
  1140.6 3.4 fusion.10
  1154.2 3.5 fusion.8
  1158.3 248.6 %psum.75 = f32[2,32,32]{1,2,0:T(8,128)S(1)} all-reduce(f32[2,32,32]{1,2,0:T(8,128)S(1)} %convolution_bitcast_fusion.43), channel_id=1, replica_groups=mesh['row'=64,'node'=4] {'row'}, use_global_device_ids=true, to_apply=%region_7.11 | all-reduce | flops 2048 | bytes 16384 | tf_op jit(solution)/shard_map/psum | solution.py:86
  1407.0 5.9 custom-call.28
  1413.2 4.9 custom-call.31
  1418.1 4.9 custom-call.29
  1425.1 246.1 %psum.76 = f32[2,32,32]{2,1,0:T(8,128)S(1)} all-reduce(f32[2,32,32]{2,1,0:T(8,128)S(1)} %convolution_bitcast_fusion.42), channel_id=1, replica_groups=mesh['row'=64,'node'=4] {'row'}, use_global_device_ids=true, to_apply=%region_8.12 | all-reduce | flops 2048 | bytes 16384 | tf_op jit(solution)/shard_map/psum | solution.py:76
  1675.0 5.7 collective-permute-start.12
  1704.0 248.0 %psum.77 = f32[2,32,32]{1,2,0:T(8,128)S(1)} all-reduce(f32[2,32,32]{1,2,0:T(8,128)S(1)} %convolution_bitcast_fusion.41), channel_id=1, replica_groups=mesh['row'=64,'node'=4] {'row'}, use_global_device_ids=true, to_apply=%region_9.13 | all-reduce | flops 2048 | bytes 16384 | tf_op jit(solution)/shard_map/psum | solution.py:86
  1952.0 5.9 custom-call.32
  1958.1 4.9 custom-call.33
  1966.2 5.7 collective-permute-start.16
  1989.1 61.5 %all-reduce.3.cloned.1.call-done = f32[16,32,1024]{2,1,0:T(8,128)} async-done(((f32[16,32,1024]{2,1,0:T(8,128)}), f32[16,32,1024]{2,1,0:T(8,128)}) %all-reduce.3.cloned.1.call-update) | async-done | bytes 2097168 | tf_op jit(solution)/shard_map/psum | solution.py:101
  2052.3 246.0 %psum.79 = f32[4,32,32]{1,2,0:T(8,128)S(1)} all-reduce(f32[4,32,32]{1,2,0:T(8,128)S(1)} %fusion.24), channel_id=1, replica_groups=mesh['row'=64,'node'=4] {'row'}, use_global_device_ids=true, to_apply=%region_11.15 | all-reduce | flops 4096 | bytes 32768 | tf_op jit(solution)/shard_map/psum | solution.py:107
  (340 shorter events, 128.7 us)
Async XLA Ops:
  7.2 2043.5 %all-reduce.3.cloned.1.call-start = ((), (), s32[]{:S(2)}) async-start(), calls=%async_computation | async-start | bytes 4194304 | tf_op jit(solution)/shard_map/psum | solution.py:101
  9.0 11.4 collective-permute-start
  16.3 10.0 collective-permute-start.1
  20.1 17.9 copy-start.27
  27.5 9.0 collective-permute-start.2
  35.7 6.8 collective-permute-start.3
  573.4 9.5 collective-permute-start.4
  581.6 6.3 collective-permute-start.5
  590.2 4.5 collective-permute-start.6
  592.8 8.6 collective-permute-start.7
  601.4 256.2 %copy-start.26 = (f32[2,32,32]{2,1,0:T(8,128)S(1)}, f32[2,32,32]{2,1,0:T(8,128)}, u32[]{:S(2)}) copy-start(f32[2,32,32]{2,1,0:T(8,128)} %custom-call.26) | copy-start | bytes 24580
  601.4 266.4 %copy-start.19 = (f32[2,32,32]{1,2,0:T(8,128)S(1)}, f32[2,32,32]{1,2,0:T(8,128)}, u32[]{:S(2)}) copy-start(f32[2,32,32]{1,2,0:T(8,128)} %copy-done.18) | copy-start | bytes 24580
  1127.9 10.1 copy-start.14
  1128.9 10.2 collective-permute-start.8
  1138.0 6.0 collective-permute-start.9
  1148.0 4.7 collective-permute-start.10
  1150.7 7.1 collective-permute-start.11
  1157.8 255.1 %copy-start.25 = (f32[2,32,32]{2,1,0:T(8,128)S(1)}, f32[2,32,32]{2,1,0:T(8,128)}, u32[]{:S(2)}) copy-start(f32[2,32,32]{2,1,0:T(8,128)} %custom-call.30) | copy-start | bytes 24580
  1157.8 265.3 %copy-start.17 = (f32[2,32,32]{1,2,0:T(8,128)S(1)}, f32[2,32,32]{1,2,0:T(8,128)}, u32[]{:S(2)}) copy-start(f32[2,32,32]{1,2,0:T(8,128)} %copy-done.16) | copy-start | bytes 24580
  1423.6 248.5 %copy-start.20 = (f32[2,32,32,1]{1,2,3,0:T(8,128)}, f32[2,32,32,1]{1,2,3,0:T(8,128)S(1)}, u32[]{:S(2)}) copy-start(f32[2,32,32,1]{1,2,3,0:T(8,128)S(1)} %convolution_bitcast_fusion.36) | copy-start | bytes 24580
  1673.3 10.1 copy-start.12
  1673.3 10.1 copy-start.21
  1675.0 9.5 collective-permute-start.12
  1683.2 5.2 collective-permute-start.13
  1692.9 5.6 collective-permute-start.14
  1696.7 5.8 collective-permute-start.15
  1702.5 260.6 %copy-start.23 = (f32[2,32,32]{2,1,0:T(8,128)S(1)}, f32[2,32,32]{2,1,0:T(8,128)}, u32[]{:S(2)}) copy-start(f32[2,32,32]{2,1,0:T(8,128)} %copy-done.22) | copy-start | bytes 24580
  1702.5 261.1 %copy-start.13 = (f32[2,32,8,128]{3,1,2,0:T(8,128)S(1)}, f32[2,32,8,128]{3,1,2,0:T(8,128)}, u32[]{:S(2)}) copy-start(f32[2,32,8,128]{3,1,2,0:T(8,128)} %convolution_add_fusion.1) | copy-start | bytes 786436
  1966.2 11.5 collective-permute-start.16
  1972.5 9.1 collective-permute-start.17
  1989.1 62.6 %copy-start.11 = (f32[32,1024]{1,0:T(8,128)S(1)}, f32[32,1024]{1,0:T(8,128)}, u32[]{:S(2)}) copy-start(f32[32,1024]{1,0:T(8,128)} %param.9) | copy-start | bytes 393220
  2051.8 247.3 %copy-start.5 = (f32[4,32,1024]{2,1,0:T(8,128)}, f32[4,32,1024]{2,1,0:T(8,128)S(1)}, u32[]{:S(2)}) copy-start(f32[4,32,1024]{2,1,0:T(8,128)S(1)} %constant_dynamic-slice_fusion) | copy-start | bytes 1572868
  (35 other events, 127.7 us)
Sparse Core Ops, SparseCore 0:
  1989.2 61.3 all-reduce.2
where the time goes:
time: 2320 us; the launch traced here: 2310 us
  blocking collectives  1980 us (85%)
  other arithmetic  88.7 us (4%)
  matrix products  83.8 us (4%)
  waiting for transfers between devices  61.6 us (3%)
  starting transfers between devices  40.2 us (2%)
  local copies, waits for them, and re-layouts  35.4 us (2%)
    psum x4, blocking collectives, residual_gram(): return lax.psum(node_gram(vectors, vectors), 'row')  989 us
    psum x3, blocking collectives, shards(): curvature = lax.psum(node_gram(direction, image), 'row')  745 us
    psum x1, blocking collectives, shards(): projected = lax.psum(local_projection, 'row')  246 us
    psum x1, waiting for transfers between devices, shards(): lax.psum(terms.reshape(MOMENTS, probe_count, block_count * block_size), '...  61.5 us
  transfers between devices with their start and end apart: 19, of which 2 were waited for; matrix products, arithmetic and copies ran while one was open for 3% of the time, Pallas kernels for 0%

commit v1 on v0

v1 whole, which is shorter than its diff:
```python
import functools
import math

import jax
import jax.numpy as jnp
import numpy as np
from jax import lax
from jax.experimental import pallas as pl
from jax.experimental.pallas import tpu as pltpu
from jax.sharding import PartitionSpec as P

NODES = 8
MOMENTS = 16
REACH = 4
ITERS = 4
PROBES = 32
BLOCK = 128
ROWS = 1024
HALF = 512
TILE = 256
DEGREE = 2 * ITERS - 1
BLOCKS = 512
ORDER_DIM = BLOCKS * BLOCK
SCALE = 16.0

f32 = jnp.float32
bf16 = jnp.bfloat16
highest = lax.Precision.HIGHEST

VMEM = pl.BlockSpec(memory_space=pltpu.VMEM)
SMEM = pl.BlockSpec(memory_space=pltpu.SMEM)


HBM = pl.BlockSpec(memory_space=pltpu.HBM)


def call(body, outs, in_specs, flops=0, bytes_accessed=0, vmem=8, scratch=()):
    return pl.pallas_call(
        body,
        out_shape=outs,
        in_specs=in_specs,
        out_specs=jax.tree.map(lambda _: VMEM, outs),
        scratch_shapes=scratch,
        compiler_params=pltpu.CompilerParams(vmem_limit_bytes=vmem << 20),
        cost_estimate=pl.CostEstimate(flops=flops, bytes_accessed=bytes_accessed, transcendentals=0),
    )


def halves(value):
    high = value.astype(bf16)
    return high, (value - high.astype(f32)).astype(bf16)


def stacked(value):
    high, low = halves(value)
    return jnp.concatenate([high, low], axis=0)


def dot_nn(left, right):
    return lax.dot_general(left, right, (((1,), (0,)), ((), ())), preferred_element_type=f32)


def dot_nt(left, right):
    return lax.dot_general(left, right, (((1,), (1,)), ((), ())), preferred_element_type=f32)


def fold(double):
    return double[:PROBES] + double[PROBES:]


def product(dot, pair, high, low):
    return fold(dot(pair, high)) + dot(pair[:PROBES], low)


def payloads(parity, near, spill, pay_core, pay_chip):
    even = parity == 0
    pay_core[...] = jnp.where(even, spill, near)
    pay_chip[...] = jnp.where(even, near, spill)


def cross_out(tail, uhi, ulo):
    pair = stacked(tail)
    first = product(dot_nn, pair, uhi[:, :TILE], ulo[:, :TILE])
    second = product(dot_nn, pair[:, TILE:], uhi[TILE:, TILE:], ulo[TILE:, TILE:])
    return jnp.concatenate([first, second], axis=1)


def cross_in(ahead, uhi, ulo):
    pair = stacked(ahead)
    first = product(dot_nt, pair[:, :TILE], uhi[:TILE, :TILE], ulo[:TILE, :TILE])
    second = product(dot_nt, pair, uhi[TILE:, :], ulo[TILE:, :])
    return jnp.concatenate([first, second], axis=1)


def band_block(step, row, neighbours, position, diag, coup):
    if step == 0:
        return diag * (0.5 / SCALE)
    block = jnp.zeros((BLOCK, BLOCK), f32)
    for f in range(neighbours.shape[0]):
        distance = (neighbours[f, row] - (position * 8 + row)) & (BLOCKS - 1)
        block = block + jnp.where(distance == step, coup[f], 0.0)
    return block * (1.0 / SCALE)


def cross_rows(i, neighbours, position, coup, uhi, ulo):
    zero = jnp.zeros((BLOCK, BLOCK), bf16)
    rows = pl.ds((i - 4) * BLOCK, BLOCK)
    for col in range(4):
        cols = pl.ds(col * BLOCK, BLOCK)
        if i + REACH < 8 + col:
            uhi[rows, cols] = zero
            ulo[rows, cols] = zero
        else:
            block = band_block(8 + col - i, i, neighbours, position, None, coup)
            uhi[rows, cols], ulo[rows, cols] = halves(block)


def cross_body(neighbours, position, coup_hbm, x_hbm, pay_core, pay_chip, coup, x, uhi, ulo, sems):
    copies = [pltpu.make_async_copy(coup_hbm.at[i], coup.at[i - 4], sems.at[i - 4]) for i in (7, 6, 5, 4)]
    for copy in copies:
        copy.start()
    load = pltpu.make_async_copy(x_hbm, x, sems.at[4])
    load.start()
    for i, copy in zip((7, 6, 5, 4), copies):
        copy.wait()
        cross_rows(i, neighbours, position[0], coup.at[i - 4], uhi, ulo)
    load.wait()
    payloads(position[0] & 1, x[:, :HALF], cross_out(x[:, HALF:], uhi, ulo), pay_core, pay_chip)


def gram_of(x, before):
    both = jnp.concatenate([before, x], axis=0)
    return lax.dot_general(x, both, (((1,), (1,)), ((), ())), precision=highest, preferred_element_type=f32)


def first_body(neighbours, position, diag, coup, x, thi, tlo, uhi, ulo, local, gram):
    zero = jnp.zeros((BLOCK, BLOCK), bf16)
    for i in range(8):
        tile, part = divmod(i, 2)
        rows = pl.ds(part * BLOCK, BLOCK)
        for col in range(min(6, 8 - 2 * tile)):
            cols = pl.ds(col * BLOCK, BLOCK)
            step = col - part
            if 0 <= step <= REACH:
                block = band_block(step, i, neighbours, position[0], diag[i] if step == 0 else None, coup.at[i])
                thi[tile, rows, cols], tlo[tile, rows, cols] = halves(block)
            else:
                thi[tile, rows, cols] = zero
                tlo[tile, rows, cols] = zero
        if i >= 4:
            cross_rows(i, neighbours, position[0], coup.at[i], uhi, ulo)
    local_body(x, x, thi, tlo, local, gram)


def local_body(x, before, thi, tlo, local, gram):
    value = x[...]
    gram[...] = gram_of(value, before[...])
    pair = stacked(value)
    wide = [jnp.zeros((2 * PROBES, TILE), f32) for _ in range(4)]
    thin = [jnp.zeros((PROBES, TILE), f32) for _ in range(4)]
    for row in range(4):
        for col in range(row, min(row + 3, 4)):
            at = slice((col - row) * TILE, (col - row + 1) * TILE)
            high, low = thi[row, :, at], tlo[row, :, at]
            from_row, from_col = pair[:, row * TILE:(row + 1) * TILE], pair[:, col * TILE:(col + 1) * TILE]
            wide[col] = wide[col] + dot_nn(from_row, high)
            thin[col] = thin[col] + dot_nn(from_row[:PROBES], low)
            wide[row] = wide[row] + dot_nt(from_col, high)
            thin[row] = thin[row] + dot_nt(from_col[:PROBES], low)
    for tile in range(4):
        local[:, tile * TILE:(tile + 1) * TILE] = fold(wide[tile]) + thin[tile]


def join_body(parity, local, got_core, got_chip, uhi, ulo, out, *pay):
    even = parity[0] & 1 == 0
    ahead = jnp.where(even, got_core[...], got_chip[...])
    arrived = jnp.where(even, got_chip[...], got_core[...])
    near = local[:, :HALF] + arrived
    tail = local[:, HALF:] + cross_in(ahead, uhi, ulo)
    out[:, :HALF] = near
    out[:, HALF:] = tail
    if pay:
        payloads(parity[0] & 1, near, cross_out(tail, uhi, ulo), *pay)


def last_gram_body(x, before, gram):
    gram[...] = gram_of(x[...], before[...])


def dot_f32(left, right):
    return lax.dot_general(left, right, (((1,), (0,)), ((), ())), precision=highest, preferred_element_type=f32)


WIDTH = NODES * PROBES
PANEL = 8


def invert(matrix):
    rows = lax.broadcasted_iota(jnp.int32, (PROBES, WIDTH), 0)
    lanes = lax.broadcasted_iota(jnp.int32, (PROBES, WIDTH), 1) % PROBES
    group = lax.broadcasted_iota(jnp.int32, (PROBES, BLOCK), 1) // PROBES * PROBES
    for start in range(0, PROBES, PANEL):
        columns = [
            jnp.concatenate(
                [jnp.take_along_axis(matrix[:, h:h + BLOCK], group + k, axis=1) for h in range(0, WIDTH, BLOCK)], axis=1
            )
            for k in range(start, start + PANEL)
        ]
        for m in range(PANEL):
            k = start + m
            on_row, on_lane = rows == k, lanes == k
            inverse = 1.0 / columns[m][k:k + 1]
            factor = jnp.where(on_row, -1.0, columns[m])
            scaled = jnp.where(on_lane[:1], 1.0, matrix[k:k + 1]) * inverse
            matrix = jnp.where(on_lane | on_row, 0.0, matrix) - factor * scaled
            for q in range(m + 1, PANEL):
                columns[q] = jnp.where(on_row, 0.0, columns[q]) - factor * (columns[q][k:k + 1] * inverse)
    return matrix


def node_diagonal():
    return (
        lax.broadcasted_iota(jnp.int32, (WIDTH, WIDTH), 0) // PROBES
        == lax.broadcasted_iota(jnp.int32, (WIDTH, WIDTH), 1) // PROBES
    )


def node_shifts():
    node = lax.broadcasted_iota(jnp.int32, (1, WIDTH), 1) // PROBES
    cosine = jnp.zeros((1, WIDTH), f32)
    square = jnp.zeros((1, WIDTH), f32)
    for j in range(NODES):
        angle = math.pi * (j + 0.5) / NODES
        cosine = jnp.where(node == j, np.float32(math.cos(angle)), cosine)
        square = jnp.where(node == j, np.float32(math.sin(angle) ** 2), square)
    return cosine, square


def grown(coeffs, blocks=1):
    return jnp.concatenate([coeffs, jnp.zeros((blocks * PROBES, WIDTH), f32)], axis=0)


def sunk(coeffs, cosine):
    below = jnp.concatenate([jnp.zeros((PROBES, WIDTH), f32), coeffs], axis=0)
    return SCALE * below - cosine * grown(coeffs)


def raised(against, cosine):
    return SCALE * against[PROBES:] - cosine * against[:-PROBES]


class Nodes:
    def __init__(self):
        self.diagonal = node_diagonal()
        self.cosine, self.square = node_shifts()

    def blocks(self, full):
        masked = jnp.where(self.diagonal, full, 0.0)
        return sum(masked[j * PROBES:(j + 1) * PROBES] for j in range(NODES))

    def spread(self, matrix):
        return jnp.where(self.diagonal, jnp.concatenate([matrix] * NODES, axis=0), 0.0)

    def inner(self, left, against):
        return self.blocks(dot_f32(left.T, against[:left.shape[0]]))

    def image(self, direction, dir_against):
        once, once_against = sunk(direction, self.cosine), raised(dir_against, self.cosine)
        image = sunk(once, self.cosine) + self.square * grown(direction, 2)
        image_against = raised(once_against, self.cosine) + self.square * dir_against[:-2 * PROBES]
        return image, image_against

    def step(self, state, last):
        direction, residual, dir_against, res_against, solution = state
        size = direction.shape[0]
        image, image_against = self.image(direction, dir_against)
        if size == PROBES:
            curvature, now = image_against[:size], res_against[:size]
        else:
            turned = direction.T
            curvature = self.blocks(dot_f32(turned, image_against[:size]))
            now = self.blocks(dot_f32(turned, res_against[:size]))
        inverse = invert(curvature)
        alpha = self.spread(dot_f32(inverse, self.spread(now)))
        if last:
            return grown(solution, 2) + dot_f32(direction, alpha)
        moved = dot_f32(jnp.concatenate([direction, image, image_against], axis=0), alpha)
        part = size + image.shape[0]
        solution = moved[:size] if solution is None else grown(solution, 2) + moved[:size]
        residual = grown(residual, 2) - moved[size:part]
        res_against = res_against[:-2 * PROBES] - moved[part:]
        beta = self.spread(dot_f32(inverse, self.spread(self.inner(image, res_against))))
        count = res_against.shape[0]
        moved = dot_f32(jnp.concatenate([direction, dir_against[:count]], axis=0), beta)
        direction = residual - grown(moved[:size], 2)
        dir_against = res_against - moved[size:]
        return direction, residual, dir_against, res_against, solution


def moment_coeffs(nodes, weights, first, share, solution):
    applied = sunk(solution, nodes.cosine)
    row = lax.broadcasted_iota(jnp.int32, (PROBES, share * PROBES), 0)
    lane = lax.broadcasted_iota(jnp.int32, (PROBES, share * PROBES), 1)
    imag, real = [], []
    for j in range(NODES):
        for part, (table, sign) in ((imag, (0, 1.0)), (real, (1, -1.0))):
            block = jnp.zeros((PROBES, share * PROBES), f32)
            for k in range(share):
                block = jnp.where(lane == row + k * PROBES, sign * weights[table, first + k, j], block)
            part.append(block)
    left = jnp.concatenate([grown(solution), applied], axis=1)
    return dot_f32(left, jnp.concatenate(imag + real, axis=0))


def moments_body(node, weights, gram, k0, k1, k2, k3, k4, k5, k6, k7, moments, projected):
    nodes = Nodes()
    count = 2 * DEGREE + 1
    against = jnp.concatenate(
        [jnp.concatenate([gram[:, (a + 1) * PROBES:(a + 2) * PROBES]] * NODES, axis=1) for a in range(count)], axis=0
    )
    eye = (
        lax.broadcasted_iota(jnp.int32, (PROBES, WIDTH), 0)
        == lax.broadcasted_iota(jnp.int32, (PROBES, WIDTH), 1) % PROBES
    ).astype(f32)
    state = (eye, eye, against, against, None)
    for iteration in range(ITERS):
        state = nodes.step(state, iteration + 1 == ITERS)
    share = moments.shape[0]
    coeffs = moment_coeffs(nodes, weights, node[0] * share, share, state)
    basis = jnp.concatenate([k[...] for k in (k0, k1, k2, k3, k4, k5, k6, k7)], axis=0)
    moments[...] = dot_f32(coeffs.T, basis).reshape(share, PROBES, ROWS)
    onto = dot_f32(gram[:, PROBES:PROBES * (DEGREE + 2)], coeffs) * (1.0 / ORDER_DIM)
    for k in range(share):
        projected[k] = onto[:, k * PROBES:(k + 1) * PROBES]


def exchange(value, partner):
    count = lax.axis_size("row")
    return lax.ppermute(value, "row", [(source, partner(source) % count) for source in range(count)])


def core_partner(i):
    return i ^ 1


def chip_partner(i):
    return i + 1 if i % 2 else i - 1


def ring_partner(stage, i):
    y, z, core = i // 16, i // 2 % 8, i % 2
    if stage < 3:
        z = (z ^ 1, z ^ 2, (6, 7, 4, 5, 2, 3, 0, 1)[z])[stage]
    else:
        y = (y ^ 1, y ^ 3)[stage - 3]
    return y * 16 + z * 2 + core


def reduce_rows(value, parity):
    half = value.shape[0] // 2
    mine = lax.dynamic_slice_in_dim(value, parity * half, half, 0)
    other = lax.dynamic_slice_in_dim(value, (1 - parity) * half, half, 0)
    mine = mine + exchange(other, core_partner)
    for stage in range(5):
        mine = mine + exchange(mine, functools.partial(ring_partner, stage))
    other = exchange(mine, core_partner)
    first = jnp.where(parity == 0, mine, other)
    second = jnp.where(parity == 0, other, mine)
    return jnp.concatenate([first, second], axis=0)


def moment_weights():
    orders = np.arange(MOMENTS)[:, None] + 1.0
    angles = np.pi * (np.arange(NODES)[None, :] + 0.5) / NODES
    imag = np.sin(orders * angles) * np.sin(angles) / 8.0
    real = np.cos(orders * angles) / 8.0
    return np.stack([imag, real]).astype(np.float32)


def shards(probes, diag_blocks, couplings, neighbours):
    moment_share = MOMENTS // lax.axis_size("node")
    position = lax.axis_index("row")
    parity = position % 2
    flag = position.reshape(1)
    node = lax.axis_index("node").reshape(1)
    near_by = neighbours.T
    def array(*shape, kind=f32):
        return jax.ShapeDtypeStruct(shape, kind)

    message = array(PROBES, HALF)
    cross = (array(HALF, HALF, kind=bf16),) * 2
    pay_core, pay_chip = call(
        cross_body,
        (message, message),
        [SMEM, SMEM, HBM, HBM],
        vmem=56,
        scratch=[
            pltpu.VMEM((4, 3, BLOCK, BLOCK), f32),
            pltpu.VMEM((PROBES, ROWS), f32),
            pltpu.VMEM((HALF, HALF), bf16),
            pltpu.VMEM((HALF, HALF), bf16),
            pltpu.SemaphoreType.DMA((5,)),
        ],
    )(near_by, flag, couplings, probes)
    vector = array(PROBES, ROWS)
    pair = array(PROBES, 2 * PROBES)
    basis = [probes]
    grams = []
    for degree in range(DEGREE):
        got_core = exchange(pay_core, core_partner)
        got_chip = exchange(pay_chip, chip_partner)
        if degree == 0:
            thi, tlo, uhi, ulo, local, gram = call(
                first_body,
                (array(4, TILE, 3 * TILE, kind=bf16),) * 2 + cross + (vector, pair),
                [SMEM, SMEM, VMEM, VMEM, VMEM],
                flops=10**9,
                bytes_accessed=4 << 20,
                vmem=16,
            )(near_by, flag, diag_blocks, couplings, probes)
        else:
            local, gram = call(local_body, (vector, pair), [VMEM] * 4, flops=10**9, bytes_accessed=4 << 20)(
                basis[-1], basis[-2], thi, tlo
            )
        grams.append(gram)
        more = degree + 1 < DEGREE
        value, *pay = call(
            join_body,
            (vector, message, message) if more else (vector,),
            [SMEM] + [VMEM] * 5,
            flops=10**8,
            bytes_accessed=2 << 20,
        )(flag, local, got_core, got_chip, uhi, ulo)
        if more:
            pay_core, pay_chip = pay
        basis.append(value)
    grams.append(call(last_gram_body, array(PROBES, 2 * PROBES), [VMEM] * 2)(basis[-1], basis[-2]))
    total = reduce_rows(jnp.concatenate(grams, axis=1), parity)
    moments, projected = call(
        moments_body,
        (array(moment_share, PROBES, ROWS), array(moment_share, PROBES, PROBES)),
        [SMEM, SMEM] + [VMEM] * 9,
        vmem=24,
    )(node, jnp.asarray(moment_weights()), total, *basis)
    return (moments, projected)


def solution(mesh):
    placed = (P(None, "row"), P("row", None, None), P("row", None, None, None), P("row", None))
    return jax.shard_map(
        shards,
        mesh=mesh,
        in_specs=placed,
        out_specs=(P("node", None, "row"), P("node", None, None)),
        check_vma=False,
    )
```

time: 2320 us -> 110 us (0.05)
  blocking collectives: 1980 us -> 0 us
  other arithmetic: 88.7 us -> 0.05 us
  matrix products: 83.8 us -> 0 us
  Pallas kernels: 0 us -> 37.3 us
  local copies, waits for them, and re-layouts: 35.4 us -> 1.17 us
  waiting for transfers between devices: 61.6 us -> 33.9 us
    psum x8 -> x0, blocking collectives: 1980 us -> none  [the longest x4 989 us: residual_gram(): return lax.psum(node_gram(vectors, vectors), 'row')]
    dot_general x57 -> x0, matrix products: 80.4 us -> none  [the longest x9 30.6 us: apply_hamiltonian(): jnp.einsum('bfcs,bfrs->bcr', gathered, couplings, precision=highest)]
    another operation x31 -> x0, other arithmetic: 78 us -> none  [the longest x19 43.3 us: single_solve(): jnp.linalg.cholesky(matrix)]
    psum x1 -> x0, waiting for transfers between devices: 61.5 us -> none  [shards(): lax.psum(terms.reshape(MOMENTS, probe_count, block_count * block_size), '...]
    pallas_call x0 -> x17, Pallas kernels: none -> 37.3 us  [the longest x1 19.5 us: shards(): call(moments_body, (array(moment_share, PROBES, ROWS), array(moment_share...]
    ppermute x18 -> x21, waiting for transfers between devices: 0.11 us -> 33.9 us  [exchange(): lax.ppermute(value, 'row', [(source, partner(source) % count) for source...]
  transfers between devices with their start and end apart: 19 -> 21, of which waited for: 2 -> 14; matrix products, arithmetic and copies ran while one was open for 3% -> 0% of each run, Pallas kernels for 0% -> 9%
where the time goes in v1:
time: 110 us
  Pallas kernels  37.3 us (34%)
  starting transfers between devices  37 us (34%)
  waiting for transfers between devices  33.9 us (31%)
  local copies, waits for them, and re-layouts  1.17 us (1%)
    ppermute x21, starting transfers between devices, exchange(): lax.ppermute(value, 'row', [(source, partner(source) % count) for source...  37 us
    ppermute x21, waiting for transfers between devices, exchange(): lax.ppermute(value, 'row', [(source, partner(source) % count) for source...  33.9 us
    pallas_call x1, Pallas kernels, shards(): call(moments_body, (array(moment_share, PROBES, ROWS), array(moment_share...  19.5 us
    pallas_call x6, Pallas kernels, shards(): call(local_body, (vector, pair), [VMEM] * 4, flops=10 ** 9, bytes_accesse...  8.1 us
    pallas_call x7, Pallas kernels, shards(): call(join_body, (vector, message, message) if more else (vector,), [SMEM]...  4.09 us
    pallas_call x1, Pallas kernels, shards(): call(cross_body, (message, message), [SMEM, SMEM, HBM, HBM], vmem=56, scr...  3.01 us
    pallas_call x1, Pallas kernels, shards(): call(first_body, (array(4, TILE, 3 * TILE, kind=bf16),) * 2 + cross + (ve...  2.38 us
  transfers between devices with their start and end apart: 21, of which 14 were waited for; matrix products, arithmetic and copies ran while one was open for 0% of the time, Pallas kernels for 9%

profile of v1, /device:TPU:1, one launch (start us, length us, event | category | flops | bytes accessed | tf_op | source)
XLA Modules:
  0.0 110.3 jit_solution(17248393106512350122)
XLA Ops:
  0.7 3.0 %shard_map.69 = (f32[32,512]{1,0:T(8,128)}, f32[32,512]{1,0:T(8,128)}) custom-call(s32[3,8]{1,0:T(4,128)} %bitcast.3, s32[1]{0:T(128)} %bitcast.2.position.parity, f32[8,3,128,128]{3,2,1,0:T(8,128)} %coup_hbm.1, f32[32,1024]{1,0:T(8,128)} %k0.1), custom_call_target="tpu_custom_call" | custom-call | tf_op jit(solution)/shard_map/pallas_call | solution.py:392
  3.7 3.3 %collective-permute-start = (f32[32,512]{1,0:T(8,128)}, f32[32,512]{1,0:T(8,128)S(1)}, u32[]{:S(2)}, u32[]{:S(2)}) collective-permute-start(f32[32,512]{1,0:T(8,128)} %get-tuple-element.42), channel_id=1, source_target_pairs={{0,4},{4,0},{8,12},{12,8},{16,20},{20,16},{24,28},{28,24},{32,36},... | collective-permute-start | bytes 196616 | tf_op jit(solution)/shard_map/ppermute | solution.py:339
  7.0 1.0 copy-done.4
  8.1 2.4 %shard_map.68 = (bf16[4,256,768]{2,1,0:T(8,128)(2,1)S(1)}, bf16[4,256,768]{2,1,0:T(8,128)(2,1)S(1)}, bf16[512,512]{1,0:T(8,128)(2,1)S(1)}, bf16[512,512]{1,0:T(8...) custom-call(s32[3,8]{1,0:T(4,128)S(1)} %bitcast.4, s32[1]{0:T(128)} %bitcast.2.position.parity, ...), custom_call_target="tpu_custom_call" | custom-call | flops 1000000000 | bytes 4194304 | tf_op jit(solution)/shard_map/pallas_call | solution.py:413
  11.5 6.3 %collective-permute-start.2 = (f32[32,512]{1,0:T(8,128)S(1)}, f32[32,512]{1,0:T(8,128)S(1)}, u32[]{:S(2)}, u32[]{:S(2)}) collective-permute-start(f32[32,512]{1,0:T(8,128)S(1)} %get-tuple-element.51), channel_id=1, source_target_pairs={{0,4},{4,0},{8,12},{12,8},{16,20},{20,16},{24,28},{28,24},{32,36},... | collective-permute-start | bytes 196616 | tf_op jit(solution)/shard_map/ppermute | solution.py:339
  17.8 1.4 %shard_map.71 = (f32[32,1024]{1,0:T(8,128)S(1)}, f32[32,64]{1,0:T(8,128)S(1)}) custom-call(f32[32,1024]{1,0:T(8,128)S(1)} %get-tuple-element.46.x.before.k1, f32[32,1024]{1,0:T(8,128)S(1)} %copy-done.1, bf16[4,256,768]{2,1,0:T(8,128)(2,1)S(1)} %get-tuple-element.47.thi, bf16[4,256,768]{2,1,0:T(8,128)(2,1)S(1)} %get-tuple-element.48.tlo), custom_call_target="tpu_custom_call" | custom-call | flops 1000000000 | bytes 4194304 | tf_op jit(solution)/shard_map/pallas_call | solution.py:422
  19.2 2.3 %collective-permute-done.3.got_chip = f32[32,512]{1,0:T(8,128)S(1)} collective-permute-done((f32[32,512]{1,0:T(8,128)S(1)}, f32[32,512]{1,0:T(8,128)S(1)}, u32[]{:S(2)}, u32[]{:S(2)}) %collective-permute-start.3) | collective-permute-done | bytes 65568 | tf_op jit(solution)/shard_map/ppermute | solution.py:339
  22.2 3.5 %collective-permute-start.4 = (f32[32,512]{1,0:T(8,128)S(1)}, f32[32,512]{1,0:T(8,128)S(1)}, u32[]{:S(2)}, u32[]{:S(2)}) collective-permute-start(f32[32,512]{1,0:T(8,128)S(1)} %get-tuple-element.56), channel_id=1, source_target_pairs={{0,4},{4,0},{8,12},{12,8},{16,20},{20,16},{24,28},{28,24},{32,36},... | collective-permute-start | bytes 196616 | tf_op jit(solution)/shard_map/ppermute | solution.py:339
  25.6 1.3 %shard_map.73 = (f32[32,1024]{1,0:T(8,128)S(1)}, f32[32,64]{1,0:T(8,128)S(1)}) custom-call(f32[32,1024]{1,0:T(8,128)S(1)} %get-tuple-element.53.x.before.k2, f32[32,1024]{1,0:T(8,128)S(1)} %get-tuple-element.46.x.before.k1, bf16[4,256,768]{2,1,0:T(8,128)(2,1)S(1)} %get-tuple-element.47.thi, bf16[4,256,768]{2,1,0:T(8,128)(2,1)S(1)} %get-tuple-element.48.tlo), custom_call_target="tpu_custom_call" | custom-call | flops 1000000000 | bytes 4194304 | tf_op jit(solution)/shard_map/pallas_call | solution.py:422
  27.0 2.3 %collective-permute-done.5.got_chip = f32[32,512]{1,0:T(8,128)S(1)} collective-permute-done((f32[32,512]{1,0:T(8,128)S(1)}, f32[32,512]{1,0:T(8,128)S(1)}, u32[]{:S(2)}, u32[]{:S(2)}) %collective-permute-start.5) | collective-permute-done | bytes 65568 | tf_op jit(solution)/shard_map/ppermute | solution.py:339
  29.9 3.5 %collective-permute-start.6 = (f32[32,512]{1,0:T(8,128)S(1)}, f32[32,512]{1,0:T(8,128)S(1)}, u32[]{:S(2)}, u32[]{:S(2)}) collective-permute-start(f32[32,512]{1,0:T(8,128)S(1)} %get-tuple-element.61), channel_id=1, source_target_pairs={{0,4},{4,0},{8,12},{12,8},{16,20},{20,16},{24,28},{28,24},{32,36},... | collective-permute-start | bytes 196616 | tf_op jit(solution)/shard_map/ppermute | solution.py:339
  33.4 1.3 %shard_map.75 = (f32[32,1024]{1,0:T(8,128)S(1)}, f32[32,64]{1,0:T(8,128)S(1)}) custom-call(f32[32,1024]{1,0:T(8,128)S(1)} %get-tuple-element.58.x.before.k3, f32[32,1024]{1,0:T(8,128)S(1)} %get-tuple-element.53.x.before.k2, bf16[4,256,768]{2,1,0:T(8,128)(2,1)S(1)} %get-tuple-element.47.thi, bf16[4,256,768]{2,1,0:T(8,128)(2,1)S(1)} %get-tuple-element.48.tlo), custom_call_target="tpu_custom_call" | custom-call | flops 1000000000 | bytes 4194304 | tf_op jit(solution)/shard_map/pallas_call | solution.py:422
  34.8 2.3 %collective-permute-done.7.got_chip = f32[32,512]{1,0:T(8,128)S(1)} collective-permute-done((f32[32,512]{1,0:T(8,128)S(1)}, f32[32,512]{1,0:T(8,128)S(1)}, u32[]{:S(2)}, u32[]{:S(2)}) %collective-permute-start.7) | collective-permute-done | bytes 65568 | tf_op jit(solution)/shard_map/ppermute | solution.py:339
  37.7 3.5 %collective-permute-start.8 = (f32[32,512]{1,0:T(8,128)S(1)}, f32[32,512]{1,0:T(8,128)S(1)}, u32[]{:S(2)}, u32[]{:S(2)}) collective-permute-start(f32[32,512]{1,0:T(8,128)S(1)} %get-tuple-element.66), channel_id=1, source_target_pairs={{0,4},{4,0},{8,12},{12,8},{16,20},{20,16},{24,28},{28,24},{32,36},... | collective-permute-start | bytes 196616 | tf_op jit(solution)/shard_map/ppermute | solution.py:339
  41.2 1.3 %shard_map.77 = (f32[32,1024]{1,0:T(8,128)S(1)}, f32[32,64]{1,0:T(8,128)S(1)}) custom-call(f32[32,1024]{1,0:T(8,128)S(1)} %get-tuple-element.63.x.before.k4, f32[32,1024]{1,0:T(8,128)S(1)} %get-tuple-element.58.x.before.k3, bf16[4,256,768]{2,1,0:T(8,128)(2,1)S(1)} %get-tuple-element.47.thi, bf16[4,256,768]{2,1,0:T(8,128)(2,1)S(1)} %get-tuple-element.48.tlo), custom_call_target="tpu_custom_call" | custom-call | flops 1000000000 | bytes 4194304 | tf_op jit(solution)/shard_map/pallas_call | solution.py:422
  42.6 2.3 %collective-permute-done.9.got_chip = f32[32,512]{1,0:T(8,128)S(1)} collective-permute-done((f32[32,512]{1,0:T(8,128)S(1)}, f32[32,512]{1,0:T(8,128)S(1)}, u32[]{:S(2)}, u32[]{:S(2)}) %collective-permute-start.9) | collective-permute-done | bytes 65568 | tf_op jit(solution)/shard_map/ppermute | solution.py:339
  45.5 3.6 %collective-permute-start.10 = (f32[32,512]{1,0:T(8,128)S(1)}, f32[32,512]{1,0:T(8,128)S(1)}, u32[]{:S(2)}, u32[]{:S(2)}) collective-permute-start(f32[32,512]{1,0:T(8,128)S(1)} %get-tuple-element.71), channel_id=1, source_target_pairs={{0,4},{4,0},{8,12},{12,8},{16,20},{20,16},{24,28},{28,24},{32,36},... | collective-permute-start | bytes 196616 | tf_op jit(solution)/shard_map/ppermute | solution.py:339
  49.2 1.4 %shard_map.79 = (f32[32,1024]{1,0:T(8,128)S(1)}, f32[32,64]{1,0:T(8,128)S(1)}) custom-call(f32[32,1024]{1,0:T(8,128)S(1)} %get-tuple-element.68.x.before.k5, f32[32,1024]{1,0:T(8,128)S(1)} %get-tuple-element.63.x.before.k4, bf16[4,256,768]{2,1,0:T(8,128)(2,1)S(1)} %get-tuple-element.47.thi, bf16[4,256,768]{2,1,0:T(8,128)(2,1)S(1)} %get-tuple-element.48.tlo), custom_call_target="tpu_custom_call" | custom-call | flops 1000000000 | bytes 4194304 | tf_op jit(solution)/shard_map/pallas_call | solution.py:422
  50.5 2.3 %collective-permute-done.11.got_chip = f32[32,512]{1,0:T(8,128)S(1)} collective-permute-done((f32[32,512]{1,0:T(8,128)S(1)}, f32[32,512]{1,0:T(8,128)S(1)}, u32[]{:S(2)}, u32[]{:S(2)}) %collective-permute-start.11) | collective-permute-done | bytes 65568 | tf_op jit(solution)/shard_map/ppermute | solution.py:339
  53.5 3.5 %collective-permute-start.12 = (f32[32,512]{1,0:T(8,128)S(1)}, f32[32,512]{1,0:T(8,128)S(1)}, u32[]{:S(2)}, u32[]{:S(2)}) collective-permute-start(f32[32,512]{1,0:T(8,128)S(1)} %get-tuple-element.76), channel_id=1, source_target_pairs={{0,4},{4,0},{8,12},{12,8},{16,20},{20,16},{24,28},{28,24},{32,36},... | collective-permute-start | bytes 196616 | tf_op jit(solution)/shard_map/ppermute | solution.py:339
  56.9 1.4 %shard_map.81 = (f32[32,1024]{1,0:T(8,128)S(1)}, f32[32,64]{1,0:T(8,128)S(1)}) custom-call(f32[32,1024]{1,0:T(8,128)S(1)} %get-tuple-element.73.x.before.k6, f32[32,1024]{1,0:T(8,128)S(1)} %get-tuple-element.68.x.before.k5, bf16[4,256,768]{2,1,0:T(8,128)(2,1)S(1)} %get-tuple-element.47.thi, bf16[4,256,768]{2,1,0:T(8,128)(2,1)S(1)} %get-tuple-element.48.tlo), custom_call_target="tpu_custom_call" | custom-call | flops 1000000000 | bytes 4194304 | tf_op jit(solution)/shard_map/pallas_call | solution.py:422
  58.3 2.3 %collective-permute-done.13.got_chip = f32[32,512]{1,0:T(8,128)S(1)} collective-permute-done((f32[32,512]{1,0:T(8,128)S(1)}, f32[32,512]{1,0:T(8,128)S(1)}, u32[]{:S(2)}, u32[]{:S(2)}) %collective-permute-start.13) | collective-permute-done | bytes 65568 | tf_op jit(solution)/shard_map/ppermute | solution.py:339
  61.4 3.5 %collective-permute-start.14 = (f32[16,512]{1,0:T(8,128)S(1)}, f32[16,512]{1,0:T(8,128)S(1)}, u32[]{:S(2)}, u32[]{:S(2)}) collective-permute-start(f32[16,512]{1,0:T(8,128)S(1)} %constant_dynamic-slice_fusion), channel_id=1, source_target_pairs={{0,4},{4,0},{8,12},{12,8},{16,20},{20,16},{24,28},{28,24},{32,36},... | collective-permute-start | bytes 98312 | tf_op jit(solution)/shard_map/ppermute | solution.py:339
  64.9 0.9 collective-permute-done.14
  65.8 2.8 %collective-permute-done.15 = f32[16,512]{1,0:T(8,128)S(1)} collective-permute-done((f32[16,512]{1,0:T(8,128)S(1)}, f32[16,512]{1,0:T(8,128)S(1)}, u32[]{:S(2)}, u32[]{:S(2)}) %collective-permute-start.15) | collective-permute-done | bytes 32800 | tf_op jit(solution)/shard_map/ppermute | solution.py:339
  68.6 3.7 %collective-permute-done.16 = f32[16,512]{1,0:T(8,128)S(1)} collective-permute-done((f32[16,512]{1,0:T(8,128)S(1)}, f32[16,512]{1,0:T(8,128)S(1)}, u32[]{:S(2)}, u32[]{:S(2)}) %collective-permute-start.16) | collective-permute-done | bytes 32800 | tf_op jit(solution)/shard_map/ppermute | solution.py:339
  72.3 4.9 %collective-permute-done.17 = f32[16,512]{1,0:T(8,128)S(1)} collective-permute-done((f32[16,512]{1,0:T(8,128)S(1)}, f32[16,512]{1,0:T(8,128)S(1)}, u32[]{:S(2)}, u32[]{:S(2)}) %collective-permute-start.17) | collective-permute-done | bytes 32800 | tf_op jit(solution)/shard_map/ppermute | solution.py:339
  77.2 3.1 %collective-permute-done.18 = f32[16,512]{1,0:T(8,128)S(1)} collective-permute-done((f32[16,512]{1,0:T(8,128)S(1)}, f32[16,512]{1,0:T(8,128)S(1)}, u32[]{:S(2)}, u32[]{:S(2)}) %collective-permute-start.18) | collective-permute-done | bytes 32800 | tf_op jit(solution)/shard_map/ppermute | solution.py:339
  80.8 3.4 %collective-permute-done.19 = f32[16,512]{1,0:T(8,128)S(1)} collective-permute-done((f32[16,512]{1,0:T(8,128)S(1)}, f32[16,512]{1,0:T(8,128)S(1)}, u32[]{:S(2)}, u32[]{:S(2)}) %collective-permute-start.19) | collective-permute-done | bytes 32800 | tf_op jit(solution)/shard_map/ppermute | solution.py:339
  84.2 5.7 %collective-permute-start.20 = (f32[16,512]{1,0:T(8,128)S(1)}, f32[16,512]{1,0:T(8,128)S(1)}, u32[]{:S(2)}, u32[]{:S(2)}) collective-permute-start(f32[16,512]{1,0:T(8,128)S(1)} %add.36), channel_id=1, source_target_pairs={{0,4},{4,0},{8,12},{12,8},{16,20},{20,16},{24,28},{28,24},{32,36},... | collective-permute-start | bytes 98312 | tf_op jit(solution)/shard_map/ppermute | solution.py:339
  90.0 0.9 collective-permute-done.20
  90.9 19.5 %shard_map.84 = (f32[4,32,1024]{2,1,0:T(8,128)}, f32[4,32,32]{2,1,0:T(8,128)}) custom-call(s32[1]{0:T(128)} %bitcast.node, f32[2,16,8]{2,1,0:T(8,128)S(1)} %copy-done.2, f32[32,512]{1,0:T(8,128)S(1)} %pad_maximum_fusion.gram, f32[32,1024]{1,0:T(8,128)S(1)} %copy-done.1, f32[32,1024]{1,0:T(8,128)S(1)} %get-tuple-element.46.x.before.k1, ...), custom_call_target="tpu_custom_call" | custom-call | tf_op jit(solution)/shard_map/pallas_call | solution.py:439
  (47 shorter events, 5.7 us)
Async XLA Ops:
  0.6 6.4 %copy-start.3 = (s32[8,3]{0,1:T(4,128)S(1)}, s32[8,3]{0,1:T(4,128)}, u32[]{:S(2)}) copy-start(s32[8,3]{0,1:T(4,128)} %param.8) | copy-start | bytes 292
  0.6 6.4 %copy-start = (f32[8,3,128,128]{3,2,1,0:T(8,128)S(1)}, f32[8,3,128,128]{3,2,1,0:T(8,128)}, u32[]{:S(2)}) copy-start(f32[8,3,128,128]{3,2,1,0:T(8,128)} %coup_hbm.1) | copy-start | bytes 4718596
  0.6 6.4 %copy-start.1 = (f32[32,1024]{1,0:T(8,128)S(1)}, f32[32,1024]{1,0:T(8,128)}, u32[]{:S(2)}) copy-start(f32[32,1024]{1,0:T(8,128)} %k0.1) | copy-start | bytes 393220
  3.7 6.8 %collective-permute-start = (f32[32,512]{1,0:T(8,128)}, f32[32,512]{1,0:T(8,128)S(1)}, u32[]{:S(2)}, u32[]{:S(2)}) collective-permute-start(f32[32,512]{1,0:T(8,128)} %get-tuple-element.42), channel_id=1, source_target_pairs={{0,4},{4,0},{8,12},{12,8},{16,20},{20,16},{24,28},{28,24},{32,36},... | collective-permute-start | bytes 196616 | tf_op jit(solution)/shard_map/ppermute | solution.py:339
  7.0 3.9 %collective-permute-start.1 = (f32[32,512]{1,0:T(8,128)}, f32[32,512]{1,0:T(8,128)S(1)}, u32[]{:S(2)}, u32[]{:S(2)}) collective-permute-start(f32[32,512]{1,0:T(8,128)} %get-tuple-element.43), channel_id=1, source_target_pairs={{0,252},{4,8},{8,4},{12,16},{16,12},{20,24},{24,20},{28,32},{32,28... | collective-permute-start | bytes 196616 | tf_op jit(solution)/shard_map/ppermute | solution.py:339
  7.0 1.0 copy-start.4
  11.5 7.7 %collective-permute-start.2 = (f32[32,512]{1,0:T(8,128)S(1)}, f32[32,512]{1,0:T(8,128)S(1)}, u32[]{:S(2)}, u32[]{:S(2)}) collective-permute-start(f32[32,512]{1,0:T(8,128)S(1)} %get-tuple-element.51), channel_id=1, source_target_pairs={{0,4},{4,0},{8,12},{12,8},{16,20},{20,16},{24,28},{28,24},{32,36},... | collective-permute-start | bytes 196616 | tf_op jit(solution)/shard_map/ppermute | solution.py:339
  17.8 3.7 %collective-permute-start.3 = (f32[32,512]{1,0:T(8,128)S(1)}, f32[32,512]{1,0:T(8,128)S(1)}, u32[]{:S(2)}, u32[]{:S(2)}) collective-permute-start(f32[32,512]{1,0:T(8,128)S(1)} %get-tuple-element.52), channel_id=1, source_target_pairs={{0,252},{4,8},{8,4},{12,16},{16,12},{20,24},{24,20},{28,32},{32,28... | collective-permute-start | bytes 196616 | tf_op jit(solution)/shard_map/ppermute | solution.py:339
  22.2 4.8 %collective-permute-start.4 = (f32[32,512]{1,0:T(8,128)S(1)}, f32[32,512]{1,0:T(8,128)S(1)}, u32[]{:S(2)}, u32[]{:S(2)}) collective-permute-start(f32[32,512]{1,0:T(8,128)S(1)} %get-tuple-element.56), channel_id=1, source_target_pairs={{0,4},{4,0},{8,12},{12,8},{16,20},{20,16},{24,28},{28,24},{32,36},... | collective-permute-start | bytes 196616 | tf_op jit(solution)/shard_map/ppermute | solution.py:339
  25.6 3.7 %collective-permute-start.5 = (f32[32,512]{1,0:T(8,128)S(1)}, f32[32,512]{1,0:T(8,128)S(1)}, u32[]{:S(2)}, u32[]{:S(2)}) collective-permute-start(f32[32,512]{1,0:T(8,128)S(1)} %get-tuple-element.57), channel_id=1, source_target_pairs={{0,252},{4,8},{8,4},{12,16},{16,12},{20,24},{24,20},{28,32},{32,28... | collective-permute-start | bytes 196616 | tf_op jit(solution)/shard_map/ppermute | solution.py:339
  29.9 4.8 %collective-permute-start.6 = (f32[32,512]{1,0:T(8,128)S(1)}, f32[32,512]{1,0:T(8,128)S(1)}, u32[]{:S(2)}, u32[]{:S(2)}) collective-permute-start(f32[32,512]{1,0:T(8,128)S(1)} %get-tuple-element.61), channel_id=1, source_target_pairs={{0,4},{4,0},{8,12},{12,8},{16,20},{20,16},{24,28},{28,24},{32,36},... | collective-permute-start | bytes 196616 | tf_op jit(solution)/shard_map/ppermute | solution.py:339
  33.4 3.7 %collective-permute-start.7 = (f32[32,512]{1,0:T(8,128)S(1)}, f32[32,512]{1,0:T(8,128)S(1)}, u32[]{:S(2)}, u32[]{:S(2)}) collective-permute-start(f32[32,512]{1,0:T(8,128)S(1)} %get-tuple-element.62), channel_id=1, source_target_pairs={{0,252},{4,8},{8,4},{12,16},{16,12},{20,24},{24,20},{28,32},{32,28... | collective-permute-start | bytes 196616 | tf_op jit(solution)/shard_map/ppermute | solution.py:339
  37.7 4.8 %collective-permute-start.8 = (f32[32,512]{1,0:T(8,128)S(1)}, f32[32,512]{1,0:T(8,128)S(1)}, u32[]{:S(2)}, u32[]{:S(2)}) collective-permute-start(f32[32,512]{1,0:T(8,128)S(1)} %get-tuple-element.66), channel_id=1, source_target_pairs={{0,4},{4,0},{8,12},{12,8},{16,20},{20,16},{24,28},{28,24},{32,36},... | collective-permute-start | bytes 196616 | tf_op jit(solution)/shard_map/ppermute | solution.py:339
  41.2 3.7 %collective-permute-start.9 = (f32[32,512]{1,0:T(8,128)S(1)}, f32[32,512]{1,0:T(8,128)S(1)}, u32[]{:S(2)}, u32[]{:S(2)}) collective-permute-start(f32[32,512]{1,0:T(8,128)S(1)} %get-tuple-element.67), channel_id=1, source_target_pairs={{0,252},{4,8},{8,4},{12,16},{16,12},{20,24},{24,20},{28,32},{32,28... | collective-permute-start | bytes 196616 | tf_op jit(solution)/shard_map/ppermute | solution.py:339
  45.5 5.0 %collective-permute-start.10 = (f32[32,512]{1,0:T(8,128)S(1)}, f32[32,512]{1,0:T(8,128)S(1)}, u32[]{:S(2)}, u32[]{:S(2)}) collective-permute-start(f32[32,512]{1,0:T(8,128)S(1)} %get-tuple-element.71), channel_id=1, source_target_pairs={{0,4},{4,0},{8,12},{12,8},{16,20},{20,16},{24,28},{28,24},{32,36},... | collective-permute-start | bytes 196616 | tf_op jit(solution)/shard_map/ppermute | solution.py:339
  49.2 3.7 %collective-permute-start.11 = (f32[32,512]{1,0:T(8,128)S(1)}, f32[32,512]{1,0:T(8,128)S(1)}, u32[]{:S(2)}, u32[]{:S(2)}) collective-permute-start(f32[32,512]{1,0:T(8,128)S(1)} %get-tuple-element.72), channel_id=1, source_target_pairs={{0,252},{4,8},{8,4},{12,16},{16,12},{20,24},{24,20},{28,32},{32,28... | collective-permute-start | bytes 196616 | tf_op jit(solution)/shard_map/ppermute | solution.py:339
  53.5 4.8 %collective-permute-start.12 = (f32[32,512]{1,0:T(8,128)S(1)}, f32[32,512]{1,0:T(8,128)S(1)}, u32[]{:S(2)}, u32[]{:S(2)}) collective-permute-start(f32[32,512]{1,0:T(8,128)S(1)} %get-tuple-element.76), channel_id=1, source_target_pairs={{0,4},{4,0},{8,12},{12,8},{16,20},{20,16},{24,28},{28,24},{32,36},... | collective-permute-start | bytes 196616 | tf_op jit(solution)/shard_map/ppermute | solution.py:339
  56.9 3.7 %collective-permute-start.13 = (f32[32,512]{1,0:T(8,128)S(1)}, f32[32,512]{1,0:T(8,128)S(1)}, u32[]{:S(2)}, u32[]{:S(2)}) collective-permute-start(f32[32,512]{1,0:T(8,128)S(1)} %get-tuple-element.77), channel_id=1, source_target_pairs={{0,252},{4,8},{8,4},{12,16},{16,12},{20,24},{24,20},{28,32},{32,28... | collective-permute-start | bytes 196616 | tf_op jit(solution)/shard_map/ppermute | solution.py:339
  58.3 32.6 %copy-start.2 = (f32[2,16,8]{2,1,0:T(8,128)S(1)}, f32[2,16,8]{2,1,0:T(8,128)}, u32[]{:S(2)}) copy-start(f32[2,16,8]{2,1,0:T(8,128)} %constant.30.clone.weights) | copy-start | bytes 3076
  61.4 4.4 %collective-permute-start.14 = (f32[16,512]{1,0:T(8,128)S(1)}, f32[16,512]{1,0:T(8,128)S(1)}, u32[]{:S(2)}, u32[]{:S(2)}) collective-permute-start(f32[16,512]{1,0:T(8,128)S(1)} %constant_dynamic-slice_fusion), channel_id=1, source_target_pairs={{0,4},{4,0},{8,12},{12,8},{16,20},{20,16},{24,28},{28,24},{32,36},... | collective-permute-start | bytes 98312 | tf_op jit(solution)/shard_map/ppermute | solution.py:339
  65.8 2.8 %collective-permute-start.15 = (f32[16,512]{1,0:T(8,128)S(1)}, f32[16,512]{1,0:T(8,128)S(1)}, u32[]{:S(2)}, u32[]{:S(2)}) collective-permute-start(f32[16,512]{1,0:T(8,128)S(1)} %dynamic-slice_add_fusion), channel_id=1, source_target_pairs={{0,8},{4,12},{8,0},{12,4},{16,24},{20,28},{24,16},{28,20},{32,40},... | collective-permute-start | bytes 98312 | tf_op jit(solution)/shard_map/ppermute | solution.py:339
  68.6 3.7 %collective-permute-start.16 = (f32[16,512]{1,0:T(8,128)S(1)}, f32[16,512]{1,0:T(8,128)S(1)}, u32[]{:S(2)}, u32[]{:S(2)}) collective-permute-start(f32[16,512]{1,0:T(8,128)S(1)} %add.32), channel_id=1, source_target_pairs={{0,16},{4,20},{8,24},{12,28},{16,0},{20,4},{24,8},{28,12},{32,48},... | collective-permute-start | bytes 98312 | tf_op jit(solution)/shard_map/ppermute | solution.py:339
  72.3 4.9 %collective-permute-start.17 = (f32[16,512]{1,0:T(8,128)S(1)}, f32[16,512]{1,0:T(8,128)S(1)}, u32[]{:S(2)}, u32[]{:S(2)}) collective-permute-start(f32[16,512]{1,0:T(8,128)S(1)} %add.33), channel_id=1, source_target_pairs={{0,48},{4,52},{8,56},{12,60},{16,32},{20,36},{24,40},{28,44},{32,1... | collective-permute-start | bytes 98312 | tf_op jit(solution)/shard_map/ppermute | solution.py:339
  77.2 3.1 %collective-permute-start.18 = (f32[16,512]{1,0:T(8,128)S(1)}, f32[16,512]{1,0:T(8,128)S(1)}, u32[]{:S(2)}, u32[]{:S(2)}) collective-permute-start(f32[16,512]{1,0:T(8,128)S(1)} %add.34), channel_id=1, source_target_pairs={{0,64},{4,68},{8,72},{12,76},{16,80},{20,84},{24,88},{28,92},{32,9... | collective-permute-start | bytes 98312 | tf_op jit(solution)/shard_map/ppermute | solution.py:339
  80.3 4.0 %collective-permute-start.19 = (f32[16,512]{1,0:T(8,128)S(1)}, f32[16,512]{1,0:T(8,128)S(1)}, u32[]{:S(2)}, u32[]{:S(2)}) collective-permute-start(f32[16,512]{1,0:T(8,128)S(1)} %add.35), channel_id=1, source_target_pairs={{0,192},{4,196},{8,200},{12,204},{16,208},{20,212},{24,216},{28,22... | collective-permute-start | bytes 98312 | tf_op jit(solution)/shard_map/ppermute | solution.py:339
  84.2 6.6 %collective-permute-start.20 = (f32[16,512]{1,0:T(8,128)S(1)}, f32[16,512]{1,0:T(8,128)S(1)}, u32[]{:S(2)}, u32[]{:S(2)}) collective-permute-start(f32[16,512]{1,0:T(8,128)S(1)} %add.36), channel_id=1, source_target_pairs={{0,4},{4,0},{8,12},{12,8},{16,20},{20,16},{24,28},{28,24},{32,36},... | collective-permute-start | bytes 98312 | tf_op jit(solution)/shard_map/ppermute | solution.py:339

commit v2 on v1

v2 whole, which is shorter than its diff:
```python
import functools
import math

import jax
import jax.numpy as jnp
import numpy as np
from jax import lax
from jax.experimental import pallas as pl
from jax.experimental.pallas import tpu as pltpu
from jax.sharding import PartitionSpec as P

NODES = 8
MOMENTS = 16
REACH = 4
ITERS = 4
PROBES = 32
BLOCK = 128
ROWS = 1024
HALF = 512
TILE = 256
DEGREE = 2 * ITERS - 1
BLOCKS = 512
ORDER_DIM = BLOCKS * BLOCK
SCALE = 16.0

f32 = jnp.float32
bf16 = jnp.bfloat16
highest = lax.Precision.HIGHEST

TILES = [(row, col) for row in range(4) for col in range(row, min(row + 3, 4))]
EDGE = [(row, col) for row in range(REACH) for col in range(row + 1)]

VMEM = pl.BlockSpec(memory_space=pltpu.VMEM)
SMEM = pl.BlockSpec(memory_space=pltpu.SMEM)


HBM = pl.BlockSpec(memory_space=pltpu.HBM)


def call(body, outs, in_specs, flops=0, bytes_accessed=0, vmem=8, scratch=(), out_specs=None, aliases=()):
    return pl.pallas_call(
        body,
        out_shape=outs,
        in_specs=in_specs,
        out_specs=jax.tree.map(lambda _: VMEM, outs) if out_specs is None else out_specs,
        input_output_aliases=dict(aliases),
        scratch_shapes=scratch,
        compiler_params=pltpu.CompilerParams(vmem_limit_bytes=vmem << 20),
        cost_estimate=pl.CostEstimate(flops=flops, bytes_accessed=bytes_accessed, transcendentals=0),
    )


def halves(value):
    high = value.astype(bf16)
    return high, (value - high.astype(f32)).astype(bf16)


def stacked(value):
    high, low = halves(value)
    return jnp.concatenate([high, low], axis=0)


def dot_nn(left, right):
    return lax.dot_general(left, right, (((1,), (0,)), ((), ())), preferred_element_type=f32)


def dot_nt(left, right):
    return lax.dot_general(left, right, (((1,), (1,)), ((), ())), preferred_element_type=f32)


def fold(double):
    half = double.shape[0] // 2
    return double[:half] + double[half:]


def product(dot, pair, high, low):
    return fold(dot(pair, high)) + dot(pair[:pair.shape[0] // 2], low)


def payloads(parity, near, spill, pay_core, pay_chip):
    even = parity == 0
    pay_core[...] = jnp.where(even, spill, near)
    pay_chip[...] = jnp.where(even, near, spill)


def cross_out(tail, uhi, ulo):
    pair = stacked(tail)
    left, right = pair[:, :TILE], pair[:, TILE:]
    first = product(dot_nn, left, uhi[0], ulo[0]) + product(dot_nn, right, uhi[1], ulo[1])
    return jnp.concatenate([first, product(dot_nn, right, uhi[2], ulo[2])], axis=1)


def cross_in(ahead, uhi, ulo):
    pair = stacked(ahead)
    left, right = pair[:, :TILE], pair[:, TILE:]
    second = product(dot_nt, left, uhi[1], ulo[1]) + product(dot_nt, right, uhi[2], ulo[2])
    return jnp.concatenate([product(dot_nt, left, uhi[0], ulo[0]), second], axis=1)


def band_block(step, row, neighbours, position, diag, coup):
    if step == 0:
        return diag * (0.5 / SCALE)
    block = jnp.zeros((BLOCK, BLOCK), f32)
    for f in range(neighbours.shape[0]):
        distance = (neighbours[f, row] - (position * 8 + row)) & (BLOCKS - 1)
        block = block + jnp.where(distance == step, coup[f], 0.0)
    return block * (1.0 / SCALE)


def cross_place(row, col):
    return row // 2 + col // 2, pl.ds(row % 2 * BLOCK, BLOCK), pl.ds(col % 2 * BLOCK, BLOCK)


def cross_zero(uhi, ulo):
    zero = jnp.zeros((BLOCK, BLOCK), bf16)
    for row, col in ((0, 1), (2, 3)):
        uhi[cross_place(row, col)] = zero
        ulo[cross_place(row, col)] = zero


def cross_rows(i, neighbours, position, coup, uhi, ulo, edge=None):
    row = i - 4
    for col in range(row + 1):
        block = band_block(8 + col - i, i, neighbours, position, None, coup)
        uhi[cross_place(row, col)], ulo[cross_place(row, col)] = halves(block)
        if edge is not None:
            edge[EDGE.index((row, col))] = block


def cross_body(neighbours, position, coup_hbm, x_hbm, pay_core, pay_chip, coup, x, uhi, ulo, sems):
    copies = [pltpu.make_async_copy(coup_hbm.at[i], coup.at[i - 4], sems.at[i - 4]) for i in (7, 6, 5, 4)]
    for copy in copies:
        copy.start()
    load = pltpu.make_async_copy(x_hbm, x, sems.at[4])
    load.start()
    cross_zero(uhi, ulo)
    for i, copy in zip((7, 6, 5, 4), copies):
        copy.wait()
        cross_rows(i, neighbours, position[0], coup.at[i - 4], uhi, ulo)
    load.wait()
    payloads(position[0] & 1, x[:, :HALF], cross_out(x[:, HALF:], uhi, ulo), pay_core, pay_chip)


def gram_of(x, before):
    both = jnp.concatenate([before, x], axis=0)
    return lax.dot_general(x, both, (((1,), (1,)), ((), ())), precision=highest, preferred_element_type=f32)


def first_body(neighbours, position, diag, coup, x, after, thi, tlo, uhi, ulo, edge, local, gram):
    zero = jnp.zeros((BLOCK, BLOCK), bf16)
    for tile, (row, col) in enumerate(TILES):
        for up in range(2):
            for across in range(2):
                i, step = 2 * row + up, 2 * (col - row) + across - up
                at = tile, pl.ds(up * BLOCK, BLOCK), pl.ds(across * BLOCK, BLOCK)
                if 0 <= step <= REACH:
                    block = band_block(step, i, neighbours, position[0], diag[i] if step == 0 else None, coup.at[i])
                    thi[at], tlo[at] = halves(block)
                else:
                    thi[at] = zero
                    tlo[at] = zero
    cross_zero(uhi, ulo)
    for i in range(4, 8):
        cross_rows(i, neighbours, position[0], coup.at[i], uhi, ulo, edge)
    value = x[...]
    local[...] = times_local(value, thi, tlo)
    gram[...] = gram_of(value, value)


def times_local(value, thi, tlo):
    pair = stacked(value)
    wide = [jnp.zeros((2 * PROBES, TILE), f32) for _ in range(4)]
    thin = [jnp.zeros((PROBES, TILE), f32) for _ in range(4)]
    for tile, (row, col) in enumerate(TILES):
        high, low = thi[tile], tlo[tile]
        from_row, from_col = pair[:, row * TILE:(row + 1) * TILE], pair[:, col * TILE:(col + 1) * TILE]
        wide[col] = wide[col] + dot_nn(from_row, high)
        thin[col] = thin[col] + dot_nn(from_row[:PROBES], low)
        wide[row] = wide[row] + dot_nt(from_col, high)
        thin[row] = thin[row] + dot_nt(from_col[:PROBES], low)
    return jnp.concatenate([fold(w) + t for w, t in zip(wide, thin)], axis=1)


def joined(local, arrived, inward):
    return jnp.concatenate([local[:, :HALF] + arrived, local[:, HALF:] + inward], axis=1)


def send_two(position, value, thi, tlo, uhi, ulo, local, spill, pay_core, pay_chip):
    following = times_local(value, thi, tlo)
    local[...] = following
    both = cross_out(jnp.concatenate([value[:, HALF:], following[:, HALF:]], axis=0), uhi, ulo)
    spill[...] = both[:PROBES]
    near = jnp.concatenate([value[:, :HALF], following[:, :HALF]], axis=0)
    payloads(position[0] & 1, near, both, pay_core, pay_chip)


def received(position, got_core, got_chip):
    even = position[0] & 1 == 0
    core, chip = got_core[...], got_chip[...]
    return jnp.where(even, core, chip), jnp.where(even, chip, core)


def start_body(position, local, got_core, got_chip, thi, tlo, uhi, ulo, kept, out, *rest):
    *sent, sems = rest
    ahead, arrived = received(position, got_core, got_chip)
    value = joined(local, arrived, cross_in(ahead, uhi, ulo))
    out[...] = value
    keep = pltpu.make_async_copy(out, kept.at[1], sems.at[0])
    keep.start()
    send_two(position, value, thi, tlo, uhi, ulo, *sent)
    keep.wait()


def double_body(
    kept_in, position, before, local, spill, correction, got_core, got_chip, thi, tlo, uhi, ulo, kept, first, second, *rest,
    degree
):
    *sent, sems = rest
    ahead, arrived = received(position, got_core, got_chip)
    ahead = jnp.concatenate([ahead[:PROBES], ahead[PROBES:] + spill[...]], axis=0)
    inward = cross_in(ahead, uhi, ulo)
    value = joined(local, arrived[:PROBES], inward[:PROBES])
    first[...] = value
    keeps = [pltpu.make_async_copy(ref, kept.at[degree + 1 + n], sems.at[n]) for n, ref in enumerate((first, second))]
    keeps[0].start()
    local = times_local(value, thi, tlo)
    after = joined(local, arrived[PROBES:] + correction[...], inward[PROBES:])
    second[...] = after
    keeps[1].start()
    if len(sent) > 2:
        send_two(position, after, thi, tlo, uhi, ulo, *sent)
    else:
        sums = jnp.concatenate([gram_of(value, before[...]), gram_of(after, value)], axis=1)
        store_halves(position, sums, *sent)
    for keep in keeps:
        keep.wait()


def store_halves(position, sums, mine, other):
    upper, lower = sums[:PROBES // 2], sums[PROBES // 2:]
    even = position[0] & 1 == 0
    mine[...] = jnp.where(even, upper, lower)
    other[...] = jnp.where(even, lower, upper)


def shadow_body(position, *refs, count, first, last):
    vectors, (done, up_hi, up_lo), outs = refs[:count], refs[count:count + 3], refs[count + 3:]
    correction, outs = outs[0], outs[1:]
    if first:
        phi, plo = outs[1:]
        cross_zero(phi, plo)
        for n, (row, col) in enumerate(EDGE):
            phi[cross_place(row, col)], plo[cross_place(row, col)] = halves(up_hi[n])
    else:
        phi, plo = up_hi, up_lo
    sums = [done[...]] + [gram_of(vectors[n][...], vectors[n - 1][...]) for n in range(1, count)]
    sums = jnp.concatenate(sums, axis=1)
    if last:
        store_halves(position, sums, *outs)
    else:
        outs[0][...] = sums
    correction[...] = cross_out(cross_in(vectors[-1][:, :HALF], phi, plo), phi, plo)


def dot_f32(left, right):
    return lax.dot_general(left, right, (((1,), (0,)), ((), ())), precision=highest, preferred_element_type=f32)


WIDTH = NODES * PROBES
PANEL = 8


def invert(matrix):
    rows = lax.broadcasted_iota(jnp.int32, (PROBES, WIDTH), 0)
    lanes = lax.broadcasted_iota(jnp.int32, (PROBES, WIDTH), 1) % PROBES
    group = lax.broadcasted_iota(jnp.int32, (PROBES, BLOCK), 1) // PROBES * PROBES
    for start in range(0, PROBES, PANEL):
        columns = [
            jnp.concatenate(
                [jnp.take_along_axis(matrix[:, h:h + BLOCK], group + k, axis=1) for h in range(0, WIDTH, BLOCK)], axis=1
            )
            for k in range(start, start + PANEL)
        ]
        for m in range(PANEL):
            k = start + m
            on_row, on_lane = rows == k, lanes == k
            inverse = 1.0 / columns[m][k:k + 1]
            factor = jnp.where(on_row, -1.0, columns[m])
            scaled = jnp.where(on_lane[:1], 1.0, matrix[k:k + 1]) * inverse
            matrix = jnp.where(on_lane | on_row, 0.0, matrix) - factor * scaled
            for q in range(m + 1, PANEL):
                columns[q] = jnp.where(on_row, 0.0, columns[q]) - factor * (columns[q][k:k + 1] * inverse)
    return matrix


def node_diagonal():
    return (
        lax.broadcasted_iota(jnp.int32, (WIDTH, WIDTH), 0) // PROBES
        == lax.broadcasted_iota(jnp.int32, (WIDTH, WIDTH), 1) // PROBES
    )


def node_shifts():
    node = lax.broadcasted_iota(jnp.int32, (1, WIDTH), 1) // PROBES
    cosine = jnp.zeros((1, WIDTH), f32)
    square = jnp.zeros((1, WIDTH), f32)
    for j in range(NODES):
        angle = math.pi * (j + 0.5) / NODES
        cosine = jnp.where(node == j, np.float32(math.cos(angle)), cosine)
        square = jnp.where(node == j, np.float32(math.sin(angle) ** 2), square)
    return cosine, square


def grown(coeffs, blocks=1):
    return jnp.concatenate([coeffs, jnp.zeros((blocks * PROBES, WIDTH), f32)], axis=0)


def sunk(coeffs, cosine):
    below = jnp.concatenate([jnp.zeros((PROBES, WIDTH), f32), coeffs], axis=0)
    return SCALE * below - cosine * grown(coeffs)


def raised(against, cosine):
    return SCALE * against[PROBES:] - cosine * against[:-PROBES]


class Nodes:
    def __init__(self):
        self.diagonal = node_diagonal()
        self.cosine, self.square = node_shifts()

    def blocks(self, full):
        masked = jnp.where(self.diagonal, full, 0.0)
        return sum(masked[j * PROBES:(j + 1) * PROBES] for j in range(NODES))

    def spread(self, matrix):
        return jnp.where(self.diagonal, jnp.concatenate([matrix] * NODES, axis=0), 0.0)

    def inner(self, left, against):
        return self.blocks(dot_f32(left.T, against[:left.shape[0]]))

    def image(self, direction, dir_against):
        once, once_against = sunk(direction, self.cosine), raised(dir_against, self.cosine)
        image = sunk(once, self.cosine) + self.square * grown(direction, 2)
        image_against = raised(once_against, self.cosine) + self.square * dir_against[:-2 * PROBES]
        return image, image_against

    def alpha(self, direction, residual, dir_against, res_against, solution):
        size = direction.shape[0]
        image, image_against = self.image(direction, dir_against)
        if size == PROBES:
            curvature, now = image_against[:size], res_against[:size]
        else:
            turned = direction.T
            curvature = self.blocks(dot_f32(turned, image_against[:size]))
            now = self.blocks(dot_f32(turned, res_against[:size]))
        inverse = invert(curvature)
        alpha = self.spread(dot_f32(inverse, self.spread(now)))
        if residual is None:
            return grown(solution, 2) + dot_f32(direction, alpha)
        moved = dot_f32(jnp.concatenate([direction, image, image_against], axis=0), alpha)
        part = size + image.shape[0]
        solution = moved[:size] if solution is None else grown(solution, 2) + moved[:size]
        residual = grown(residual, 2) - moved[size:part]
        res_against = res_against[:-2 * PROBES] - moved[part:]
        return image, inverse, residual, res_against, solution

    def beta(self, direction, dir_against, image, inverse, residual, res_against):
        size, count = direction.shape[0], res_against.shape[0]
        beta = self.spread(dot_f32(inverse, self.spread(self.inner(image, res_against))))
        moved = dot_f32(jnp.concatenate([direction, dir_against[:count]], axis=0), beta)
        return residual - grown(moved[:size], 2), res_against - moved[size:]


def moment_coeffs(nodes, weights, first, share, solution):
    applied = sunk(solution, nodes.cosine)
    row = lax.broadcasted_iota(jnp.int32, (PROBES, share * PROBES), 0)
    lane = lax.broadcasted_iota(jnp.int32, (PROBES, share * PROBES), 1)
    imag, real = [], []
    for j in range(NODES):
        for part, (table, sign) in ((imag, (0, 1.0)), (real, (1, -1.0))):
            block = jnp.zeros((PROBES, share * PROBES), f32)
            for k in range(share):
                block = jnp.where(lane == row + k * PROBES, sign * weights[table, first + k, j], block)
            part.append(block)
    left = jnp.concatenate([grown(solution), applied], axis=1)
    return dot_f32(left, jnp.concatenate(imag + real, axis=0))


def whole(position, mine, other):
    even = position[0] & 1 == 0
    upper, lower = jnp.where(even, mine[...], other[...]), jnp.where(even, other[...], mine[...])
    return jnp.concatenate([upper, lower], axis=0)


def store(outs, values):
    for out, value in zip(outs, values):
        out[...] = value


def zeroth_body(position, mine, other, *outs):
    nodes = Nodes()
    sums = whole(position, mine, other)
    against = jnp.concatenate(
        [
            jnp.concatenate([sums[:, at:at + PROBES]] * NODES, axis=1)
            for at in range(PROBES, sums.shape[1], PROBES)
        ],
        axis=0,
    )
    eye = (
        lax.broadcasted_iota(jnp.int32, (PROBES, WIDTH), 0)
        == lax.broadcasted_iota(jnp.int32, (PROBES, WIDTH), 1) % PROBES
    ).astype(f32)
    image, inverse, residual, res_against, solution = nodes.alpha(eye, eye, against, against, None)
    direction, dir_against = nodes.beta(eye, against, image, inverse, residual, res_against)
    store(outs, (direction, residual, dir_against, res_against, solution))


def iterate_body(*refs):
    nodes = Nodes()
    direction, residual, dir_against, res_against, solution = (ref[...] for ref in refs[:5])
    image, inverse, residual, res_against, solution = nodes.alpha(
        direction, residual, dir_against, res_against, solution
    )
    direction, dir_against = nodes.beta(direction, dir_against, image, inverse, residual, res_against)
    store(refs[5:], (direction, residual, dir_against, res_against, solution))


def alpha_body(*refs):
    store(refs[5:], Nodes().alpha(*(ref[...] for ref in refs[:5])))


def moments_body(
    node, position, weights, mine, other, mine_late, other_late, direction, dir_against,
    image, inverse, residual, res_against, solution, k0, kept, moments, projected, basis, sems
):
    loads = [pltpu.make_async_copy(k0, basis.at[0], sems.at[0])]
    loads += [pltpu.make_async_copy(kept.at[d], basis.at[d], sems.at[d]) for d in range(1, DEGREE + 1)]
    for load in loads:
        load.start()
    nodes = Nodes()
    sums = jnp.concatenate([whole(position, mine, other)[:, PROBES:], whole(position, mine_late, other_late)], axis=1)

    def against(coeffs, old):
        size = coeffs.shape[0]
        rows = [sums[:, a:a + size] for a in range(old.shape[0], (DEGREE + 2) * PROBES, PROBES)]
        return jnp.concatenate([old, dot_f32(jnp.concatenate(rows, axis=0), coeffs)], axis=0)

    direction, residual = direction[...], residual[...]
    res_against = against(residual, res_against[...])
    dir_against = against(direction, dir_against[...])
    direction, dir_against = nodes.beta(direction, dir_against, image[...], inverse[...], residual, res_against)
    result = nodes.alpha(direction, None, dir_against, res_against, solution[...])
    share = moments.shape[0]
    coeffs = moment_coeffs(nodes, weights, node[0] * share, share, result)
    onto = dot_f32(sums[:, :PROBES * (DEGREE + 1)], coeffs) * (1.0 / ORDER_DIM)
    for k in range(share):
        projected[k] = onto[:, k * PROBES:(k + 1) * PROBES]
    turned = coeffs.T
    for load in loads:
        load.wait()
    moments[...] = dot_f32(turned, basis[...].reshape((DEGREE + 1) * PROBES, ROWS)).reshape(share, PROBES, ROWS)


def add_body(left, right, out):
    out[...] = left[...] + right[...]


def exchange(value, partner):
    count = lax.axis_size("row")
    return lax.ppermute(value, "row", [(source, partner(source) % count) for source in range(count)])


def core_partner(i):
    return i ^ 1


def chip_partner(i):
    return i + 1 if i % 2 else i - 1


def ring_partner(stage, i):
    y, z, core = i // 16, i // 2 % 8, i % 2
    if stage < 3:
        z = (z ^ 1, z ^ 2, (6, 7, 4, 5, 2, 3, 0, 1)[z])[stage]
    else:
        y = (y ^ 1, y ^ 3)[stage - 3]
    return y * 16 + z * 2 + core


def add(left, right):
    return call(add_body, jax.ShapeDtypeStruct(left.shape, f32), [VMEM] * 2, vmem=4)(left, right)


def stage(value, number):
    return add(value, exchange(value, functools.partial(ring_partner, number)))


def moment_weights():
    orders = np.arange(MOMENTS)[:, None] + 1.0
    angles = np.pi * (np.arange(NODES)[None, :] + 0.5) / NODES
    imag = np.sin(orders * angles) * np.sin(angles) / 8.0
    real = np.cos(orders * angles) / 8.0
    return np.stack([imag, real]).astype(np.float32)


def shards(probes, diag_blocks, couplings, neighbours):
    moment_share = MOMENTS // lax.axis_size("node")
    position = lax.axis_index("row")
    flag = position.reshape(1)
    node = lax.axis_index("node").reshape(1)
    near_by = neighbours.T
    def array(*shape, kind=f32):
        return jax.ShapeDtypeStruct(shape, kind)

    message = array(PROBES, HALF)
    vector = array(PROBES, ROWS)
    pair = array(PROBES, 2 * PROBES)
    double = array(2 * PROBES, HALF)
    band = (array(len(TILES), TILE, TILE, kind=bf16),) * 2
    cross = (array(3, TILE, TILE, kind=bf16),) * 2
    stack = array(DEGREE + 1, PROBES, ROWS)
    copies = pltpu.SemaphoreType.DMA((2,))
    pay_core, pay_chip = call(
        cross_body,
        (message, message),
        [SMEM, SMEM, HBM, HBM],
        vmem=56,
        scratch=[
            pltpu.VMEM((4, 3, BLOCK, BLOCK), f32),
            pltpu.VMEM((PROBES, ROWS), f32),
            pltpu.VMEM((3, TILE, TILE), bf16),
            pltpu.VMEM((3, TILE, TILE), bf16),
            pltpu.SemaphoreType.DMA((5,)),
        ],
    )(near_by, flag, couplings, probes)
    got_core = exchange(pay_core, core_partner)
    got_chip = exchange(pay_chip, chip_partner)
    thi, tlo, uhi, ulo, edge, local, gram = call(
        first_body,
        band + cross + (array(len(EDGE), BLOCK, BLOCK), vector, pair),
        [SMEM, SMEM, VMEM, VMEM, VMEM, HBM],
        flops=10**9,
        bytes_accessed=4 << 20,
        vmem=16,
    )(near_by, flag, diag_blocks, couplings, probes, pay_chip)
    edge, got_chip = lax.optimization_barrier((edge, got_chip))
    edge = exchange(edge, lambda i: i + 1)
    blocks = (thi, tlo, uhi, ulo)
    sent = (vector, message, double, double)
    kept, value, local, spill, pay_core, pay_chip = call(
        start_body,
        (stack, vector) + sent,
        [SMEM] + [VMEM] * 7,
        flops=10**9,
        bytes_accessed=4 << 20,
        out_specs=(HBM,) + (VMEM,) * 5,
        scratch=[copies],
    )(flag, local, got_core, got_chip, *blocks)
    fresh = [probes, value]
    previous = (edge, edge)
    for degree in range(1, DEGREE, 2):
        got_core = exchange(pay_core, core_partner)
        got_chip = exchange(pay_chip, chip_partner)
        more = degree + 2 < DEGREE
        first = degree == 1
        lanes = gram.shape[1] + 2 * PROBES * (len(fresh) - 1)
        sums = (array(PROBES, lanes),) if more else (array(PROBES // 2, lanes),) * 2
        correction, *made = call(
            functools.partial(shadow_body, count=len(fresh), first=first, last=not more),
            (message,) + sums + (cross if first else ()),
            [SMEM] + [VMEM] * (len(fresh) + 3),
            flops=10**9,
            bytes_accessed=2 << 20,
        )(flag, *fresh, gram, *previous)
        if first:
            previous = made[1:]
        if more:
            gram = made[0]
        else:
            early = stage(add(made[0], exchange(made[1], core_partner)), 0)
            early, got_core, got_chip = lax.optimization_barrier((early, got_core, got_chip))
            arrived = exchange(early, functools.partial(ring_partner, 3))
        outs = (stack, vector, vector) + (sent if more else (array(PROBES // 2, 4 * PROBES),) * 2)
        kept, value, after, *rest = call(
            functools.partial(double_body, degree=degree),
            outs,
            [HBM, SMEM] + [VMEM] * 10,
            flops=10**9,
            bytes_accessed=4 << 20,
            out_specs=(HBM,) + (VMEM,) * (len(outs) - 1),
            scratch=[copies],
            aliases=((0, 0),),
        )(kept, flag, fresh[-1], local, spill, correction, got_core, got_chip, *blocks)
        fresh = [fresh[-1], value, after]
        if more:
            local, spill, pay_core, pay_chip = rest
    late, other, arrived = lax.optimization_barrier((*rest, arrived))
    early = add(early, arrived)

    def coeffs(blocks):
        return array(blocks * PROBES, WIDTH)

    work = dict(flops=3 * 10**9, bytes_accessed=4 << 20, vmem=16)
    early, late = lax.optimization_barrier((stage(early, 1), add(late, exchange(other, core_partner))))
    early, late = lax.optimization_barrier((stage(early, 2), stage(late, 3)))
    early, late = lax.optimization_barrier((stage(early, 4), stage(late, 0)))

    def beside(number, body, blocks, specs, *args):
        got = exchange(late, functools.partial(ring_partner, number))
        made = call(body, tuple(map(coeffs, blocks)), specs, **work)(*args)
        got, made = lax.optimization_barrier((got, made))
        return add(late, got), made

    early = (early, exchange(early, core_partner))
    late, state = beside(4, zeroth_body, (3, 3, 9, 9, 1), [SMEM, VMEM, VMEM], flag, *early)
    late, state = beside(2, iterate_body, (5, 5, 7, 7, 3), [VMEM] * 5, *state)
    direction, _, dir_against, _, _ = state
    late, state = beside(1, alpha_body, (7, 1, 7, 5, 5), [VMEM] * 5, *state)
    late = (late, exchange(late, core_partner))
    moments, projected = call(
        moments_body,
        (array(moment_share, PROBES, ROWS), array(moment_share, PROBES, PROBES)),
        [SMEM] * 3 + [VMEM] * 11 + [HBM] * 2,
        vmem=24,
        scratch=[pltpu.VMEM((DEGREE + 1, PROBES, ROWS), f32), pltpu.SemaphoreType.DMA((DEGREE + 1,))],
    )(node, flag, jnp.asarray(moment_weights()), *early, *late, direction, dir_against, *state, probes, kept)
    return (moments, projected)


def solution(mesh):
    placed = (P(None, "row"), P("row", None, None), P("row", None, None, None), P("row", None))
    return jax.shard_map(
        shards,
        mesh=mesh,
        in_specs=placed,
        out_specs=(P("node", None, "row"), P("node", None, None)),
        check_vma=False,
    )
```

time: 110 us -> 103 us (0.936)
  waiting for transfers between devices: 33.9 us -> 20.7 us
  Pallas kernels: 37.3 us -> 41.1 us
    pallas_call x15 -> x23, Pallas kernels: 14.9 us -> 28.3 us  [the longest x3 10.5 us: beside(): made = call(body, tuple(map(coeffs, blocks)), specs, **work)(*args)]
    ppermute x21 -> x23, waiting for transfers between devices: 33.9 us -> 20.7 us  [exchange(): lax.ppermute(value, 'row', [(source, partner(source) % count) for source...]
    pallas_call x1, Pallas kernels: 19.5 us -> 9.73 us  [shards(): call(moments_body, (array(moment_share, PROBES, ROWS), array(moment_share...]
    ppermute x21 -> x23, starting transfers between devices: 37 us -> 38 us  [exchange(): lax.ppermute(value, 'row', [(source, partner(source) % count) for source...]
  transfers between devices with their start and end apart: 21 -> 23, of which waited for: 14 -> 14; matrix products, arithmetic and copies ran while one was open for 0% -> 0% of each run, Pallas kernels for 9% -> 21%
where the time goes in v2:
time: 103 us
  Pallas kernels  41.1 us (40%)
  starting transfers between devices  38 us (37%)
  waiting for transfers between devices  20.7 us (20%)
  local copies, waits for them, and re-layouts  1.9 us (2%)
  between operations  1.05 us (1%)
    ppermute x23, starting transfers between devices, exchange(): lax.ppermute(value, 'row', [(source, partner(source) % count) for source...  38 us
    ppermute x23, waiting for transfers between devices, exchange(): lax.ppermute(value, 'row', [(source, partner(source) % count) for source...  20.7 us
    pallas_call x3, Pallas kernels, beside(): made = call(body, tuple(map(coeffs, blocks)), specs, **work)(*args)  10.5 us
    pallas_call x3, Pallas kernels, shards(): call(functools.partial(double_body, degree=degree), outs, [HBM, SMEM] + [...  10.4 us
    pallas_call x1, Pallas kernels, shards(): call(moments_body, (array(moment_share, PROBES, ROWS), array(moment_share...  9.73 us
    pallas_call x1, Pallas kernels, shards(): call(cross_body, (message, message), [SMEM, SMEM, HBM, HBM], vmem=56, scr...  3.01 us
    pallas_call x3, Pallas kernels, shards(): call(functools.partial(shadow_body, count=len(fresh), first=first, last=n...  2.73 us
    pallas_call x1, Pallas kernels, shards(): call(first_body, band + cross + (array(len(EDGE), BLOCK, BLOCK), vector,...  2.58 us
  transfers between devices with their start and end apart: 23, of which 14 were waited for; matrix products, arithmetic and copies ran while one was open for 0% of the time, Pallas kernels for 21%

profile of v2, /device:TPU:1, one launch (start us, length us, event | category | flops | bytes accessed | tf_op | source)
XLA Modules:
  0.0 102.7 jit_solution(4079038466561072345)
XLA Ops:
  0.7 3.0 %shard_map.68 = (f32[32,512]{1,0:T(8,128)}, f32[32,512]{1,0:T(8,128)}) custom-call(s32[3,8]{1,0:T(4,128)} %bitcast.3, s32[1]{0:T(128)} %bitcast.1.position, f32[8,3,128,128]{3,2,1,0:T(8,128)} %coup.1, f32[32,1024]{1,0:T(8,128)} %k0.1), custom_call_target="tpu_custom_call" | custom-call | tf_op jit(solution)/shard_map/pallas_call | solution.py:525
  3.7 3.1 %collective-permute-start.1 = (f32[32,512]{1,0:T(8,128)}, f32[32,512]{1,0:T(8,128)S(1)}, u32[]{:S(2)}, u32[]{:S(2)}) collective-permute-start(f32[32,512]{1,0:T(8,128)} %get-tuple-element.90.after), channel_id=1, source_target_pairs={{0,252},{4,8},{8,4},{12,16},{16,12},{20,24},{24,20},{28,32},{32,28... | collective-permute-start | bytes 196616 | tf_op jit(solution)/shard_map/ppermute | solution.py:472
  6.8 1.0 %copy-done.4 = f32[8,128,128]{2,1,0:T(8,128)S(1)} copy-done((f32[8,128,128]{2,1,0:T(8,128)S(1)}, f32[8,128,128]{2,1,0:T(8,128)}, u32[]{:S(2)}) %copy-start.4) | copy-done | bytes 524312
  8.7 2.6 %shard_map.69 = (bf16[9,256,256]{2,1,0:T(8,128)(2,1)S(1)}, bf16[9,256,256]{2,1,0:T(8,128)(2,1)S(1)}, bf16[3,256,256]{2,1,0:T(8,128)(2,1)S(1)}, bf16[3,256,256]{2...) custom-call(s32[3,8]{1,0:T(4,128)S(1)} %bitcast.4, ...), custom_call_target="tpu_custom_call" | custom-call | flops 1000000000 | bytes 4194304 | tf_op jit(solution)/shard_map/pallas_call | solution.py:540
  11.4 6.3 %collective-permute-start = (f32[32,512]{1,0:T(8,128)S(1)}, f32[32,512]{1,0:T(8,128)S(1)}, u32[]{:S(2)}, u32[]{:S(2)}) collective-permute-start(f32[32,512]{1,0:T(8,128)S(1)} %copy-done.6), channel_id=1, source_target_pairs={{0,4},{4,0},{8,12},{12,8},{16,20},{20,16},{24,28},{28,24},{32,36},... | collective-permute-start | bytes 196616 | tf_op jit(solution)/shard_map/ppermute | solution.py:472
  17.7 1.6 %collective-permute-done.got_core = f32[32,512]{1,0:T(8,128)S(1)} collective-permute-done((f32[32,512]{1,0:T(8,128)S(1)}, f32[32,512]{1,0:T(8,128)S(1)}, u32[]{:S(2)}, u32[]{:S(2)}) %collective-permute-start) | collective-permute-done | bytes 65568 | tf_op jit(solution)/shard_map/ppermute | solution.py:472
  19.3 2.1 %shard_map.70 = (f32[8,32,1024]{2,1,0:T(8,128)S(1)}, f32[32,1024]{1,0:T(8,128)S(1)}, f32[32,1024]{1,0:T(8,128)S(1)}, f32[32,512]{1,0:T(8,128)S(1)}, f32[64,512]{1,0:T(8,128)S(1)}, /*index=5*/f32[64,512]{1,0:T(8,128)S(1)}) custom-call(s32[1]{0:T(128)} %bitcast.1.position, f32[32,1024]{1,0:T(8,128)S(1)} %get-tuple-element.91.local, ...), custom_call_target="tpu_custom_call" | custom-call | flops 1000000000 | bytes 4194304 | tf_op jit(solution)/shard_map/pallas_call | solution.py:552
  22.8 3.5 %collective-permute-done.4.got_chip = f32[64,512]{1,0:T(8,128)S(1)} collective-permute-done((f32[64,512]{1,0:T(8,128)S(1)}, f32[64,512]{1,0:T(8,128)S(1)}, u32[]{:S(2)}, u32[]{:S(2)}) %collective-permute-start.4) | collective-permute-done | bytes 131104 | tf_op jit(solution)/shard_map/ppermute | solution.py:472
  26.3 3.5 %shard_map.72 = (f32[8,32,1024]{2,1,0:T(8,128)S(1)}, f32[32,1024]{1,0:T(8,128)S(1)}, f32[32,1024]{1,0:T(8,128)S(1)}, f32[32,1024]{1,0:T(8,128)S(1)}, f32[32,512]...) custom-call(f32[8,32,1024]{2,1,0:T(8,128)S(1)} %get-tuple-element.99.kept_in, ...), custom_call_target="tpu_custom_call", output_to_operand_aliasing={{0}: (0, {})} | custom-call | flops 1000000000 | bytes 4194304 | tf_op jit(solution)/shard_map/pallas_call | solution.py:586
  29.8 6.1 %collective-permute-start.5 = (f32[64,512]{1,0:T(8,128)S(1)}, f32[64,512]{1,0:T(8,128)S(1)}, u32[]{:S(2)}, u32[]{:S(2)}) collective-permute-start(f32[64,512]{1,0:T(8,128)S(1)} %get-tuple-element.117), channel_id=1, source_target_pairs={{0,4},{4,0},{8,12},{12,8},{16,20},{20,16},{24,28},{28,24},{32,36},... | collective-permute-start | bytes 393224 | tf_op jit(solution)/shard_map/ppermute | solution.py:472
  37.0 3.3 %collective-permute-done.6.got_chip = f32[64,512]{1,0:T(8,128)S(1)} collective-permute-done((f32[64,512]{1,0:T(8,128)S(1)}, f32[64,512]{1,0:T(8,128)S(1)}, u32[]{:S(2)}, u32[]{:S(2)}) %collective-permute-start.6) | collective-permute-done | bytes 131104 | tf_op jit(solution)/shard_map/ppermute | solution.py:472
  40.3 3.5 %shard_map.74 = (f32[8,32,1024]{2,1,0:T(8,128)S(1)}, f32[32,1024]{1,0:T(8,128)S(1)}, f32[32,1024]{1,0:T(8,128)S(1)}, f32[32,1024]{1,0:T(8,128)S(1)}, f32[32,512]...) custom-call(f32[8,32,1024]{2,1,0:T(8,128)S(1)} %get-tuple-element.109.kept_in, ...), custom_call_target="tpu_custom_call", output_to_operand_aliasing={{0}: (0, {})} | custom-call | flops 1000000000 | bytes 4194304 | tf_op jit(solution)/shard_map/pallas_call | solution.py:586
  43.9 3.7 %collective-permute-start.9 = (f32[64,512]{1,0:T(8,128)S(1)}, f32[64,512]{1,0:T(8,128)S(1)}, u32[]{:S(2)}, u32[]{:S(2)}) collective-permute-start(f32[64,512]{1,0:T(8,128)S(1)} %get-tuple-element.124), channel_id=1, source_target_pairs={{0,4},{4,0},{8,12},{12,8},{16,20},{20,16},{24,28},{28,24},{32,36},... | collective-permute-start | bytes 393224 | tf_op jit(solution)/shard_map/ppermute | solution.py:472
  47.6 1.0 shard_map.75
  48.6 1.8 %collective-permute-start.7 = (f32[16,384]{1,0:T(8,128)S(1)}, f32[16,384]{1,0:T(8,128)S(1)}, u32[]{:S(2)}, u32[]{:S(2)}) collective-permute-start(f32[16,384]{1,0:T(8,128)S(1)} %get-tuple-element.123), channel_id=1, source_target_pairs={{0,4},{4,0},{8,12},{12,8},{16,20},{20,16},{24,28},{28,24},{32,36},... | collective-permute-start | bytes 73736 | tf_op jit(solution)/shard_map/ppermute | solution.py:472
  51.4 2.9 %collective-permute-done.8.right = f32[16,384]{1,0:T(8,128)S(1)} collective-permute-done((f32[16,384]{1,0:T(8,128)S(1)}, f32[16,384]{1,0:T(8,128)S(1)}, u32[]{:S(2)}, u32[]{:S(2)}) %collective-permute-start.8) | collective-permute-done | bytes 24608 | tf_op jit(solution)/shard_map/ppermute | solution.py:472
  54.4 3.3 %shard_map.78 = (f32[8,32,1024]{2,1,0:T(8,128)S(1)}, f32[32,1024]{1,0:T(8,128)}, f32[32,1024]{1,0:T(8,128)}, f32[16,128]{1,0:T(8,128)S(1)}, f32[16,128]{1,0:T(8,128)S(1)}) custom-call(f32[8,32,1024]{2,1,0:T(8,128)S(1)} %get-tuple-element.127.kept_in, s32[1]{0:T(128)} %bitcast.1.position, ...), custom_call_target="tpu_custom_call", output_to_operand_aliasing={{0}: (0, {})} | custom-call | flops 1000000000 | bytes 4194304 | tf_op jit(solution)/shard_map/pallas_call | solution.py:586
  57.8 1.7 %collective-permute-start.13 = (f32[16,128]{1,0:T(8,128)S(1)}, f32[16,128]{1,0:T(8,128)S(1)}, u32[]{:S(2)}, u32[]{:S(2)}) collective-permute-start(f32[16,128]{1,0:T(8,128)S(1)} %get-tuple-element.137), channel_id=1, source_target_pairs={{0,4},{4,0},{8,12},{12,8},{16,20},{20,16},{24,28},{28,24},{32,36},... | collective-permute-start | bytes 24584 | tf_op jit(solution)/shard_map/ppermute | solution.py:472
  60.3 1.0 collective-permute-done.12.right
  61.3 1.5 %collective-permute-start.15 = (f32[16,128]{1,0:T(8,128)S(1)}, f32[16,128]{1,0:T(8,128)S(1)}, u32[]{:S(2)}, u32[]{:S(2)}) collective-permute-start(f32[16,128]{1,0:T(8,128)S(1)} %shard_map.81.left), channel_id=1, source_target_pairs={{0,64},{4,68},{8,72},{12,76},{16,80},{20,84},{24,88},{28,92},{32,9... | collective-permute-start | bytes 24584 | tf_op jit(solution)/shard_map/ppermute | solution.py:472
  62.9 1.1 %collective-permute-done.15.right = f32[16,128]{1,0:T(8,128)S(1)} collective-permute-done((f32[16,128]{1,0:T(8,128)S(1)}, f32[16,128]{1,0:T(8,128)S(1)}, u32[]{:S(2)}, u32[]{:S(2)}) %collective-permute-start.15) | collective-permute-done | bytes 8224 | tf_op jit(solution)/shard_map/ppermute | solution.py:472
  63.9 2.2 %collective-permute-done.14.right = f32[16,384]{1,0:T(8,128)S(1)} collective-permute-done((f32[16,384]{1,0:T(8,128)S(1)}, f32[16,384]{1,0:T(8,128)S(1)}, u32[]{:S(2)}, u32[]{:S(2)}) %collective-permute-start.14) | collective-permute-done | bytes 24608 | tf_op jit(solution)/shard_map/ppermute | solution.py:472
  67.0 1.5 %collective-permute-start.17 = (f32[16,128]{1,0:T(8,128)S(1)}, f32[16,128]{1,0:T(8,128)S(1)}, u32[]{:S(2)}, u32[]{:S(2)}) collective-permute-start(f32[16,128]{1,0:T(8,128)S(1)} %shard_map.83.left), channel_id=1, source_target_pairs={{0,8},{4,12},{8,0},{12,4},{16,24},{20,28},{24,16},{28,20},{32,40},... | collective-permute-start | bytes 24584 | tf_op jit(solution)/shard_map/ppermute | solution.py:472
  68.5 1.3 %collective-permute-done.17.right = f32[16,128]{1,0:T(8,128)S(1)} collective-permute-done((f32[16,128]{1,0:T(8,128)S(1)}, f32[16,128]{1,0:T(8,128)S(1)}, u32[]{:S(2)}, u32[]{:S(2)}) %collective-permute-start.17) | collective-permute-done | bytes 8224 | tf_op jit(solution)/shard_map/ppermute | solution.py:472
  70.0 5.2 %collective-permute-start.18 = (f32[16,384]{1,0:T(8,128)S(1)}, f32[16,384]{1,0:T(8,128)S(1)}, u32[]{:S(2)}, u32[]{:S(2)}) collective-permute-start(f32[16,384]{1,0:T(8,128)S(1)} %shard_map.84.mine), channel_id=1, source_target_pairs={{0,4},{4,0},{8,12},{12,8},{16,20},{20,16},{24,28},{28,24},{32,36},... | collective-permute-start | bytes 73736 | tf_op jit(solution)/shard_map/ppermute | solution.py:472
  75.2 1.7 %collective-permute-start.19 = (f32[16,128]{1,0:T(8,128)S(1)}, f32[16,128]{1,0:T(8,128)S(1)}, u32[]{:S(2)}, u32[]{:S(2)}) collective-permute-start(f32[16,128]{1,0:T(8,128)S(1)} %shard_map.85.left), channel_id=1, source_target_pairs={{0,192},{4,196},{8,200},{12,204},{16,208},{20,212},{24,216},{28,22... | collective-permute-start | bytes 24584 | tf_op jit(solution)/shard_map/ppermute | solution.py:472
  76.9 3.6 %shard_map.86 = (f32[96,256]{1,0:T(8,128)S(1)}, f32[96,256]{1,0:T(8,128)S(1)}, f32[288,256]{1,0:T(8,128)S(1)}, f32[288,256]{1,0:T(8,128)S(1)}, f32[32,256]{1,0:T(8,128)S(1)}) custom-call(s32[1]{0:T(128)} %bitcast.1.position, f32[16,384]{1,0:T(8,128)S(1)} %shard_map.84.mine, f32[16,384]{1,0:T(8,128)S(1)} %collective-permute-done.18.other), custom_call_target="tpu_custom_call" | custom-call | flops 3000000000 | bytes 4194304 | tf_op jit(solution)/shard_map/pallas_call | solution.py:612
  80.5 2.0 %collective-permute-start.20 = (f32[16,128]{1,0:T(8,128)S(1)}, f32[16,128]{1,0:T(8,128)S(1)}, u32[]{:S(2)}, u32[]{:S(2)}) collective-permute-start(f32[16,128]{1,0:T(8,128)S(1)} %shard_map.87.left), channel_id=1, source_target_pairs={{0,48},{4,52},{8,56},{12,60},{16,32},{20,36},{24,40},{28,44},{32,1... | collective-permute-start | bytes 24584 | tf_op jit(solution)/shard_map/ppermute | solution.py:472
  82.5 4.1 %shard_map.88 = (f32[160,256]{1,0:T(8,128)S(1)}, f32[160,256]{1,0:T(8,128)S(1)}, f32[224,256]{1,0:T(8,128)S(1)}, f32[224,256]{1,0:T(8,128)S(1)}, f32[96,256]{1,0:T(8,128)S(1)}) custom-call(f32[96,256]{1,0:T(8,128)S(1)} %get-tuple-element.150.refs_0_, f32[96,256]{1,0:T(8,128)S(1)} %get-tuple-element.151.refs_1_, f32[288,256]{1,0:T(8,128)S(1)} %get-tuple-element.152.refs_2_, ...), custom_call_target="tpu_custom_call" | custom-call | flops 3000000000 | bytes 4194304 | tf_op jit(solution)/shard_map/pallas_call | solution.py:612
  86.8 2.8 %shard_map.90 = (f32[224,256]{1,0:T(8,128)S(1)}, f32[32,256]{1,0:T(8,128)S(1)}, f32[224,256]{1,0:T(8,128)S(1)}, f32[160,256]{1,0:T(8,128)S(1)}, f32[160,256]{1,0:T(8,128)S(1)}) custom-call(f32[160,256]{1,0:T(8,128)S(1)} %get-tuple-element.161.refs_0_.direction, f32[160,256]{1,0:T(8,128)S(1)} %get-tuple-element.162.refs_1_, ...), custom_call_target="tpu_custom_call" | custom-call | flops 3000000000 | bytes 4194304 | tf_op jit(solution)/shard_map/pallas_call | solution.py:612
  90.2 1.8 %collective-permute-start.22 = (f32[16,128]{1,0:T(8,128)S(1)}, f32[16,128]{1,0:T(8,128)S(1)}, u32[]{:S(2)}, u32[]{:S(2)}) collective-permute-start(f32[16,128]{1,0:T(8,128)S(1)} %shard_map.91.mine_late), channel_id=1, source_target_pairs={{0,4},{4,0},{8,12},{12,8},{16,20},{20,16},{24,28},{28,24},{32,36},... | collective-permute-start | bytes 24584 | tf_op jit(solution)/shard_map/ppermute | solution.py:472
  92.8 9.7 %shard_map.92 = (f32[4,32,1024]{2,1,0:T(8,128)}, f32[4,32,32]{2,1,0:T(8,128)}) custom-call(s32[1]{0:T(128)} %bitcast.node, s32[1]{0:T(128)} %bitcast.1.position, f32[2,16,8]{2,1,0:T(8,128)S(1)} %copy-done.2, f32[16,384]{1,0:T(8,128)S(1)} %shard_map.84.mine, f32[16,384]{1,0:T(8,128)S(1)} %collective-permute-done.18.other, f32[16,128]{1,0:T(8,128)S(1)} %shard_map.91.mine_late, ...), custom_call_target="tpu_custom_call" | custom-call | tf_op jit(solution)/shard_map/pallas_call | solution.py:622
  (53 shorter events, 8.2 us)
Async XLA Ops:
  0.6 6.2 %copy-start.1 = (f32[32,1024]{1,0:T(8,128)S(1)}, f32[32,1024]{1,0:T(8,128)}, u32[]{:S(2)}) copy-start(f32[32,1024]{1,0:T(8,128)} %k0.1) | copy-start | bytes 393220
  0.6 6.2 %copy-start = (f32[8,3,128,128]{3,2,1,0:T(8,128)S(1)}, f32[8,3,128,128]{3,2,1,0:T(8,128)}, u32[]{:S(2)}) copy-start(f32[8,3,128,128]{3,2,1,0:T(8,128)} %coup.1) | copy-start | bytes 4718596
  0.6 6.2 %copy-start.3 = (s32[8,3]{0,1:T(4,128)S(1)}, s32[8,3]{0,1:T(4,128)}, u32[]{:S(2)}) copy-start(s32[8,3]{0,1:T(4,128)} %param.8) | copy-start | bytes 292
  3.7 7.6 %collective-permute-start.1 = (f32[32,512]{1,0:T(8,128)}, f32[32,512]{1,0:T(8,128)S(1)}, u32[]{:S(2)}, u32[]{:S(2)}) collective-permute-start(f32[32,512]{1,0:T(8,128)} %get-tuple-element.90.after), channel_id=1, source_target_pairs={{0,252},{4,8},{8,4},{12,16},{16,12},{20,24},{24,20},{28,32},{32,28... | collective-permute-start | bytes 196616 | tf_op jit(solution)/shard_map/ppermute | solution.py:472
  6.8 1.0 %copy-start.4 = (f32[8,128,128]{2,1,0:T(8,128)S(1)}, f32[8,128,128]{2,1,0:T(8,128)}, u32[]{:S(2)}) copy-start(f32[8,128,128]{2,1,0:T(8,128)} %diag.1) | copy-start | bytes 1572868
  7.9 0.8 copy-start.5
  8.7 2.7 %copy-start.6 = (f32[32,512]{1,0:T(8,128)S(1)}, f32[32,512]{1,0:T(8,128)}, u32[]{:S(2)}) copy-start(f32[32,512]{1,0:T(8,128)} %get-tuple-element.92) | copy-start | bytes 196612
  11.3 10.3 %collective-permute-start.2 = (f32[10,128,128]{2,1,0:T(8,128)S(1)}, f32[10,128,128]{2,1,0:T(8,128)S(1)}, u32[]{:S(2)}, u32[]{:S(2)}) collective-permute-start(f32[10,128,128]{2,1,0:T(8,128)S(1)} %get-tuple-element.104), channel_id=1, source_target_pairs={{0,4},{4,8},{8,12},{12,16},{16,20},{20,24},{24,28},{28,32},{32,36}... | collective-permute-start | bytes 1966088 | tf_op jit(solution)/shard_map/ppermute | solution.py:472
  11.4 7.9 %collective-permute-start = (f32[32,512]{1,0:T(8,128)S(1)}, f32[32,512]{1,0:T(8,128)S(1)}, u32[]{:S(2)}, u32[]{:S(2)}) collective-permute-start(f32[32,512]{1,0:T(8,128)S(1)} %copy-done.6), channel_id=1, source_target_pairs={{0,4},{4,0},{8,12},{12,8},{16,20},{20,16},{24,28},{28,24},{32,36},... | collective-permute-start | bytes 196616 | tf_op jit(solution)/shard_map/ppermute | solution.py:472
  21.4 1.4 %collective-permute-start.3 = (f32[64,512]{1,0:T(8,128)S(1)}, f32[64,512]{1,0:T(8,128)S(1)}, u32[]{:S(2)}, u32[]{:S(2)}) collective-permute-start(f32[64,512]{1,0:T(8,128)S(1)} %get-tuple-element.106), channel_id=1, source_target_pairs={{0,4},{4,0},{8,12},{12,8},{16,20},{20,16},{24,28},{28,24},{32,36},... | collective-permute-start | bytes 393224 | tf_op jit(solution)/shard_map/ppermute | solution.py:472
  21.6 4.7 %collective-permute-start.4 = (f32[64,512]{1,0:T(8,128)S(1)}, f32[64,512]{1,0:T(8,128)S(1)}, u32[]{:S(2)}, u32[]{:S(2)}) collective-permute-start(f32[64,512]{1,0:T(8,128)S(1)} %get-tuple-element.107), channel_id=1, source_target_pairs={{0,252},{4,8},{8,4},{12,16},{16,12},{20,24},{24,20},{28,32},{32,28... | collective-permute-start | bytes 393224 | tf_op jit(solution)/shard_map/ppermute | solution.py:472
  29.8 7.2 %collective-permute-start.5 = (f32[64,512]{1,0:T(8,128)S(1)}, f32[64,512]{1,0:T(8,128)S(1)}, u32[]{:S(2)}, u32[]{:S(2)}) collective-permute-start(f32[64,512]{1,0:T(8,128)S(1)} %get-tuple-element.117), channel_id=1, source_target_pairs={{0,4},{4,0},{8,12},{12,8},{16,20},{20,16},{24,28},{28,24},{32,36},... | collective-permute-start | bytes 393224 | tf_op jit(solution)/shard_map/ppermute | solution.py:472
  35.9 4.4 %collective-permute-start.6 = (f32[64,512]{1,0:T(8,128)S(1)}, f32[64,512]{1,0:T(8,128)S(1)}, u32[]{:S(2)}, u32[]{:S(2)}) collective-permute-start(f32[64,512]{1,0:T(8,128)S(1)} %get-tuple-element.118), channel_id=1, source_target_pairs={{0,252},{4,8},{8,4},{12,16},{16,12},{20,24},{24,20},{28,32},{32,28... | collective-permute-start | bytes 393224 | tf_op jit(solution)/shard_map/ppermute | solution.py:472
  43.9 10.4 %collective-permute-start.9 = (f32[64,512]{1,0:T(8,128)S(1)}, f32[64,512]{1,0:T(8,128)S(1)}, u32[]{:S(2)}, u32[]{:S(2)}) collective-permute-start(f32[64,512]{1,0:T(8,128)S(1)} %get-tuple-element.124), channel_id=1, source_target_pairs={{0,4},{4,0},{8,12},{12,8},{16,20},{20,16},{24,28},{28,24},{32,36},... | collective-permute-start | bytes 393224 | tf_op jit(solution)/shard_map/ppermute | solution.py:472
  47.6 6.7 %collective-permute-start.10 = (f32[64,512]{1,0:T(8,128)S(1)}, f32[64,512]{1,0:T(8,128)S(1)}, u32[]{:S(2)}, u32[]{:S(2)}) collective-permute-start(f32[64,512]{1,0:T(8,128)S(1)} %get-tuple-element.125), channel_id=1, source_target_pairs={{0,252},{4,8},{8,4},{12,16},{16,12},{20,24},{24,20},{28,32},{32,28... | collective-permute-start | bytes 393224 | tf_op jit(solution)/shard_map/ppermute | solution.py:472
  48.6 2.7 %collective-permute-start.7 = (f32[16,384]{1,0:T(8,128)S(1)}, f32[16,384]{1,0:T(8,128)S(1)}, u32[]{:S(2)}, u32[]{:S(2)}) collective-permute-start(f32[16,384]{1,0:T(8,128)S(1)} %get-tuple-element.123), channel_id=1, source_target_pairs={{0,4},{4,0},{8,12},{12,8},{16,20},{20,16},{24,28},{28,24},{32,36},... | collective-permute-start | bytes 73736 | tf_op jit(solution)/shard_map/ppermute | solution.py:472
  51.3 3.0 %collective-permute-start.8 = (f32[16,384]{1,0:T(8,128)S(1)}, f32[16,384]{1,0:T(8,128)S(1)}, u32[]{:S(2)}, u32[]{:S(2)}) collective-permute-start(f32[16,384]{1,0:T(8,128)S(1)} %shard_map.76.left), channel_id=1, source_target_pairs={{0,8},{4,12},{8,0},{12,4},{16,24},{20,28},{24,16},{28,20},{32,40},... | collective-permute-start | bytes 73736 | tf_op jit(solution)/shard_map/ppermute | solution.py:472
  54.3 3.4 %collective-permute-start.11 = (f32[16,384]{1,0:T(8,128)S(1)}, f32[16,384]{1,0:T(8,128)S(1)}, u32[]{:S(2)}, u32[]{:S(2)}) collective-permute-start(f32[16,384]{1,0:T(8,128)S(1)} %shard_map.77.left), channel_id=1, source_target_pairs={{0,64},{4,68},{8,72},{12,76},{16,80},{20,84},{24,88},{28,92},{32,9... | collective-permute-start | bytes 73736 | tf_op jit(solution)/shard_map/ppermute | solution.py:472
  57.7 3.7 %collective-permute-start.12 = (f32[16,384]{1,0:T(8,128)S(1)}, f32[16,384]{1,0:T(8,128)S(1)}, u32[]{:S(2)}, u32[]{:S(2)}) collective-permute-start(f32[16,384]{1,0:T(8,128)S(1)} %shard_map.79.left), channel_id=1, source_target_pairs={{0,16},{4,20},{8,24},{12,28},{16,0},{20,4},{24,8},{28,12},{32,48},... | collective-permute-start | bytes 73736 | tf_op jit(solution)/shard_map/ppermute | solution.py:472
  57.8 2.5 %collective-permute-start.13 = (f32[16,128]{1,0:T(8,128)S(1)}, f32[16,128]{1,0:T(8,128)S(1)}, u32[]{:S(2)}, u32[]{:S(2)}) collective-permute-start(f32[16,128]{1,0:T(8,128)S(1)} %get-tuple-element.137), channel_id=1, source_target_pairs={{0,4},{4,0},{8,12},{12,8},{16,20},{20,16},{24,28},{28,24},{32,36},... | collective-permute-start | bytes 24584 | tf_op jit(solution)/shard_map/ppermute | solution.py:472
  61.3 4.8 %collective-permute-start.14 = (f32[16,384]{1,0:T(8,128)S(1)}, f32[16,384]{1,0:T(8,128)S(1)}, u32[]{:S(2)}, u32[]{:S(2)}) collective-permute-start(f32[16,384]{1,0:T(8,128)S(1)} %shard_map.80.left), channel_id=1, source_target_pairs={{0,48},{4,52},{8,56},{12,60},{16,32},{20,36},{24,40},{28,44},{32,1... | collective-permute-start | bytes 73736 | tf_op jit(solution)/shard_map/ppermute | solution.py:472
  61.3 2.6 %collective-permute-start.15 = (f32[16,128]{1,0:T(8,128)S(1)}, f32[16,128]{1,0:T(8,128)S(1)}, u32[]{:S(2)}, u32[]{:S(2)}) collective-permute-start(f32[16,128]{1,0:T(8,128)S(1)} %shard_map.81.left), channel_id=1, source_target_pairs={{0,64},{4,68},{8,72},{12,76},{16,80},{20,84},{24,88},{28,92},{32,9... | collective-permute-start | bytes 24584 | tf_op jit(solution)/shard_map/ppermute | solution.py:472
  66.1 3.9 %collective-permute-start.16 = (f32[16,384]{1,0:T(8,128)S(1)}, f32[16,384]{1,0:T(8,128)S(1)}, u32[]{:S(2)}, u32[]{:S(2)}) collective-permute-start(f32[16,384]{1,0:T(8,128)S(1)} %shard_map.82.left), channel_id=1, source_target_pairs={{0,192},{4,196},{8,200},{12,204},{16,208},{20,212},{24,216},{28,22... | collective-permute-start | bytes 73736 | tf_op jit(solution)/shard_map/ppermute | solution.py:472
  67.0 2.7 %collective-permute-start.17 = (f32[16,128]{1,0:T(8,128)S(1)}, f32[16,128]{1,0:T(8,128)S(1)}, u32[]{:S(2)}, u32[]{:S(2)}) collective-permute-start(f32[16,128]{1,0:T(8,128)S(1)} %shard_map.83.left), channel_id=1, source_target_pairs={{0,8},{4,12},{8,0},{12,4},{16,24},{20,28},{24,16},{28,20},{32,40},... | collective-permute-start | bytes 24584 | tf_op jit(solution)/shard_map/ppermute | solution.py:472
  70.0 6.9 %collective-permute-start.18 = (f32[16,384]{1,0:T(8,128)S(1)}, f32[16,384]{1,0:T(8,128)S(1)}, u32[]{:S(2)}, u32[]{:S(2)}) collective-permute-start(f32[16,384]{1,0:T(8,128)S(1)} %shard_map.84.mine), channel_id=1, source_target_pairs={{0,4},{4,0},{8,12},{12,8},{16,20},{20,16},{24,28},{28,24},{32,36},... | collective-permute-start | bytes 73736 | tf_op jit(solution)/shard_map/ppermute | solution.py:472
  75.2 5.3 %collective-permute-start.19 = (f32[16,128]{1,0:T(8,128)S(1)}, f32[16,128]{1,0:T(8,128)S(1)}, u32[]{:S(2)}, u32[]{:S(2)}) collective-permute-start(f32[16,128]{1,0:T(8,128)S(1)} %shard_map.85.left), channel_id=1, source_target_pairs={{0,192},{4,196},{8,200},{12,204},{16,208},{20,212},{24,216},{28,22... | collective-permute-start | bytes 24584 | tf_op jit(solution)/shard_map/ppermute | solution.py:472
  80.5 6.1 %collective-permute-start.20 = (f32[16,128]{1,0:T(8,128)S(1)}, f32[16,128]{1,0:T(8,128)S(1)}, u32[]{:S(2)}, u32[]{:S(2)}) collective-permute-start(f32[16,128]{1,0:T(8,128)S(1)} %shard_map.87.left), channel_id=1, source_target_pairs={{0,48},{4,52},{8,56},{12,60},{16,32},{20,36},{24,40},{28,44},{32,1... | collective-permute-start | bytes 24584 | tf_op jit(solution)/shard_map/ppermute | solution.py:472
  86.7 6.1 %copy-start.2 = (f32[2,16,8]{2,1,0:T(8,128)S(1)}, f32[2,16,8]{2,1,0:T(8,128)}, u32[]{:S(2)}) copy-start(f32[2,16,8]{2,1,0:T(8,128)} %constant.11.clone.weights) | copy-start | bytes 3076
  86.7 3.5 %collective-permute-start.21 = (f32[16,128]{1,0:T(8,128)S(1)}, f32[16,128]{1,0:T(8,128)S(1)}, u32[]{:S(2)}, u32[]{:S(2)}) collective-permute-start(f32[16,128]{1,0:T(8,128)S(1)} %shard_map.89.left), channel_id=1, source_target_pairs={{0,16},{4,20},{8,24},{12,28},{16,0},{20,4},{24,8},{28,12},{32,48},... | collective-permute-start | bytes 24584 | tf_op jit(solution)/shard_map/ppermute | solution.py:472
  90.2 2.6 %collective-permute-start.22 = (f32[16,128]{1,0:T(8,128)S(1)}, f32[16,128]{1,0:T(8,128)S(1)}, u32[]{:S(2)}, u32[]{:S(2)}) collective-permute-start(f32[16,128]{1,0:T(8,128)S(1)} %shard_map.91.mine_late), channel_id=1, source_target_pairs={{0,4},{4,0},{8,12},{12,8},{16,20},{20,16},{24,28},{28,24},{32,36},... | collective-permute-start | bytes 24584 | tf_op jit(solution)/shard_map/ppermute | solution.py:472

commit v3 on v2

--- a/solution.py
+++ b/solution.py
@@ -465,6 +465,12 @@
 
 def add_body(left, right, out):
     out[...] = left[...] + right[...]
+
+
+def pack_body(early, early_got, late, late_got, out):
+    lanes = early.shape[1]
+    out[:, :lanes] = early[...] + early_got[...]
+    out[:, lanes:] = late[...] + late_got[...]
 
 
 def exchange(value, partner):
@@ -544,7 +550,7 @@
         flops=10**9,
         bytes_accessed=4 << 20,
         vmem=16,
-    )(near_by, flag, diag_blocks, couplings, probes, pay_chip)
+    )(near_by, flag, diag_blocks, couplings, probes, got_core)
     edge, got_chip = lax.optimization_barrier((edge, got_chip))
     edge = exchange(edge, lambda i: i + 1)
     blocks = (thi, tlo, uhi, ulo)
@@ -603,9 +609,12 @@
         return array(blocks * PROBES, WIDTH)
 
     work = dict(flops=3 * 10**9, bytes_accessed=4 << 20, vmem=16)
-    early, late = lax.optimization_barrier((stage(early, 1), add(late, exchange(other, core_partner))))
-    early, late = lax.optimization_barrier((stage(early, 2), stage(late, 3)))
-    early, late = lax.optimization_barrier((stage(early, 4), stage(late, 0)))
+    lanes = early.shape[1]
+    pack = call(pack_body, array(PROBES // 2, lanes + late.shape[1]), [VMEM] * 4, vmem=4)(
+        early, exchange(early, functools.partial(ring_partner, 1)), late, exchange(other, core_partner)
+    )
+    pack = stage(stage(pack, 2), 4)
+    early, late = pack[:, :lanes], pack[:, lanes:]
 
     def beside(number, body, blocks, specs, *args):
         got = exchange(late, functools.partial(ring_partner, number))
@@ -614,8 +623,8 @@
         return add(late, got), made
 
     early = (early, exchange(early, core_partner))
-    late, state = beside(4, zeroth_body, (3, 3, 9, 9, 1), [SMEM, VMEM, VMEM], flag, *early)
-    late, state = beside(2, iterate_body, (5, 5, 7, 7, 3), [VMEM] * 5, *state)
+    late, state = beside(3, zeroth_body, (3, 3, 9, 9, 1), [SMEM, VMEM, VMEM], flag, *early)
+    late, state = beside(0, iterate_body, (5, 5, 7, 7, 3), [VMEM] * 5, *state)
     direction, _, dir_against, _, _ = state
     late, state = beside(1, alpha_body, (7, 1, 7, 5, 5), [VMEM] * 5, *state)
     late = (late, exchange(late, core_partner))

time: 103 us -> 101 us (0.981)
  starting transfers between devices: 38 us -> 34.9 us
  waiting for transfers between devices: 20.7 us -> 22.2 us
    ppermute x23 -> x21, starting transfers between devices: 38 us -> 34.9 us  [exchange(): lax.ppermute(value, 'row', [(source, partner(source) % count) for source...]
    ppermute x23 -> x21, waiting for transfers between devices: 20.7 us -> 22.2 us  [exchange(): lax.ppermute(value, 'row', [(source, partner(source) % count) for source...]
  transfers between devices with their start and end apart: 23 -> 21, of which waited for: 14 -> 12; matrix products, arithmetic and copies ran while one was open for 0% -> 0% of each run, Pallas kernels for 21% -> 21%
where the time goes in v3:
time: 101 us; the launch traced here: 100 us
  Pallas kernels  41.1 us (41%)
  starting transfers between devices  34.9 us (35%)
  waiting for transfers between devices  22.2 us (22%)
  local copies, waits for them, and re-layouts  1.06 us (1%)
  between operations  1.06 us (1%)
    ppermute x21, starting transfers between devices, exchange(): lax.ppermute(value, 'row', [(source, partner(source) % count) for source...  34.9 us
    ppermute x21, waiting for transfers between devices, exchange(): lax.ppermute(value, 'row', [(source, partner(source) % count) for source...  22.2 us
    pallas_call x3, Pallas kernels, beside(): made = call(body, tuple(map(coeffs, blocks)), specs, **work)(*args)  10.5 us
    pallas_call x3, Pallas kernels, shards(): call(functools.partial(double_body, degree=degree), outs, [HBM, SMEM] + [...  10.4 us
    pallas_call x1, Pallas kernels, shards(): call(moments_body, (array(moment_share, PROBES, ROWS), array(moment_share...  9.73 us
    pallas_call x1, Pallas kernels, shards(): call(cross_body, (message, message), [SMEM, SMEM, HBM, HBM], vmem=56, scr...  3.01 us
    pallas_call x3, Pallas kernels, shards(): call(functools.partial(shadow_body, count=len(fresh), first=first, last=n...  2.73 us
    pallas_call x1, Pallas kernels, shards(): call(first_body, band + cross + (array(len(EDGE), BLOCK, BLOCK), vector,...  2.58 us
  transfers between devices with their start and end apart: 21, of which 12 were waited for; matrix products, arithmetic and copies ran while one was open for 0% of the time, Pallas kernels for 21%

profile of v3, /device:TPU:1, one launch (start us, length us, event | category | flops | bytes accessed | tf_op | source)
XLA Modules:
  0.0 100.4 jit_solution(14767728801648739098)
XLA Ops:
  0.7 3.0 %shard_map.68 = (f32[32,512]{1,0:T(8,128)}, f32[32,512]{1,0:T(8,128)}) custom-call(s32[3,8]{1,0:T(4,128)} %bitcast.3, s32[1]{0:T(128)} %bitcast.1.position, f32[8,3,128,128]{3,2,1,0:T(8,128)} %coup.1, f32[32,1024]{1,0:T(8,128)} %k0.1), custom_call_target="tpu_custom_call" | custom-call | tf_op jit(solution)/shard_map/pallas_call | solution.py:531
  3.7 3.3 %collective-permute-start = (f32[32,512]{1,0:T(8,128)}, f32[32,512]{1,0:T(8,128)S(1)}, u32[]{:S(2)}, u32[]{:S(2)}) collective-permute-start(f32[32,512]{1,0:T(8,128)} %get-tuple-element.84), channel_id=1, source_target_pairs={{0,4},{4,0},{8,12},{12,8},{16,20},{20,16},{24,28},{28,24},{32,36},... | collective-permute-start | bytes 196616 | tf_op jit(solution)/shard_map/ppermute | solution.py:478
  7.0 1.1 %collective-permute-done.after.got_core = f32[32,512]{1,0:T(8,128)S(1)} collective-permute-done((f32[32,512]{1,0:T(8,128)}, f32[32,512]{1,0:T(8,128)S(1)}, u32[]{:S(2)}, u32[]{:S(2)}) %collective-permute-start) | collective-permute-done | bytes 65568 | tf_op jit(solution)/shard_map/ppermute | solution.py:478
  8.1 1.0 %copy-done.4 = f32[8,128,128]{2,1,0:T(8,128)S(1)} copy-done((f32[8,128,128]{2,1,0:T(8,128)S(1)}, f32[8,128,128]{2,1,0:T(8,128)}, u32[]{:S(2)}) %copy-start.4) | copy-done | bytes 524312
  9.2 2.6 %shard_map.69 = (bf16[9,256,256]{2,1,0:T(8,128)(2,1)S(1)}, bf16[9,256,256]{2,1,0:T(8,128)(2,1)S(1)}, bf16[3,256,256]{2,1,0:T(8,128)(2,1)S(1)}, bf16[3,256,256]{2...) custom-call(s32[3,8]{1,0:T(4,128)S(1)} %bitcast.4, ...), custom_call_target="tpu_custom_call" | custom-call | flops 1000000000 | bytes 4194304 | tf_op jit(solution)/shard_map/pallas_call | solution.py:546
  12.5 2.1 %shard_map.70 = (f32[8,32,1024]{2,1,0:T(8,128)S(1)}, f32[32,1024]{1,0:T(8,128)S(1)}, f32[32,1024]{1,0:T(8,128)S(1)}, f32[32,512]{1,0:T(8,128)S(1)}, f32[64,512]{1,0:T(8,128)S(1)}, /*index=5*/f32[64,512]{1,0:T(8,128)S(1)}) custom-call(s32[1]{0:T(128)} %bitcast.1.position, f32[32,1024]{1,0:T(8,128)S(1)} %get-tuple-element.85.local, ...), custom_call_target="tpu_custom_call" | custom-call | flops 1000000000 | bytes 4194304 | tf_op jit(solution)/shard_map/pallas_call | solution.py:558
  14.6 5.0 %collective-permute-start.3 = (f32[64,512]{1,0:T(8,128)S(1)}, f32[64,512]{1,0:T(8,128)S(1)}, u32[]{:S(2)}, u32[]{:S(2)}) collective-permute-start(f32[64,512]{1,0:T(8,128)S(1)} %get-tuple-element.100), channel_id=1, source_target_pairs={{0,4},{4,0},{8,12},{12,8},{16,20},{20,16},{24,28},{28,24},{32,36},... | collective-permute-start | bytes 393224 | tf_op jit(solution)/shard_map/ppermute | solution.py:478
  20.0 0.7 shard_map.71
  20.8 3.5 %collective-permute-done.4.got_chip = f32[64,512]{1,0:T(8,128)S(1)} collective-permute-done((f32[64,512]{1,0:T(8,128)S(1)}, f32[64,512]{1,0:T(8,128)S(1)}, u32[]{:S(2)}, u32[]{:S(2)}) %collective-permute-start.4) | collective-permute-done | bytes 131104 | tf_op jit(solution)/shard_map/ppermute | solution.py:478
  24.3 3.5 %shard_map.72 = (f32[8,32,1024]{2,1,0:T(8,128)S(1)}, f32[32,1024]{1,0:T(8,128)S(1)}, f32[32,1024]{1,0:T(8,128)S(1)}, f32[32,1024]{1,0:T(8,128)S(1)}, f32[32,512]...) custom-call(f32[8,32,1024]{2,1,0:T(8,128)S(1)} %get-tuple-element.93.kept_in, ...), custom_call_target="tpu_custom_call", output_to_operand_aliasing={{0}: (0, {})} | custom-call | flops 1000000000 | bytes 4194304 | tf_op jit(solution)/shard_map/pallas_call | solution.py:592
  27.9 7.9 %collective-permute-start.5 = (f32[64,512]{1,0:T(8,128)S(1)}, f32[64,512]{1,0:T(8,128)S(1)}, u32[]{:S(2)}, u32[]{:S(2)}) collective-permute-start(f32[64,512]{1,0:T(8,128)S(1)} %get-tuple-element.111), channel_id=1, source_target_pairs={{0,4},{4,0},{8,12},{12,8},{16,20},{20,16},{24,28},{28,24},{32,36},... | collective-permute-start | bytes 393224 | tf_op jit(solution)/shard_map/ppermute | solution.py:478
  35.8 1.0 shard_map.73
  36.8 3.3 %collective-permute-done.6.got_chip = f32[64,512]{1,0:T(8,128)S(1)} collective-permute-done((f32[64,512]{1,0:T(8,128)S(1)}, f32[64,512]{1,0:T(8,128)S(1)}, u32[]{:S(2)}, u32[]{:S(2)}) %collective-permute-start.6) | collective-permute-done | bytes 131104 | tf_op jit(solution)/shard_map/ppermute | solution.py:478
  40.2 3.5 %shard_map.74 = (f32[8,32,1024]{2,1,0:T(8,128)S(1)}, f32[32,1024]{1,0:T(8,128)S(1)}, f32[32,1024]{1,0:T(8,128)S(1)}, f32[32,1024]{1,0:T(8,128)S(1)}, f32[32,512]...) custom-call(f32[8,32,1024]{2,1,0:T(8,128)S(1)} %get-tuple-element.103.kept_in, ...), custom_call_target="tpu_custom_call", output_to_operand_aliasing={{0}: (0, {})} | custom-call | flops 1000000000 | bytes 4194304 | tf_op jit(solution)/shard_map/pallas_call | solution.py:592
  43.7 3.7 %collective-permute-start.9 = (f32[64,512]{1,0:T(8,128)S(1)}, f32[64,512]{1,0:T(8,128)S(1)}, u32[]{:S(2)}, u32[]{:S(2)}) collective-permute-start(f32[64,512]{1,0:T(8,128)S(1)} %get-tuple-element.118), channel_id=1, source_target_pairs={{0,4},{4,0},{8,12},{12,8},{16,20},{20,16},{24,28},{28,24},{32,36},... | collective-permute-start | bytes 393224 | tf_op jit(solution)/shard_map/ppermute | solution.py:478
  47.4 1.0 shard_map.75
  48.9 0.8 collective-permute-done.7.right
  49.8 1.4 %collective-permute-start.8 = (f32[16,384]{1,0:T(8,128)S(1)}, f32[16,384]{1,0:T(8,128)S(1)}, u32[]{:S(2)}, u32[]{:S(2)}) collective-permute-start(f32[16,384]{1,0:T(8,128)S(1)} %shard_map.76.left), channel_id=1, source_target_pairs={{0,8},{4,12},{8,0},{12,4},{16,24},{20,28},{24,16},{28,20},{32,40},... | collective-permute-start | bytes 73736 | tf_op jit(solution)/shard_map/ppermute | solution.py:478
  51.2 1.2 %collective-permute-done.8.right = f32[16,384]{1,0:T(8,128)S(1)} collective-permute-done((f32[16,384]{1,0:T(8,128)S(1)}, f32[16,384]{1,0:T(8,128)S(1)}, u32[]{:S(2)}, u32[]{:S(2)}) %collective-permute-start.8) | collective-permute-done | bytes 24608 | tf_op jit(solution)/shard_map/ppermute | solution.py:478
  52.6 3.3 %shard_map.78 = (f32[8,32,1024]{2,1,0:T(8,128)S(1)}, f32[32,1024]{1,0:T(8,128)}, f32[32,1024]{1,0:T(8,128)}, f32[16,128]{1,0:T(8,128)S(1)}, f32[16,128]{1,0:T(8,128)S(1)}) custom-call(f32[8,32,1024]{2,1,0:T(8,128)S(1)} %get-tuple-element.121.kept_in, s32[1]{0:T(128)} %bitcast.1.position, ...), custom_call_target="tpu_custom_call", output_to_operand_aliasing={{0}: (0, {})} | custom-call | flops 1000000000 | bytes 4194304 | tf_op jit(solution)/shard_map/pallas_call | solution.py:592
  56.0 3.2 %collective-permute-start.13 = (f32[16,128]{1,0:T(8,128)S(1)}, f32[16,128]{1,0:T(8,128)S(1)}, u32[]{:S(2)}, u32[]{:S(2)}) collective-permute-start(f32[16,128]{1,0:T(8,128)S(1)} %get-tuple-element.131), channel_id=1, source_target_pairs={{0,4},{4,0},{8,12},{12,8},{16,20},{20,16},{24,28},{28,24},{32,36},... | collective-permute-start | bytes 24584 | tf_op jit(solution)/shard_map/ppermute | solution.py:478
  59.2 0.8 collective-permute-done.13.late_got
  60.1 4.9 %collective-permute-done.14.right = f32[16,512]{1,0:T(8,128)S(1)} collective-permute-done((f32[16,512]{1,0:T(8,128)S(1)}, f32[16,512]{1,0:T(8,128)S(1)}, u32[]{:S(2)}, u32[]{:S(2)}) %collective-permute-start.14) | collective-permute-done | bytes 32800 | tf_op jit(solution)/shard_map/ppermute | solution.py:478
  65.6 3.7 %collective-permute-done.15.right = f32[16,512]{1,0:T(8,128)S(1)} collective-permute-done((f32[16,512]{1,0:T(8,128)S(1)}, f32[16,512]{1,0:T(8,128)S(1)}, u32[]{:S(2)}, u32[]{:S(2)}) %collective-permute-start.15) | collective-permute-done | bytes 32800 | tf_op jit(solution)/shard_map/ppermute | solution.py:478
  69.3 6.0 %collective-permute-start.16 = (f32[16,384]{1,0:T(8,128)S(1)}, f32[16,384]{1,0:T(8,128)S(1)}, u32[]{:S(2)}, u32[]{:S(2)}) collective-permute-start(f32[16,384]{1,0:T(8,128)S(1)} %slice.8.mine), channel_id=1, source_target_pairs={{0,4},{4,0},{8,12},{12,8},{16,20},{20,16},{24,28},{28,24},{32,36},... | collective-permute-start | bytes 73736 | tf_op jit(solution)/shard_map/ppermute | solution.py:478
  75.4 0.7 collective-permute-done.16.other
  76.2 3.6 %shard_map.83 = (f32[96,256]{1,0:T(8,128)S(1)}, f32[96,256]{1,0:T(8,128)S(1)}, f32[288,256]{1,0:T(8,128)S(1)}, f32[288,256]{1,0:T(8,128)S(1)}, f32[32,256]{1,0:T(8,128)S(1)}) custom-call(s32[1]{0:T(128)} %bitcast.1.position, f32[16,384]{1,0:T(8,128)S(1)} %slice.8.mine, f32[16,384]{1,0:T(8,128)S(1)} %collective-permute-done.16.other), custom_call_target="tpu_custom_call" | custom-call | flops 3000000000 | bytes 4194304 | tf_op jit(solution)/shard_map/pallas_call | solution.py:621
  80.2 4.1 %shard_map.85 = (f32[160,256]{1,0:T(8,128)S(1)}, f32[160,256]{1,0:T(8,128)S(1)}, f32[224,256]{1,0:T(8,128)S(1)}, f32[224,256]{1,0:T(8,128)S(1)}, f32[96,256]{1,0:T(8,128)S(1)}) custom-call(f32[96,256]{1,0:T(8,128)S(1)} %get-tuple-element.138.refs_0_, f32[96,256]{1,0:T(8,128)S(1)} %get-tuple-element.139.refs_1_, f32[288,256]{1,0:T(8,128)S(1)} %get-tuple-element.140.refs_2_, ...), custom_call_target="tpu_custom_call" | custom-call | flops 3000000000 | bytes 4194304 | tf_op jit(solution)/shard_map/pallas_call | solution.py:621
  84.4 2.8 %shard_map.87 = (f32[224,256]{1,0:T(8,128)S(1)}, f32[32,256]{1,0:T(8,128)S(1)}, f32[224,256]{1,0:T(8,128)S(1)}, f32[160,256]{1,0:T(8,128)S(1)}, f32[160,256]{1,0:T(8,128)S(1)}) custom-call(f32[160,256]{1,0:T(8,128)S(1)} %get-tuple-element.149.refs_0_.direction, f32[160,256]{1,0:T(8,128)S(1)} %get-tuple-element.150.refs_1_, ...), custom_call_target="tpu_custom_call" | custom-call | flops 3000000000 | bytes 4194304 | tf_op jit(solution)/shard_map/pallas_call | solution.py:621
  87.8 1.8 %collective-permute-start.20 = (f32[16,128]{1,0:T(8,128)S(1)}, f32[16,128]{1,0:T(8,128)S(1)}, u32[]{:S(2)}, u32[]{:S(2)}) collective-permute-start(f32[16,128]{1,0:T(8,128)S(1)} %shard_map.88.mine_late), channel_id=1, source_target_pairs={{0,4},{4,0},{8,12},{12,8},{16,20},{20,16},{24,28},{28,24},{32,36},... | collective-permute-start | bytes 24584 | tf_op jit(solution)/shard_map/ppermute | solution.py:478
  89.6 0.8 collective-permute-done.20.other_late
  90.4 9.7 %shard_map.89 = (f32[4,32,1024]{2,1,0:T(8,128)}, f32[4,32,32]{2,1,0:T(8,128)}) custom-call(s32[1]{0:T(128)} %bitcast.node, s32[1]{0:T(128)} %bitcast.1.position, f32[2,16,8]{2,1,0:T(8,128)S(1)} %copy-done.2, f32[16,384]{1,0:T(8,128)S(1)} %slice.8.mine, f32[16,384]{1,0:T(8,128)S(1)} %collective-permute-done.16.other, f32[16,128]{1,0:T(8,128)S(1)} %shard_map.88.mine_late, ...), custom_call_target="tpu_custom_call" | custom-call | tf_op jit(solution)/shard_map/pallas_call | solution.py:631
  (44 shorter events, 3.7 us)
Async XLA Ops:
  0.6 7.5 %copy-start.1 = (f32[32,1024]{1,0:T(8,128)S(1)}, f32[32,1024]{1,0:T(8,128)}, u32[]{:S(2)}) copy-start(f32[32,1024]{1,0:T(8,128)} %k0.1) | copy-start | bytes 393220
  0.6 7.5 %copy-start = (f32[8,3,128,128]{3,2,1,0:T(8,128)S(1)}, f32[8,3,128,128]{3,2,1,0:T(8,128)}, u32[]{:S(2)}) copy-start(f32[8,3,128,128]{3,2,1,0:T(8,128)} %coup.1) | copy-start | bytes 4718596
  0.6 7.5 %copy-start.3 = (s32[8,3]{0,1:T(4,128)S(1)}, s32[8,3]{0,1:T(4,128)}, u32[]{:S(2)}) copy-start(s32[8,3]{0,1:T(4,128)} %param.8) | copy-start | bytes 292
  3.7 4.4 %collective-permute-start = (f32[32,512]{1,0:T(8,128)}, f32[32,512]{1,0:T(8,128)S(1)}, u32[]{:S(2)}, u32[]{:S(2)}) collective-permute-start(f32[32,512]{1,0:T(8,128)} %get-tuple-element.84), channel_id=1, source_target_pairs={{0,4},{4,0},{8,12},{12,8},{16,20},{20,16},{24,28},{28,24},{32,36},... | collective-permute-start | bytes 196616 | tf_op jit(solution)/shard_map/ppermute | solution.py:478
  7.0 4.7 %collective-permute-start.1 = (f32[32,512]{1,0:T(8,128)}, f32[32,512]{1,0:T(8,128)S(1)}, u32[]{:S(2)}, u32[]{:S(2)}) collective-permute-start(f32[32,512]{1,0:T(8,128)} %get-tuple-element.87), channel_id=1, source_target_pairs={{0,252},{4,8},{8,4},{12,16},{16,12},{20,24},{24,20},{28,32},{32,28... | collective-permute-start | bytes 196616 | tf_op jit(solution)/shard_map/ppermute | solution.py:478
  8.1 1.0 %copy-start.4 = (f32[8,128,128]{2,1,0:T(8,128)S(1)}, f32[8,128,128]{2,1,0:T(8,128)}, u32[]{:S(2)}) copy-start(f32[8,128,128]{2,1,0:T(8,128)} %diag.1) | copy-start | bytes 1572868
  11.8 8.2 %collective-permute-start.2 = (f32[10,128,128]{2,1,0:T(8,128)S(1)}, f32[10,128,128]{2,1,0:T(8,128)S(1)}, u32[]{:S(2)}, u32[]{:S(2)}) collective-permute-start(f32[10,128,128]{2,1,0:T(8,128)S(1)} %get-tuple-element.98), channel_id=1, source_target_pairs={{0,4},{4,8},{8,12},{12,16},{16,20},{20,24},{24,28},{28,32},{32,36}... | collective-permute-start | bytes 1966088 | tf_op jit(solution)/shard_map/ppermute | solution.py:478
  14.6 6.2 %collective-permute-start.3 = (f32[64,512]{1,0:T(8,128)S(1)}, f32[64,512]{1,0:T(8,128)S(1)}, u32[]{:S(2)}, u32[]{:S(2)}) collective-permute-start(f32[64,512]{1,0:T(8,128)S(1)} %get-tuple-element.100), channel_id=1, source_target_pairs={{0,4},{4,0},{8,12},{12,8},{16,20},{20,16},{24,28},{28,24},{32,36},... | collective-permute-start | bytes 393224 | tf_op jit(solution)/shard_map/ppermute | solution.py:478
  19.6 4.7 %collective-permute-start.4 = (f32[64,512]{1,0:T(8,128)S(1)}, f32[64,512]{1,0:T(8,128)S(1)}, u32[]{:S(2)}, u32[]{:S(2)}) collective-permute-start(f32[64,512]{1,0:T(8,128)S(1)} %get-tuple-element.101), channel_id=1, source_target_pairs={{0,252},{4,8},{8,4},{12,16},{16,12},{20,24},{24,20},{28,32},{32,28... | collective-permute-start | bytes 393224 | tf_op jit(solution)/shard_map/ppermute | solution.py:478
  27.9 9.0 %collective-permute-start.5 = (f32[64,512]{1,0:T(8,128)S(1)}, f32[64,512]{1,0:T(8,128)S(1)}, u32[]{:S(2)}, u32[]{:S(2)}) collective-permute-start(f32[64,512]{1,0:T(8,128)S(1)} %get-tuple-element.111), channel_id=1, source_target_pairs={{0,4},{4,0},{8,12},{12,8},{16,20},{20,16},{24,28},{28,24},{32,36},... | collective-permute-start | bytes 393224 | tf_op jit(solution)/shard_map/ppermute | solution.py:478
  35.8 4.4 %collective-permute-start.6 = (f32[64,512]{1,0:T(8,128)S(1)}, f32[64,512]{1,0:T(8,128)S(1)}, u32[]{:S(2)}, u32[]{:S(2)}) collective-permute-start(f32[64,512]{1,0:T(8,128)S(1)} %get-tuple-element.112), channel_id=1, source_target_pairs={{0,252},{4,8},{8,4},{12,16},{16,12},{20,24},{24,20},{28,32},{32,28... | collective-permute-start | bytes 393224 | tf_op jit(solution)/shard_map/ppermute | solution.py:478
  43.7 8.7 %collective-permute-start.9 = (f32[64,512]{1,0:T(8,128)S(1)}, f32[64,512]{1,0:T(8,128)S(1)}, u32[]{:S(2)}, u32[]{:S(2)}) collective-permute-start(f32[64,512]{1,0:T(8,128)S(1)} %get-tuple-element.118), channel_id=1, source_target_pairs={{0,4},{4,0},{8,12},{12,8},{16,20},{20,16},{24,28},{28,24},{32,36},... | collective-permute-start | bytes 393224 | tf_op jit(solution)/shard_map/ppermute | solution.py:478
  47.4 5.1 %collective-permute-start.10 = (f32[64,512]{1,0:T(8,128)S(1)}, f32[64,512]{1,0:T(8,128)S(1)}, u32[]{:S(2)}, u32[]{:S(2)}) collective-permute-start(f32[64,512]{1,0:T(8,128)S(1)} %get-tuple-element.119), channel_id=1, source_target_pairs={{0,252},{4,8},{8,4},{12,16},{16,12},{20,24},{24,20},{28,32},{32,28... | collective-permute-start | bytes 393224 | tf_op jit(solution)/shard_map/ppermute | solution.py:478
  48.4 1.4 %collective-permute-start.7 = (f32[16,384]{1,0:T(8,128)S(1)}, f32[16,384]{1,0:T(8,128)S(1)}, u32[]{:S(2)}, u32[]{:S(2)}) collective-permute-start(f32[16,384]{1,0:T(8,128)S(1)} %get-tuple-element.117), channel_id=1, source_target_pairs={{0,4},{4,0},{8,12},{12,8},{16,20},{20,16},{24,28},{28,24},{32,36},... | collective-permute-start | bytes 73736 | tf_op jit(solution)/shard_map/ppermute | solution.py:478
  49.8 2.7 %collective-permute-start.8 = (f32[16,384]{1,0:T(8,128)S(1)}, f32[16,384]{1,0:T(8,128)S(1)}, u32[]{:S(2)}, u32[]{:S(2)}) collective-permute-start(f32[16,384]{1,0:T(8,128)S(1)} %shard_map.76.left), channel_id=1, source_target_pairs={{0,8},{4,12},{8,0},{12,4},{16,24},{20,28},{24,16},{28,20},{32,40},... | collective-permute-start | bytes 73736 | tf_op jit(solution)/shard_map/ppermute | solution.py:478
  52.5 3.4 %collective-permute-start.11 = (f32[16,384]{1,0:T(8,128)S(1)}, f32[16,384]{1,0:T(8,128)S(1)}, u32[]{:S(2)}, u32[]{:S(2)}) collective-permute-start(f32[16,384]{1,0:T(8,128)S(1)} %shard_map.77.left), channel_id=1, source_target_pairs={{0,64},{4,68},{8,72},{12,76},{16,80},{20,84},{24,88},{28,92},{32,9... | collective-permute-start | bytes 73736 | tf_op jit(solution)/shard_map/ppermute | solution.py:478
  55.9 4.1 %collective-permute-start.12 = (f32[16,384]{1,0:T(8,128)S(1)}, f32[16,384]{1,0:T(8,128)S(1)}, u32[]{:S(2)}, u32[]{:S(2)}) collective-permute-start(f32[16,384]{1,0:T(8,128)S(1)} %shard_map.79.early), channel_id=1, source_target_pairs={{0,16},{4,20},{8,24},{12,28},{16,0},{20,4},{24,8},{28,12},{32,48},... | collective-permute-start | bytes 73736 | tf_op jit(solution)/shard_map/ppermute | solution.py:478
  56.0 4.0 %collective-permute-start.13 = (f32[16,128]{1,0:T(8,128)S(1)}, f32[16,128]{1,0:T(8,128)S(1)}, u32[]{:S(2)}, u32[]{:S(2)}) collective-permute-start(f32[16,128]{1,0:T(8,128)S(1)} %get-tuple-element.131), channel_id=1, source_target_pairs={{0,4},{4,0},{8,12},{12,8},{16,20},{20,16},{24,28},{28,24},{32,36},... | collective-permute-start | bytes 24584 | tf_op jit(solution)/shard_map/ppermute | solution.py:478
  60.0 5.0 %collective-permute-start.14 = (f32[16,512]{1,0:T(8,128)S(1)}, f32[16,512]{1,0:T(8,128)S(1)}, u32[]{:S(2)}, u32[]{:S(2)}) collective-permute-start(f32[16,512]{1,0:T(8,128)S(1)} %shard_map.80.left), channel_id=1, source_target_pairs={{0,48},{4,52},{8,56},{12,60},{16,32},{20,36},{24,40},{28,44},{32,1... | collective-permute-start | bytes 98312 | tf_op jit(solution)/shard_map/ppermute | solution.py:478
  65.1 4.3 %collective-permute-start.15 = (f32[16,512]{1,0:T(8,128)S(1)}, f32[16,512]{1,0:T(8,128)S(1)}, u32[]{:S(2)}, u32[]{:S(2)}) collective-permute-start(f32[16,512]{1,0:T(8,128)S(1)} %shard_map.81.left), channel_id=1, source_target_pairs={{0,192},{4,196},{8,200},{12,204},{16,208},{20,212},{24,216},{28,22... | collective-permute-start | bytes 98312 | tf_op jit(solution)/shard_map/ppermute | solution.py:478
  69.3 6.8 %collective-permute-start.16 = (f32[16,384]{1,0:T(8,128)S(1)}, f32[16,384]{1,0:T(8,128)S(1)}, u32[]{:S(2)}, u32[]{:S(2)}) collective-permute-start(f32[16,384]{1,0:T(8,128)S(1)} %slice.8.mine), channel_id=1, source_target_pairs={{0,4},{4,0},{8,12},{12,8},{16,20},{20,16},{24,28},{28,24},{32,36},... | collective-permute-start | bytes 73736 | tf_op jit(solution)/shard_map/ppermute | solution.py:478
  75.3 4.5 %collective-permute-start.17 = (f32[16,128]{1,0:T(8,128)S(1)}, f32[16,128]{1,0:T(8,128)S(1)}, u32[]{:S(2)}, u32[]{:S(2)}) collective-permute-start(f32[16,128]{1,0:T(8,128)S(1)} %slice.9.left), channel_id=1, source_target_pairs={{0,64},{4,68},{8,72},{12,76},{16,80},{20,84},{24,88},{28,92},{32,9... | collective-permute-start | bytes 24584 | tf_op jit(solution)/shard_map/ppermute | solution.py:478
  79.8 4.5 %collective-permute-start.18 = (f32[16,128]{1,0:T(8,128)S(1)}, f32[16,128]{1,0:T(8,128)S(1)}, u32[]{:S(2)}, u32[]{:S(2)}) collective-permute-start(f32[16,128]{1,0:T(8,128)S(1)} %shard_map.84.left), channel_id=1, source_target_pairs={{0,8},{4,12},{8,0},{12,4},{16,24},{20,28},{24,16},{28,20},{32,40},... | collective-permute-start | bytes 24584 | tf_op jit(solution)/shard_map/ppermute | solution.py:478
  84.3 6.1 %copy-start.2 = (f32[2,16,8]{2,1,0:T(8,128)S(1)}, f32[2,16,8]{2,1,0:T(8,128)}, u32[]{:S(2)}) copy-start(f32[2,16,8]{2,1,0:T(8,128)} %constant.11.clone.weights) | copy-start | bytes 3076
  84.3 3.5 %collective-permute-start.19 = (f32[16,128]{1,0:T(8,128)S(1)}, f32[16,128]{1,0:T(8,128)S(1)}, u32[]{:S(2)}, u32[]{:S(2)}) collective-permute-start(f32[16,128]{1,0:T(8,128)S(1)} %shard_map.86.left), channel_id=1, source_target_pairs={{0,16},{4,20},{8,24},{12,28},{16,0},{20,4},{24,8},{28,12},{32,48},... | collective-permute-start | bytes 24584 | tf_op jit(solution)/shard_map/ppermute | solution.py:478
  87.8 2.6 %collective-permute-start.20 = (f32[16,128]{1,0:T(8,128)S(1)}, f32[16,128]{1,0:T(8,128)S(1)}, u32[]{:S(2)}, u32[]{:S(2)}) collective-permute-start(f32[16,128]{1,0:T(8,128)S(1)} %shard_map.88.mine_late), channel_id=1, source_target_pairs={{0,4},{4,0},{8,12},{12,8},{16,20},{20,16},{24,28},{28,24},{32,36},... | collective-permute-start | bytes 24584 | tf_op jit(solution)/shard_map/ppermute | solution.py:478

commit v4 on v3

--- a/solution.py
+++ b/solution.py
@@ -230,7 +230,8 @@
     if len(sent) > 2:
         send_two(position, after, thi, tlo, uhi, ulo, *sent)
     else:
-        sums = jnp.concatenate([gram_of(value, before[...]), gram_of(after, value)], axis=1)
+        both = gram_of(jnp.concatenate([value, after], axis=0), before[...])
+        sums = jnp.concatenate([both[:PROBES, :2 * PROBES], both[PROBES:, PROBES:]], axis=1)
         store_halves(position, sums, *sent)
     for keep in keeps:
         keep.wait()
@@ -352,8 +353,8 @@
             curvature, now = image_against[:size], res_against[:size]
         else:
             turned = direction.T
-            curvature = self.blocks(dot_f32(turned, image_against[:size]))
-            now = self.blocks(dot_f32(turned, res_against[:size]))
+            both = dot_f32(turned, jnp.concatenate([image_against[:size], res_against[:size]], axis=1))
+            curvature, now = self.blocks(both[:, :WIDTH]), self.blocks(both[:, WIDTH:])
         inverse = invert(curvature)
         alpha = self.spread(dot_f32(inverse, self.spread(now)))
         if residual is None:

time: 101 us -> 101 us (level)
  no operation moved by 1% of the time
where the time goes in v4:
time: 101 us; the launch traced here: 100 us
  Pallas kernels  41.4 us (41%)
  starting transfers between devices  35.4 us (35%)
  waiting for transfers between devices  21.3 us (21%)
  local copies, waits for them, and re-layouts  1.06 us (1%)
  between operations  1.06 us (1%)
    ppermute x21, starting transfers between devices, exchange(): lax.ppermute(value, 'row', [(source, partner(source) % count) for source...  35.4 us
    ppermute x21, waiting for transfers between devices, exchange(): lax.ppermute(value, 'row', [(source, partner(source) % count) for source...  21.3 us
    pallas_call x3, Pallas kernels, shards(): call(functools.partial(double_body, degree=degree), outs, [HBM, SMEM] + [...  10.7 us
    pallas_call x3, Pallas kernels, beside(): made = call(body, tuple(map(coeffs, blocks)), specs, **work)(*args)  10.5 us
    pallas_call x1, Pallas kernels, shards(): call(moments_body, (array(moment_share, PROBES, ROWS), array(moment_share...  9.73 us
    pallas_call x1, Pallas kernels, shards(): call(cross_body, (message, message), [SMEM, SMEM, HBM, HBM], vmem=56, scr...  3.01 us
    pallas_call x3, Pallas kernels, shards(): call(functools.partial(shadow_body, count=len(fresh), first=first, last=n...  2.73 us
    pallas_call x1, Pallas kernels, shards(): call(first_body, band + cross + (array(len(EDGE), BLOCK, BLOCK), vector,...  2.57 us
  transfers between devices with their start and end apart: 21, of which 12 were waited for; matrix products, arithmetic and copies ran while one was open for 0% of the time, Pallas kernels for 21%

profile of v4, /device:TPU:1, one launch (start us, length us, event | category | flops | bytes accessed | tf_op | source)
XLA Modules:
  0.0 100.4 jit_solution(12046891933741297254)
XLA Ops:
  0.7 3.0 %shard_map.68 = (f32[32,512]{1,0:T(8,128)}, f32[32,512]{1,0:T(8,128)}) custom-call(s32[3,8]{1,0:T(4,128)} %bitcast.3, s32[1]{0:T(128)} %bitcast.1.position, f32[8,3,128,128]{3,2,1,0:T(8,128)} %coup.1, f32[32,1024]{1,0:T(8,128)} %k0.1), custom_call_target="tpu_custom_call" | custom-call | tf_op jit(solution)/shard_map/pallas_call | solution.py:532
  3.7 3.3 %collective-permute-start = (f32[32,512]{1,0:T(8,128)}, f32[32,512]{1,0:T(8,128)S(1)}, u32[]{:S(2)}, u32[]{:S(2)}) collective-permute-start(f32[32,512]{1,0:T(8,128)} %get-tuple-element.84), channel_id=1, source_target_pairs={{0,4},{4,0},{8,12},{12,8},{16,20},{20,16},{24,28},{28,24},{32,36},... | collective-permute-start | bytes 196616 | tf_op jit(solution)/shard_map/ppermute | solution.py:479
  7.0 1.1 %collective-permute-done.after.got_core = f32[32,512]{1,0:T(8,128)S(1)} collective-permute-done((f32[32,512]{1,0:T(8,128)}, f32[32,512]{1,0:T(8,128)S(1)}, u32[]{:S(2)}, u32[]{:S(2)}) %collective-permute-start) | collective-permute-done | bytes 65568 | tf_op jit(solution)/shard_map/ppermute | solution.py:479
  8.1 1.0 %copy-done.4 = f32[8,128,128]{2,1,0:T(8,128)S(1)} copy-done((f32[8,128,128]{2,1,0:T(8,128)S(1)}, f32[8,128,128]{2,1,0:T(8,128)}, u32[]{:S(2)}) %copy-start.4) | copy-done | bytes 524312
  9.2 2.6 %shard_map.69 = (bf16[9,256,256]{2,1,0:T(8,128)(2,1)S(1)}, bf16[9,256,256]{2,1,0:T(8,128)(2,1)S(1)}, bf16[3,256,256]{2,1,0:T(8,128)(2,1)S(1)}, bf16[3,256,256]{2...) custom-call(s32[3,8]{1,0:T(4,128)S(1)} %bitcast.4, ...), custom_call_target="tpu_custom_call" | custom-call | flops 1000000000 | bytes 4194304 | tf_op jit(solution)/shard_map/pallas_call | solution.py:547
  12.5 2.1 %shard_map.70 = (f32[8,32,1024]{2,1,0:T(8,128)S(1)}, f32[32,1024]{1,0:T(8,128)S(1)}, f32[32,1024]{1,0:T(8,128)S(1)}, f32[32,512]{1,0:T(8,128)S(1)}, f32[64,512]{1,0:T(8,128)S(1)}, /*index=5*/f32[64,512]{1,0:T(8,128)S(1)}) custom-call(s32[1]{0:T(128)} %bitcast.1.position, f32[32,1024]{1,0:T(8,128)S(1)} %get-tuple-element.85.local, ...), custom_call_target="tpu_custom_call" | custom-call | flops 1000000000 | bytes 4194304 | tf_op jit(solution)/shard_map/pallas_call | solution.py:559
  14.6 5.0 %collective-permute-start.3 = (f32[64,512]{1,0:T(8,128)S(1)}, f32[64,512]{1,0:T(8,128)S(1)}, u32[]{:S(2)}, u32[]{:S(2)}) collective-permute-start(f32[64,512]{1,0:T(8,128)S(1)} %get-tuple-element.100), channel_id=1, source_target_pairs={{0,4},{4,0},{8,12},{12,8},{16,20},{20,16},{24,28},{28,24},{32,36},... | collective-permute-start | bytes 393224 | tf_op jit(solution)/shard_map/ppermute | solution.py:479
  20.0 0.7 shard_map.71
  20.8 3.5 %collective-permute-done.4.got_chip = f32[64,512]{1,0:T(8,128)S(1)} collective-permute-done((f32[64,512]{1,0:T(8,128)S(1)}, f32[64,512]{1,0:T(8,128)S(1)}, u32[]{:S(2)}, u32[]{:S(2)}) %collective-permute-start.4) | collective-permute-done | bytes 131104 | tf_op jit(solution)/shard_map/ppermute | solution.py:479
  24.3 3.5 %shard_map.72 = (f32[8,32,1024]{2,1,0:T(8,128)S(1)}, f32[32,1024]{1,0:T(8,128)S(1)}, f32[32,1024]{1,0:T(8,128)S(1)}, f32[32,1024]{1,0:T(8,128)S(1)}, f32[32,512]...) custom-call(f32[8,32,1024]{2,1,0:T(8,128)S(1)} %get-tuple-element.93.kept_in, ...), custom_call_target="tpu_custom_call", output_to_operand_aliasing={{0}: (0, {})} | custom-call | flops 1000000000 | bytes 4194304 | tf_op jit(solution)/shard_map/pallas_call | solution.py:593
  27.9 7.9 %collective-permute-start.5 = (f32[64,512]{1,0:T(8,128)S(1)}, f32[64,512]{1,0:T(8,128)S(1)}, u32[]{:S(2)}, u32[]{:S(2)}) collective-permute-start(f32[64,512]{1,0:T(8,128)S(1)} %get-tuple-element.111), channel_id=1, source_target_pairs={{0,4},{4,0},{8,12},{12,8},{16,20},{20,16},{24,28},{28,24},{32,36},... | collective-permute-start | bytes 393224 | tf_op jit(solution)/shard_map/ppermute | solution.py:479
  35.8 1.0 shard_map.73
  36.8 3.3 %collective-permute-done.6.got_chip = f32[64,512]{1,0:T(8,128)S(1)} collective-permute-done((f32[64,512]{1,0:T(8,128)S(1)}, f32[64,512]{1,0:T(8,128)S(1)}, u32[]{:S(2)}, u32[]{:S(2)}) %collective-permute-start.6) | collective-permute-done | bytes 131104 | tf_op jit(solution)/shard_map/ppermute | solution.py:479
  40.2 3.5 %shard_map.74 = (f32[8,32,1024]{2,1,0:T(8,128)S(1)}, f32[32,1024]{1,0:T(8,128)S(1)}, f32[32,1024]{1,0:T(8,128)S(1)}, f32[32,1024]{1,0:T(8,128)S(1)}, f32[32,512]...) custom-call(f32[8,32,1024]{2,1,0:T(8,128)S(1)} %get-tuple-element.103.kept_in, ...), custom_call_target="tpu_custom_call", output_to_operand_aliasing={{0}: (0, {})} | custom-call | flops 1000000000 | bytes 4194304 | tf_op jit(solution)/shard_map/pallas_call | solution.py:593
  43.7 3.7 %collective-permute-start.9 = (f32[64,512]{1,0:T(8,128)S(1)}, f32[64,512]{1,0:T(8,128)S(1)}, u32[]{:S(2)}, u32[]{:S(2)}) collective-permute-start(f32[64,512]{1,0:T(8,128)S(1)} %get-tuple-element.118), channel_id=1, source_target_pairs={{0,4},{4,0},{8,12},{12,8},{16,20},{20,16},{24,28},{28,24},{32,36},... | collective-permute-start | bytes 393224 | tf_op jit(solution)/shard_map/ppermute | solution.py:479
  47.4 1.0 shard_map.75
  48.9 0.8 collective-permute-done.7.right
  49.8 1.4 %collective-permute-start.8 = (f32[16,384]{1,0:T(8,128)S(1)}, f32[16,384]{1,0:T(8,128)S(1)}, u32[]{:S(2)}, u32[]{:S(2)}) collective-permute-start(f32[16,384]{1,0:T(8,128)S(1)} %shard_map.76.left), channel_id=1, source_target_pairs={{0,8},{4,12},{8,0},{12,4},{16,24},{20,28},{24,16},{28,20},{32,40},... | collective-permute-start | bytes 73736 | tf_op jit(solution)/shard_map/ppermute | solution.py:479
  51.2 1.2 %collective-permute-done.8.right = f32[16,384]{1,0:T(8,128)S(1)} collective-permute-done((f32[16,384]{1,0:T(8,128)S(1)}, f32[16,384]{1,0:T(8,128)S(1)}, u32[]{:S(2)}, u32[]{:S(2)}) %collective-permute-start.8) | collective-permute-done | bytes 24608 | tf_op jit(solution)/shard_map/ppermute | solution.py:479
  52.6 3.7 %shard_map.78 = (f32[8,32,1024]{2,1,0:T(8,128)S(1)}, f32[32,1024]{1,0:T(8,128)}, f32[32,1024]{1,0:T(8,128)}, f32[16,128]{1,0:T(8,128)S(1)}, f32[16,128]{1,0:T(8,128)S(1)}) custom-call(f32[8,32,1024]{2,1,0:T(8,128)S(1)} %get-tuple-element.121.kept_in, s32[1]{0:T(128)} %bitcast.1.position, ...), custom_call_target="tpu_custom_call", output_to_operand_aliasing={{0}: (0, {})} | custom-call | flops 1000000000 | bytes 4194304 | tf_op jit(solution)/shard_map/pallas_call | solution.py:593
  56.4 2.8 %collective-permute-start.13 = (f32[16,128]{1,0:T(8,128)S(1)}, f32[16,128]{1,0:T(8,128)S(1)}, u32[]{:S(2)}, u32[]{:S(2)}) collective-permute-start(f32[16,128]{1,0:T(8,128)S(1)} %get-tuple-element.131), channel_id=1, source_target_pairs={{0,4},{4,0},{8,12},{12,8},{16,20},{20,16},{24,28},{28,24},{32,36},... | collective-permute-start | bytes 24584 | tf_op jit(solution)/shard_map/ppermute | solution.py:479
  59.2 0.8 collective-permute-done.13.late_got
  60.1 4.9 %collective-permute-done.14.right = f32[16,512]{1,0:T(8,128)S(1)} collective-permute-done((f32[16,512]{1,0:T(8,128)S(1)}, f32[16,512]{1,0:T(8,128)S(1)}, u32[]{:S(2)}, u32[]{:S(2)}) %collective-permute-start.14) | collective-permute-done | bytes 32800 | tf_op jit(solution)/shard_map/ppermute | solution.py:479
  65.0 1.0 collective-permute-start.15
  66.0 3.3 %collective-permute-done.15.right = f32[16,512]{1,0:T(8,128)S(1)} collective-permute-done((f32[16,512]{1,0:T(8,128)S(1)}, f32[16,512]{1,0:T(8,128)S(1)}, u32[]{:S(2)}, u32[]{:S(2)}) %collective-permute-start.15) | collective-permute-done | bytes 32800 | tf_op jit(solution)/shard_map/ppermute | solution.py:479
  69.3 6.0 %collective-permute-start.16 = (f32[16,384]{1,0:T(8,128)S(1)}, f32[16,384]{1,0:T(8,128)S(1)}, u32[]{:S(2)}, u32[]{:S(2)}) collective-permute-start(f32[16,384]{1,0:T(8,128)S(1)} %slice.8.mine), channel_id=1, source_target_pairs={{0,4},{4,0},{8,12},{12,8},{16,20},{20,16},{24,28},{28,24},{32,36},... | collective-permute-start | bytes 73736 | tf_op jit(solution)/shard_map/ppermute | solution.py:479
  76.2 3.6 %shard_map.83 = (f32[96,256]{1,0:T(8,128)S(1)}, f32[96,256]{1,0:T(8,128)S(1)}, f32[288,256]{1,0:T(8,128)S(1)}, f32[288,256]{1,0:T(8,128)S(1)}, f32[32,256]{1,0:T(8,128)S(1)}) custom-call(s32[1]{0:T(128)} %bitcast.1.position, f32[16,384]{1,0:T(8,128)S(1)} %slice.8.mine, f32[16,384]{1,0:T(8,128)S(1)} %collective-permute-done.16.other), custom_call_target="tpu_custom_call" | custom-call | flops 3000000000 | bytes 4194304 | tf_op jit(solution)/shard_map/pallas_call | solution.py:622
  80.2 4.1 %shard_map.85 = (f32[160,256]{1,0:T(8,128)S(1)}, f32[160,256]{1,0:T(8,128)S(1)}, f32[224,256]{1,0:T(8,128)S(1)}, f32[224,256]{1,0:T(8,128)S(1)}, f32[96,256]{1,0:T(8,128)S(1)}) custom-call(f32[96,256]{1,0:T(8,128)S(1)} %get-tuple-element.138.refs_0_, f32[96,256]{1,0:T(8,128)S(1)} %get-tuple-element.139.refs_1_, f32[288,256]{1,0:T(8,128)S(1)} %get-tuple-element.140.refs_2_, ...), custom_call_target="tpu_custom_call" | custom-call | flops 3000000000 | bytes 4194304 | tf_op jit(solution)/shard_map/pallas_call | solution.py:622
  84.4 2.8 %shard_map.87 = (f32[224,256]{1,0:T(8,128)S(1)}, f32[32,256]{1,0:T(8,128)S(1)}, f32[224,256]{1,0:T(8,128)S(1)}, f32[160,256]{1,0:T(8,128)S(1)}, f32[160,256]{1,0:T(8,128)S(1)}) custom-call(f32[160,256]{1,0:T(8,128)S(1)} %get-tuple-element.149.refs_0_.direction, f32[160,256]{1,0:T(8,128)S(1)} %get-tuple-element.150.refs_1_, ...), custom_call_target="tpu_custom_call" | custom-call | flops 3000000000 | bytes 4194304 | tf_op jit(solution)/shard_map/pallas_call | solution.py:622
  87.8 1.8 %collective-permute-start.20 = (f32[16,128]{1,0:T(8,128)S(1)}, f32[16,128]{1,0:T(8,128)S(1)}, u32[]{:S(2)}, u32[]{:S(2)}) collective-permute-start(f32[16,128]{1,0:T(8,128)S(1)} %shard_map.88.mine_late), channel_id=1, source_target_pairs={{0,4},{4,0},{8,12},{12,8},{16,20},{20,16},{24,28},{28,24},{32,36},... | collective-permute-start | bytes 24584 | tf_op jit(solution)/shard_map/ppermute | solution.py:479
  89.6 0.8 collective-permute-done.20.other_late
  90.4 9.7 %shard_map.89 = (f32[4,32,1024]{2,1,0:T(8,128)}, f32[4,32,32]{2,1,0:T(8,128)}) custom-call(s32[1]{0:T(128)} %bitcast.node, s32[1]{0:T(128)} %bitcast.1.position, f32[2,16,8]{2,1,0:T(8,128)S(1)} %copy-done.2, f32[16,384]{1,0:T(8,128)S(1)} %slice.8.mine, f32[16,384]{1,0:T(8,128)S(1)} %collective-permute-done.16.other, f32[16,128]{1,0:T(8,128)S(1)} %shard_map.88.mine_late, ...), custom_call_target="tpu_custom_call" | custom-call | tf_op jit(solution)/shard_map/pallas_call | solution.py:632
  (44 shorter events, 4.0 us)
Async XLA Ops:
  0.6 7.5 %copy-start.1 = (f32[32,1024]{1,0:T(8,128)S(1)}, f32[32,1024]{1,0:T(8,128)}, u32[]{:S(2)}) copy-start(f32[32,1024]{1,0:T(8,128)} %k0.1) | copy-start | bytes 393220
  0.6 7.5 %copy-start = (f32[8,3,128,128]{3,2,1,0:T(8,128)S(1)}, f32[8,3,128,128]{3,2,1,0:T(8,128)}, u32[]{:S(2)}) copy-start(f32[8,3,128,128]{3,2,1,0:T(8,128)} %coup.1) | copy-start | bytes 4718596
  0.6 7.5 %copy-start.3 = (s32[8,3]{0,1:T(4,128)S(1)}, s32[8,3]{0,1:T(4,128)}, u32[]{:S(2)}) copy-start(s32[8,3]{0,1:T(4,128)} %param.8) | copy-start | bytes 292
  3.7 4.4 %collective-permute-start = (f32[32,512]{1,0:T(8,128)}, f32[32,512]{1,0:T(8,128)S(1)}, u32[]{:S(2)}, u32[]{:S(2)}) collective-permute-start(f32[32,512]{1,0:T(8,128)} %get-tuple-element.84), channel_id=1, source_target_pairs={{0,4},{4,0},{8,12},{12,8},{16,20},{20,16},{24,28},{28,24},{32,36},... | collective-permute-start | bytes 196616 | tf_op jit(solution)/shard_map/ppermute | solution.py:479
  7.0 4.7 %collective-permute-start.1 = (f32[32,512]{1,0:T(8,128)}, f32[32,512]{1,0:T(8,128)S(1)}, u32[]{:S(2)}, u32[]{:S(2)}) collective-permute-start(f32[32,512]{1,0:T(8,128)} %get-tuple-element.87), channel_id=1, source_target_pairs={{0,252},{4,8},{8,4},{12,16},{16,12},{20,24},{24,20},{28,32},{32,28... | collective-permute-start | bytes 196616 | tf_op jit(solution)/shard_map/ppermute | solution.py:479
  8.1 1.0 %copy-start.4 = (f32[8,128,128]{2,1,0:T(8,128)S(1)}, f32[8,128,128]{2,1,0:T(8,128)}, u32[]{:S(2)}) copy-start(f32[8,128,128]{2,1,0:T(8,128)} %diag.1) | copy-start | bytes 1572868
  11.8 8.3 %collective-permute-start.2 = (f32[10,128,128]{2,1,0:T(8,128)S(1)}, f32[10,128,128]{2,1,0:T(8,128)S(1)}, u32[]{:S(2)}, u32[]{:S(2)}) collective-permute-start(f32[10,128,128]{2,1,0:T(8,128)S(1)} %get-tuple-element.98), channel_id=1, source_target_pairs={{0,4},{4,8},{8,12},{12,16},{16,20},{20,24},{24,28},{28,32},{32,36}... | collective-permute-start | bytes 1966088 | tf_op jit(solution)/shard_map/ppermute | solution.py:479
  14.6 6.2 %collective-permute-start.3 = (f32[64,512]{1,0:T(8,128)S(1)}, f32[64,512]{1,0:T(8,128)S(1)}, u32[]{:S(2)}, u32[]{:S(2)}) collective-permute-start(f32[64,512]{1,0:T(8,128)S(1)} %get-tuple-element.100), channel_id=1, source_target_pairs={{0,4},{4,0},{8,12},{12,8},{16,20},{20,16},{24,28},{28,24},{32,36},... | collective-permute-start | bytes 393224 | tf_op jit(solution)/shard_map/ppermute | solution.py:479
  19.6 4.7 %collective-permute-start.4 = (f32[64,512]{1,0:T(8,128)S(1)}, f32[64,512]{1,0:T(8,128)S(1)}, u32[]{:S(2)}, u32[]{:S(2)}) collective-permute-start(f32[64,512]{1,0:T(8,128)S(1)} %get-tuple-element.101), channel_id=1, source_target_pairs={{0,252},{4,8},{8,4},{12,16},{16,12},{20,24},{24,20},{28,32},{32,28... | collective-permute-start | bytes 393224 | tf_op jit(solution)/shard_map/ppermute | solution.py:479
  27.9 9.0 %collective-permute-start.5 = (f32[64,512]{1,0:T(8,128)S(1)}, f32[64,512]{1,0:T(8,128)S(1)}, u32[]{:S(2)}, u32[]{:S(2)}) collective-permute-start(f32[64,512]{1,0:T(8,128)S(1)} %get-tuple-element.111), channel_id=1, source_target_pairs={{0,4},{4,0},{8,12},{12,8},{16,20},{20,16},{24,28},{28,24},{32,36},... | collective-permute-start | bytes 393224 | tf_op jit(solution)/shard_map/ppermute | solution.py:479
  35.8 4.4 %collective-permute-start.6 = (f32[64,512]{1,0:T(8,128)S(1)}, f32[64,512]{1,0:T(8,128)S(1)}, u32[]{:S(2)}, u32[]{:S(2)}) collective-permute-start(f32[64,512]{1,0:T(8,128)S(1)} %get-tuple-element.112), channel_id=1, source_target_pairs={{0,252},{4,8},{8,4},{12,16},{16,12},{20,24},{24,20},{28,32},{32,28... | collective-permute-start | bytes 393224 | tf_op jit(solution)/shard_map/ppermute | solution.py:479
  43.7 8.7 %collective-permute-start.9 = (f32[64,512]{1,0:T(8,128)S(1)}, f32[64,512]{1,0:T(8,128)S(1)}, u32[]{:S(2)}, u32[]{:S(2)}) collective-permute-start(f32[64,512]{1,0:T(8,128)S(1)} %get-tuple-element.118), channel_id=1, source_target_pairs={{0,4},{4,0},{8,12},{12,8},{16,20},{20,16},{24,28},{28,24},{32,36},... | collective-permute-start | bytes 393224 | tf_op jit(solution)/shard_map/ppermute | solution.py:479
  47.4 5.1 %collective-permute-start.10 = (f32[64,512]{1,0:T(8,128)S(1)}, f32[64,512]{1,0:T(8,128)S(1)}, u32[]{:S(2)}, u32[]{:S(2)}) collective-permute-start(f32[64,512]{1,0:T(8,128)S(1)} %get-tuple-element.119), channel_id=1, source_target_pairs={{0,252},{4,8},{8,4},{12,16},{16,12},{20,24},{24,20},{28,32},{32,28... | collective-permute-start | bytes 393224 | tf_op jit(solution)/shard_map/ppermute | solution.py:479
  48.4 1.4 %collective-permute-start.7 = (f32[16,384]{1,0:T(8,128)S(1)}, f32[16,384]{1,0:T(8,128)S(1)}, u32[]{:S(2)}, u32[]{:S(2)}) collective-permute-start(f32[16,384]{1,0:T(8,128)S(1)} %get-tuple-element.117), channel_id=1, source_target_pairs={{0,4},{4,0},{8,12},{12,8},{16,20},{20,16},{24,28},{28,24},{32,36},... | collective-permute-start | bytes 73736 | tf_op jit(solution)/shard_map/ppermute | solution.py:479
  49.8 2.7 %collective-permute-start.8 = (f32[16,384]{1,0:T(8,128)S(1)}, f32[16,384]{1,0:T(8,128)S(1)}, u32[]{:S(2)}, u32[]{:S(2)}) collective-permute-start(f32[16,384]{1,0:T(8,128)S(1)} %shard_map.76.left), channel_id=1, source_target_pairs={{0,8},{4,12},{8,0},{12,4},{16,24},{20,28},{24,16},{28,20},{32,40},... | collective-permute-start | bytes 73736 | tf_op jit(solution)/shard_map/ppermute | solution.py:479
  52.5 3.8 %collective-permute-start.11 = (f32[16,384]{1,0:T(8,128)S(1)}, f32[16,384]{1,0:T(8,128)S(1)}, u32[]{:S(2)}, u32[]{:S(2)}) collective-permute-start(f32[16,384]{1,0:T(8,128)S(1)} %shard_map.77.left), channel_id=1, source_target_pairs={{0,64},{4,68},{8,72},{12,76},{16,80},{20,84},{24,88},{28,92},{32,9... | collective-permute-start | bytes 73736 | tf_op jit(solution)/shard_map/ppermute | solution.py:479
  56.3 3.7 %collective-permute-start.12 = (f32[16,384]{1,0:T(8,128)S(1)}, f32[16,384]{1,0:T(8,128)S(1)}, u32[]{:S(2)}, u32[]{:S(2)}) collective-permute-start(f32[16,384]{1,0:T(8,128)S(1)} %shard_map.79.early), channel_id=1, source_target_pairs={{0,16},{4,20},{8,24},{12,28},{16,0},{20,4},{24,8},{28,12},{32,48},... | collective-permute-start | bytes 73736 | tf_op jit(solution)/shard_map/ppermute | solution.py:479
  56.4 3.6 %collective-permute-start.13 = (f32[16,128]{1,0:T(8,128)S(1)}, f32[16,128]{1,0:T(8,128)S(1)}, u32[]{:S(2)}, u32[]{:S(2)}) collective-permute-start(f32[16,128]{1,0:T(8,128)S(1)} %get-tuple-element.131), channel_id=1, source_target_pairs={{0,4},{4,0},{8,12},{12,8},{16,20},{20,16},{24,28},{28,24},{32,36},... | collective-permute-start | bytes 24584 | tf_op jit(solution)/shard_map/ppermute | solution.py:479
  60.0 5.0 %collective-permute-start.14 = (f32[16,512]{1,0:T(8,128)S(1)}, f32[16,512]{1,0:T(8,128)S(1)}, u32[]{:S(2)}, u32[]{:S(2)}) collective-permute-start(f32[16,512]{1,0:T(8,128)S(1)} %shard_map.80.left), channel_id=1, source_target_pairs={{0,48},{4,52},{8,56},{12,60},{16,32},{20,36},{24,40},{28,44},{32,1... | collective-permute-start | bytes 98312 | tf_op jit(solution)/shard_map/ppermute | solution.py:479
  65.0 4.3 %collective-permute-start.15 = (f32[16,512]{1,0:T(8,128)S(1)}, f32[16,512]{1,0:T(8,128)S(1)}, u32[]{:S(2)}, u32[]{:S(2)}) collective-permute-start(f32[16,512]{1,0:T(8,128)S(1)} %shard_map.81.left), channel_id=1, source_target_pairs={{0,192},{4,196},{8,200},{12,204},{16,208},{20,212},{24,216},{28,22... | collective-permute-start | bytes 98312 | tf_op jit(solution)/shard_map/ppermute | solution.py:479
  69.3 6.9 %collective-permute-start.16 = (f32[16,384]{1,0:T(8,128)S(1)}, f32[16,384]{1,0:T(8,128)S(1)}, u32[]{:S(2)}, u32[]{:S(2)}) collective-permute-start(f32[16,384]{1,0:T(8,128)S(1)} %slice.8.mine), channel_id=1, source_target_pairs={{0,4},{4,0},{8,12},{12,8},{16,20},{20,16},{24,28},{28,24},{32,36},... | collective-permute-start | bytes 73736 | tf_op jit(solution)/shard_map/ppermute | solution.py:479
  75.3 4.5 %collective-permute-start.17 = (f32[16,128]{1,0:T(8,128)S(1)}, f32[16,128]{1,0:T(8,128)S(1)}, u32[]{:S(2)}, u32[]{:S(2)}) collective-permute-start(f32[16,128]{1,0:T(8,128)S(1)} %slice.9.left), channel_id=1, source_target_pairs={{0,64},{4,68},{8,72},{12,76},{16,80},{20,84},{24,88},{28,92},{32,9... | collective-permute-start | bytes 24584 | tf_op jit(solution)/shard_map/ppermute | solution.py:479
  79.8 4.5 %collective-permute-start.18 = (f32[16,128]{1,0:T(8,128)S(1)}, f32[16,128]{1,0:T(8,128)S(1)}, u32[]{:S(2)}, u32[]{:S(2)}) collective-permute-start(f32[16,128]{1,0:T(8,128)S(1)} %shard_map.84.left), channel_id=1, source_target_pairs={{0,8},{4,12},{8,0},{12,4},{16,24},{20,28},{24,16},{28,20},{32,40},... | collective-permute-start | bytes 24584 | tf_op jit(solution)/shard_map/ppermute | solution.py:479
  84.3 6.1 %copy-start.2 = (f32[2,16,8]{2,1,0:T(8,128)S(1)}, f32[2,16,8]{2,1,0:T(8,128)}, u32[]{:S(2)}) copy-start(f32[2,16,8]{2,1,0:T(8,128)} %constant.11.clone.weights) | copy-start | bytes 3076
  84.3 3.5 %collective-permute-start.19 = (f32[16,128]{1,0:T(8,128)S(1)}, f32[16,128]{1,0:T(8,128)S(1)}, u32[]{:S(2)}, u32[]{:S(2)}) collective-permute-start(f32[16,128]{1,0:T(8,128)S(1)} %shard_map.86.left), channel_id=1, source_target_pairs={{0,16},{4,20},{8,24},{12,28},{16,0},{20,4},{24,8},{28,12},{32,48},... | collective-permute-start | bytes 24584 | tf_op jit(solution)/shard_map/ppermute | solution.py:479
  87.8 2.6 %collective-permute-start.20 = (f32[16,128]{1,0:T(8,128)S(1)}, f32[16,128]{1,0:T(8,128)S(1)}, u32[]{:S(2)}, u32[]{:S(2)}) collective-permute-start(f32[16,128]{1,0:T(8,128)S(1)} %shard_map.88.mine_late), channel_id=1, source_target_pairs={{0,4},{4,0},{8,12},{12,8},{16,20},{20,16},{24,28},{28,24},{32,36},... | collective-permute-start | bytes 24584 | tf_op jit(solution)/shard_map/ppermute | solution.py:479

commit v5 on v3

--- a/solution.py
+++ b/solution.py
@@ -624,9 +624,9 @@
 
     early = (early, exchange(early, core_partner))
     late, state = beside(3, zeroth_body, (3, 3, 9, 9, 1), [SMEM, VMEM, VMEM], flag, *early)
-    late, state = beside(0, iterate_body, (5, 5, 7, 7, 3), [VMEM] * 5, *state)
+    late, state = beside(1, iterate_body, (5, 5, 7, 7, 3), [VMEM] * 5, *state)
     direction, _, dir_against, _, _ = state
-    late, state = beside(1, alpha_body, (7, 1, 7, 5, 5), [VMEM] * 5, *state)
+    late, state = beside(0, alpha_body, (7, 1, 7, 5, 5), [VMEM] * 5, *state)
     late = (late, exchange(late, core_partner))
     moments, projected = call(
         moments_body,

time: 101 us -> 99.6 us (0.986)
  transfers between devices with their start and end apart: 21 -> 21, of which waited for: 12 -> 11; matrix products, arithmetic and copies ran while one was open for 0% -> 0% of each run, Pallas kernels for 21% -> 21%
where the time goes in v5:
time: 99.6 us; the launch traced here: 99.4 us
  Pallas kernels  41.1 us (41%)
  starting transfers between devices  34.6 us (35%)
  waiting for transfers between devices  21.6 us (22%)
  between operations  1.07 us (1%)
  local copies, waits for them, and re-layouts  1.06 us (1%)
    ppermute x21, starting transfers between devices, exchange(): lax.ppermute(value, 'row', [(source, partner(source) % count) for source...  34.6 us
    ppermute x21, waiting for transfers between devices, exchange(): lax.ppermute(value, 'row', [(source, partner(source) % count) for source...  21.6 us
    pallas_call x3, Pallas kernels, beside(): made = call(body, tuple(map(coeffs, blocks)), specs, **work)(*args)  10.5 us
    pallas_call x3, Pallas kernels, shards(): call(functools.partial(double_body, degree=degree), outs, [HBM, SMEM] + [...  10.4 us
    pallas_call x1, Pallas kernels, shards(): call(moments_body, (array(moment_share, PROBES, ROWS), array(moment_share...  9.73 us
    pallas_call x1, Pallas kernels, shards(): call(cross_body, (message, message), [SMEM, SMEM, HBM, HBM], vmem=56, scr...  3.01 us
    pallas_call x3, Pallas kernels, shards(): call(functools.partial(shadow_body, count=len(fresh), first=first, last=n...  2.73 us
    pallas_call x1, Pallas kernels, shards(): call(first_body, band + cross + (array(len(EDGE), BLOCK, BLOCK), vector,...  2.57 us
  transfers between devices with their start and end apart: 21, of which 11 were waited for; matrix products, arithmetic and copies ran while one was open for 0% of the time, Pallas kernels for 21%

profile of v5, /device:TPU:1, one launch (start us, length us, event | category | flops | bytes accessed | tf_op | source)
XLA Modules:
  0.0 99.4 jit_solution(15421382514812706383)
XLA Ops:
  0.7 3.0 %shard_map.68 = (f32[32,512]{1,0:T(8,128)}, f32[32,512]{1,0:T(8,128)}) custom-call(s32[3,8]{1,0:T(4,128)} %bitcast.3, s32[1]{0:T(128)} %bitcast.1.position, f32[8,3,128,128]{3,2,1,0:T(8,128)} %coup.1, f32[32,1024]{1,0:T(8,128)} %k0.1), custom_call_target="tpu_custom_call" | custom-call | tf_op jit(solution)/shard_map/pallas_call | solution.py:531
  3.7 3.3 %collective-permute-start = (f32[32,512]{1,0:T(8,128)}, f32[32,512]{1,0:T(8,128)S(1)}, u32[]{:S(2)}, u32[]{:S(2)}) collective-permute-start(f32[32,512]{1,0:T(8,128)} %get-tuple-element.84), channel_id=1, source_target_pairs={{0,4},{4,0},{8,12},{12,8},{16,20},{20,16},{24,28},{28,24},{32,36},... | collective-permute-start | bytes 196616 | tf_op jit(solution)/shard_map/ppermute | solution.py:478
  7.0 1.1 %collective-permute-done.after.got_core = f32[32,512]{1,0:T(8,128)S(1)} collective-permute-done((f32[32,512]{1,0:T(8,128)}, f32[32,512]{1,0:T(8,128)S(1)}, u32[]{:S(2)}, u32[]{:S(2)}) %collective-permute-start) | collective-permute-done | bytes 65568 | tf_op jit(solution)/shard_map/ppermute | solution.py:478
  8.1 1.0 %copy-done.4 = f32[8,128,128]{2,1,0:T(8,128)S(1)} copy-done((f32[8,128,128]{2,1,0:T(8,128)S(1)}, f32[8,128,128]{2,1,0:T(8,128)}, u32[]{:S(2)}) %copy-start.4) | copy-done | bytes 524312
  9.2 2.6 %shard_map.69 = (bf16[9,256,256]{2,1,0:T(8,128)(2,1)S(1)}, bf16[9,256,256]{2,1,0:T(8,128)(2,1)S(1)}, bf16[3,256,256]{2,1,0:T(8,128)(2,1)S(1)}, bf16[3,256,256]{2...) custom-call(s32[3,8]{1,0:T(4,128)S(1)} %bitcast.4, ...), custom_call_target="tpu_custom_call" | custom-call | flops 1000000000 | bytes 4194304 | tf_op jit(solution)/shard_map/pallas_call | solution.py:546
  12.5 2.1 %shard_map.70 = (f32[8,32,1024]{2,1,0:T(8,128)S(1)}, f32[32,1024]{1,0:T(8,128)S(1)}, f32[32,1024]{1,0:T(8,128)S(1)}, f32[32,512]{1,0:T(8,128)S(1)}, f32[64,512]{1,0:T(8,128)S(1)}, /*index=5*/f32[64,512]{1,0:T(8,128)S(1)}) custom-call(s32[1]{0:T(128)} %bitcast.1.position, f32[32,1024]{1,0:T(8,128)S(1)} %get-tuple-element.85.local, ...), custom_call_target="tpu_custom_call" | custom-call | flops 1000000000 | bytes 4194304 | tf_op jit(solution)/shard_map/pallas_call | solution.py:558
  14.6 5.0 %collective-permute-start.3 = (f32[64,512]{1,0:T(8,128)S(1)}, f32[64,512]{1,0:T(8,128)S(1)}, u32[]{:S(2)}, u32[]{:S(2)}) collective-permute-start(f32[64,512]{1,0:T(8,128)S(1)} %get-tuple-element.100), channel_id=1, source_target_pairs={{0,4},{4,0},{8,12},{12,8},{16,20},{20,16},{24,28},{28,24},{32,36},... | collective-permute-start | bytes 393224 | tf_op jit(solution)/shard_map/ppermute | solution.py:478
  20.0 0.7 shard_map.71
  20.8 3.5 %collective-permute-done.4.got_chip = f32[64,512]{1,0:T(8,128)S(1)} collective-permute-done((f32[64,512]{1,0:T(8,128)S(1)}, f32[64,512]{1,0:T(8,128)S(1)}, u32[]{:S(2)}, u32[]{:S(2)}) %collective-permute-start.4) | collective-permute-done | bytes 131104 | tf_op jit(solution)/shard_map/ppermute | solution.py:478
  24.3 3.5 %shard_map.72 = (f32[8,32,1024]{2,1,0:T(8,128)S(1)}, f32[32,1024]{1,0:T(8,128)S(1)}, f32[32,1024]{1,0:T(8,128)S(1)}, f32[32,1024]{1,0:T(8,128)S(1)}, f32[32,512]...) custom-call(f32[8,32,1024]{2,1,0:T(8,128)S(1)} %get-tuple-element.93.kept_in, ...), custom_call_target="tpu_custom_call", output_to_operand_aliasing={{0}: (0, {})} | custom-call | flops 1000000000 | bytes 4194304 | tf_op jit(solution)/shard_map/pallas_call | solution.py:592
  27.9 7.9 %collective-permute-start.5 = (f32[64,512]{1,0:T(8,128)S(1)}, f32[64,512]{1,0:T(8,128)S(1)}, u32[]{:S(2)}, u32[]{:S(2)}) collective-permute-start(f32[64,512]{1,0:T(8,128)S(1)} %get-tuple-element.111), channel_id=1, source_target_pairs={{0,4},{4,0},{8,12},{12,8},{16,20},{20,16},{24,28},{28,24},{32,36},... | collective-permute-start | bytes 393224 | tf_op jit(solution)/shard_map/ppermute | solution.py:478
  35.8 1.0 %shard_map.73 = (f32[32,512]{1,0:T(8,128)S(1)}, f32[32,256]{1,0:T(8,128)S(1)}) custom-call(s32[1]{0:T(128)} %bitcast.1.position, f32[32,1024]{1,0:T(8,128)S(1)} %get-tuple-element.94.refs_1_.before.refs_0_, f32[32,1024]{1,0:T(8,128)S(1)} %get-tuple-element.106.refs_1_, f32[32,1024]{1,0:T(8,128)S(1)} %get-tuple-element.102.refs_2_.before.refs_0_, ...), custom_call_target="tpu_custom_call" | custom-call | flops 1000000000 | bytes 2097152 | tf_op jit(solution)/shard_map/pallas_call | solution.py:576
  36.8 3.3 %collective-permute-done.6.got_chip = f32[64,512]{1,0:T(8,128)S(1)} collective-permute-done((f32[64,512]{1,0:T(8,128)S(1)}, f32[64,512]{1,0:T(8,128)S(1)}, u32[]{:S(2)}, u32[]{:S(2)}) %collective-permute-start.6) | collective-permute-done | bytes 131104 | tf_op jit(solution)/shard_map/ppermute | solution.py:478
  40.2 3.5 %shard_map.74 = (f32[8,32,1024]{2,1,0:T(8,128)S(1)}, f32[32,1024]{1,0:T(8,128)S(1)}, f32[32,1024]{1,0:T(8,128)S(1)}, f32[32,1024]{1,0:T(8,128)S(1)}, f32[32,512]...) custom-call(f32[8,32,1024]{2,1,0:T(8,128)S(1)} %get-tuple-element.103.kept_in, ...), custom_call_target="tpu_custom_call", output_to_operand_aliasing={{0}: (0, {})} | custom-call | flops 1000000000 | bytes 4194304 | tf_op jit(solution)/shard_map/pallas_call | solution.py:592
  43.7 3.7 %collective-permute-start.9 = (f32[64,512]{1,0:T(8,128)S(1)}, f32[64,512]{1,0:T(8,128)S(1)}, u32[]{:S(2)}, u32[]{:S(2)}) collective-permute-start(f32[64,512]{1,0:T(8,128)S(1)} %get-tuple-element.118), channel_id=1, source_target_pairs={{0,4},{4,0},{8,12},{12,8},{16,20},{20,16},{24,28},{28,24},{32,36},... | collective-permute-start | bytes 393224 | tf_op jit(solution)/shard_map/ppermute | solution.py:478
  47.4 1.0 %shard_map.75 = (f32[32,512]{1,0:T(8,128)S(1)}, f32[16,384]{1,0:T(8,128)S(1)}, f32[16,384]{1,0:T(8,128)S(1)}) custom-call(s32[1]{0:T(128)} %bitcast.1.position, f32[32,1024]{1,0:T(8,128)S(1)} %get-tuple-element.102.refs_2_.before.refs_0_, f32[32,1024]{1,0:T(8,128)S(1)} %get-tuple-element.113.refs_1_, f32[32,1024]{1,0:T(8,128)S(1)} %get-tuple-element.114.refs_2_.before, ...), custom_call_target="tpu_custom_call" | custom-call | flops 1000000000 | bytes 2097152 | tf_op jit(solution)/shard_map/pallas_call | solution.py:576
  48.9 0.8 collective-permute-done.7.right
  49.8 1.4 %collective-permute-start.8 = (f32[16,384]{1,0:T(8,128)S(1)}, f32[16,384]{1,0:T(8,128)S(1)}, u32[]{:S(2)}, u32[]{:S(2)}) collective-permute-start(f32[16,384]{1,0:T(8,128)S(1)} %shard_map.76.left), channel_id=1, source_target_pairs={{0,8},{4,12},{8,0},{12,4},{16,24},{20,28},{24,16},{28,20},{32,40},... | collective-permute-start | bytes 73736 | tf_op jit(solution)/shard_map/ppermute | solution.py:478
  51.2 1.2 %collective-permute-done.8.right = f32[16,384]{1,0:T(8,128)S(1)} collective-permute-done((f32[16,384]{1,0:T(8,128)S(1)}, f32[16,384]{1,0:T(8,128)S(1)}, u32[]{:S(2)}, u32[]{:S(2)}) %collective-permute-start.8) | collective-permute-done | bytes 24608 | tf_op jit(solution)/shard_map/ppermute | solution.py:478
  52.6 3.3 %shard_map.78 = (f32[8,32,1024]{2,1,0:T(8,128)S(1)}, f32[32,1024]{1,0:T(8,128)}, f32[32,1024]{1,0:T(8,128)}, f32[16,128]{1,0:T(8,128)S(1)}, f32[16,128]{1,0:T(8,128)S(1)}) custom-call(f32[8,32,1024]{2,1,0:T(8,128)S(1)} %get-tuple-element.121.kept_in, s32[1]{0:T(128)} %bitcast.1.position, ...), custom_call_target="tpu_custom_call", output_to_operand_aliasing={{0}: (0, {})} | custom-call | flops 1000000000 | bytes 4194304 | tf_op jit(solution)/shard_map/pallas_call | solution.py:592
  56.0 3.2 %collective-permute-start.13 = (f32[16,128]{1,0:T(8,128)S(1)}, f32[16,128]{1,0:T(8,128)S(1)}, u32[]{:S(2)}, u32[]{:S(2)}) collective-permute-start(f32[16,128]{1,0:T(8,128)S(1)} %get-tuple-element.131), channel_id=1, source_target_pairs={{0,4},{4,0},{8,12},{12,8},{16,20},{20,16},{24,28},{28,24},{32,36},... | collective-permute-start | bytes 24584 | tf_op jit(solution)/shard_map/ppermute | solution.py:478
  59.2 0.8 collective-permute-done.13.late_got
  60.1 4.9 %collective-permute-done.14.right = f32[16,512]{1,0:T(8,128)S(1)} collective-permute-done((f32[16,512]{1,0:T(8,128)S(1)}, f32[16,512]{1,0:T(8,128)S(1)}, u32[]{:S(2)}, u32[]{:S(2)}) %collective-permute-start.14) | collective-permute-done | bytes 32800 | tf_op jit(solution)/shard_map/ppermute | solution.py:478
  65.6 3.7 %collective-permute-done.15.right = f32[16,512]{1,0:T(8,128)S(1)} collective-permute-done((f32[16,512]{1,0:T(8,128)S(1)}, f32[16,512]{1,0:T(8,128)S(1)}, u32[]{:S(2)}, u32[]{:S(2)}) %collective-permute-start.15) | collective-permute-done | bytes 32800 | tf_op jit(solution)/shard_map/ppermute | solution.py:478
  69.3 6.0 %collective-permute-start.16 = (f32[16,384]{1,0:T(8,128)S(1)}, f32[16,384]{1,0:T(8,128)S(1)}, u32[]{:S(2)}, u32[]{:S(2)}) collective-permute-start(f32[16,384]{1,0:T(8,128)S(1)} %slice.8.mine), channel_id=1, source_target_pairs={{0,4},{4,0},{8,12},{12,8},{16,20},{20,16},{24,28},{28,24},{32,36},... | collective-permute-start | bytes 73736 | tf_op jit(solution)/shard_map/ppermute | solution.py:478
  75.4 0.7 collective-permute-done.16.other
  76.2 3.6 %shard_map.83 = (f32[96,256]{1,0:T(8,128)S(1)}, f32[96,256]{1,0:T(8,128)S(1)}, f32[288,256]{1,0:T(8,128)S(1)}, f32[288,256]{1,0:T(8,128)S(1)}, f32[32,256]{1,0:T(8,128)S(1)}) custom-call(s32[1]{0:T(128)} %bitcast.1.position, f32[16,384]{1,0:T(8,128)S(1)} %slice.8.mine, f32[16,384]{1,0:T(8,128)S(1)} %collective-permute-done.16.other), custom_call_target="tpu_custom_call" | custom-call | flops 3000000000 | bytes 4194304 | tf_op jit(solution)/shard_map/pallas_call | solution.py:621
  80.1 4.1 %shard_map.85 = (f32[160,256]{1,0:T(8,128)S(1)}, f32[160,256]{1,0:T(8,128)S(1)}, f32[224,256]{1,0:T(8,128)S(1)}, f32[224,256]{1,0:T(8,128)S(1)}, f32[96,256]{1,0:T(8,128)S(1)}) custom-call(f32[96,256]{1,0:T(8,128)S(1)} %get-tuple-element.138.refs_0_, f32[96,256]{1,0:T(8,128)S(1)} %get-tuple-element.139.refs_1_, f32[288,256]{1,0:T(8,128)S(1)} %get-tuple-element.140.refs_2_, ...), custom_call_target="tpu_custom_call" | custom-call | flops 3000000000 | bytes 4194304 | tf_op jit(solution)/shard_map/pallas_call | solution.py:621
  84.4 2.8 %shard_map.87 = (f32[224,256]{1,0:T(8,128)S(1)}, f32[32,256]{1,0:T(8,128)S(1)}, f32[224,256]{1,0:T(8,128)S(1)}, f32[160,256]{1,0:T(8,128)S(1)}, f32[160,256]{1,0:T(8,128)S(1)}) custom-call(f32[160,256]{1,0:T(8,128)S(1)} %get-tuple-element.149.refs_0_.direction, f32[160,256]{1,0:T(8,128)S(1)} %get-tuple-element.150.refs_1_, ...), custom_call_target="tpu_custom_call" | custom-call | flops 3000000000 | bytes 4194304 | tf_op jit(solution)/shard_map/pallas_call | solution.py:621
  87.2 1.4 %collective-permute-start.20 = (f32[16,128]{1,0:T(8,128)S(1)}, f32[16,128]{1,0:T(8,128)S(1)}, u32[]{:S(2)}, u32[]{:S(2)}) collective-permute-start(f32[16,128]{1,0:T(8,128)S(1)} %shard_map.88.mine_late), channel_id=1, source_target_pairs={{0,4},{4,0},{8,12},{12,8},{16,20},{20,16},{24,28},{28,24},{32,36},... | collective-permute-start | bytes 24584 | tf_op jit(solution)/shard_map/ppermute | solution.py:478
  88.7 0.8 collective-permute-done.20.other_late
  89.5 9.7 %shard_map.89 = (f32[4,32,1024]{2,1,0:T(8,128)}, f32[4,32,32]{2,1,0:T(8,128)}) custom-call(s32[1]{0:T(128)} %bitcast.node, s32[1]{0:T(128)} %bitcast.1.position, f32[2,16,8]{2,1,0:T(8,128)S(1)} %copy-done.2, f32[16,384]{1,0:T(8,128)S(1)} %slice.8.mine, f32[16,384]{1,0:T(8,128)S(1)} %collective-permute-done.16.other, f32[16,128]{1,0:T(8,128)S(1)} %shard_map.88.mine_late, ...), custom_call_target="tpu_custom_call" | custom-call | tf_op jit(solution)/shard_map/pallas_call | solution.py:631
  (44 shorter events, 3.2 us)
Async XLA Ops:
  0.6 7.5 %copy-start.1 = (f32[32,1024]{1,0:T(8,128)S(1)}, f32[32,1024]{1,0:T(8,128)}, u32[]{:S(2)}) copy-start(f32[32,1024]{1,0:T(8,128)} %k0.1) | copy-start | bytes 393220
  0.6 7.5 %copy-start = (f32[8,3,128,128]{3,2,1,0:T(8,128)S(1)}, f32[8,3,128,128]{3,2,1,0:T(8,128)}, u32[]{:S(2)}) copy-start(f32[8,3,128,128]{3,2,1,0:T(8,128)} %coup.1) | copy-start | bytes 4718596
  0.6 7.5 %copy-start.3 = (s32[8,3]{0,1:T(4,128)S(1)}, s32[8,3]{0,1:T(4,128)}, u32[]{:S(2)}) copy-start(s32[8,3]{0,1:T(4,128)} %param.8) | copy-start | bytes 292
  3.7 4.4 %collective-permute-start = (f32[32,512]{1,0:T(8,128)}, f32[32,512]{1,0:T(8,128)S(1)}, u32[]{:S(2)}, u32[]{:S(2)}) collective-permute-start(f32[32,512]{1,0:T(8,128)} %get-tuple-element.84), channel_id=1, source_target_pairs={{0,4},{4,0},{8,12},{12,8},{16,20},{20,16},{24,28},{28,24},{32,36},... | collective-permute-start | bytes 196616 | tf_op jit(solution)/shard_map/ppermute | solution.py:478
  7.0 4.7 %collective-permute-start.1 = (f32[32,512]{1,0:T(8,128)}, f32[32,512]{1,0:T(8,128)S(1)}, u32[]{:S(2)}, u32[]{:S(2)}) collective-permute-start(f32[32,512]{1,0:T(8,128)} %get-tuple-element.87), channel_id=1, source_target_pairs={{0,252},{4,8},{8,4},{12,16},{16,12},{20,24},{24,20},{28,32},{32,28... | collective-permute-start | bytes 196616 | tf_op jit(solution)/shard_map/ppermute | solution.py:478
  8.1 1.0 %copy-start.4 = (f32[8,128,128]{2,1,0:T(8,128)S(1)}, f32[8,128,128]{2,1,0:T(8,128)}, u32[]{:S(2)}) copy-start(f32[8,128,128]{2,1,0:T(8,128)} %diag.1) | copy-start | bytes 1572868
  11.8 8.3 %collective-permute-start.2 = (f32[10,128,128]{2,1,0:T(8,128)S(1)}, f32[10,128,128]{2,1,0:T(8,128)S(1)}, u32[]{:S(2)}, u32[]{:S(2)}) collective-permute-start(f32[10,128,128]{2,1,0:T(8,128)S(1)} %get-tuple-element.98), channel_id=1, source_target_pairs={{0,4},{4,8},{8,12},{12,16},{16,20},{20,24},{24,28},{28,32},{32,36}... | collective-permute-start | bytes 1966088 | tf_op jit(solution)/shard_map/ppermute | solution.py:478
  14.6 6.2 %collective-permute-start.3 = (f32[64,512]{1,0:T(8,128)S(1)}, f32[64,512]{1,0:T(8,128)S(1)}, u32[]{:S(2)}, u32[]{:S(2)}) collective-permute-start(f32[64,512]{1,0:T(8,128)S(1)} %get-tuple-element.100), channel_id=1, source_target_pairs={{0,4},{4,0},{8,12},{12,8},{16,20},{20,16},{24,28},{28,24},{32,36},... | collective-permute-start | bytes 393224 | tf_op jit(solution)/shard_map/ppermute | solution.py:478
  19.6 4.7 %collective-permute-start.4 = (f32[64,512]{1,0:T(8,128)S(1)}, f32[64,512]{1,0:T(8,128)S(1)}, u32[]{:S(2)}, u32[]{:S(2)}) collective-permute-start(f32[64,512]{1,0:T(8,128)S(1)} %get-tuple-element.101), channel_id=1, source_target_pairs={{0,252},{4,8},{8,4},{12,16},{16,12},{20,24},{24,20},{28,32},{32,28... | collective-permute-start | bytes 393224 | tf_op jit(solution)/shard_map/ppermute | solution.py:478
  27.9 9.0 %collective-permute-start.5 = (f32[64,512]{1,0:T(8,128)S(1)}, f32[64,512]{1,0:T(8,128)S(1)}, u32[]{:S(2)}, u32[]{:S(2)}) collective-permute-start(f32[64,512]{1,0:T(8,128)S(1)} %get-tuple-element.111), channel_id=1, source_target_pairs={{0,4},{4,0},{8,12},{12,8},{16,20},{20,16},{24,28},{28,24},{32,36},... | collective-permute-start | bytes 393224 | tf_op jit(solution)/shard_map/ppermute | solution.py:478
  35.8 4.4 %collective-permute-start.6 = (f32[64,512]{1,0:T(8,128)S(1)}, f32[64,512]{1,0:T(8,128)S(1)}, u32[]{:S(2)}, u32[]{:S(2)}) collective-permute-start(f32[64,512]{1,0:T(8,128)S(1)} %get-tuple-element.112), channel_id=1, source_target_pairs={{0,252},{4,8},{8,4},{12,16},{16,12},{20,24},{24,20},{28,32},{32,28... | collective-permute-start | bytes 393224 | tf_op jit(solution)/shard_map/ppermute | solution.py:478
  43.7 8.7 %collective-permute-start.9 = (f32[64,512]{1,0:T(8,128)S(1)}, f32[64,512]{1,0:T(8,128)S(1)}, u32[]{:S(2)}, u32[]{:S(2)}) collective-permute-start(f32[64,512]{1,0:T(8,128)S(1)} %get-tuple-element.118), channel_id=1, source_target_pairs={{0,4},{4,0},{8,12},{12,8},{16,20},{20,16},{24,28},{28,24},{32,36},... | collective-permute-start | bytes 393224 | tf_op jit(solution)/shard_map/ppermute | solution.py:478
  47.4 5.1 %collective-permute-start.10 = (f32[64,512]{1,0:T(8,128)S(1)}, f32[64,512]{1,0:T(8,128)S(1)}, u32[]{:S(2)}, u32[]{:S(2)}) collective-permute-start(f32[64,512]{1,0:T(8,128)S(1)} %get-tuple-element.119), channel_id=1, source_target_pairs={{0,252},{4,8},{8,4},{12,16},{16,12},{20,24},{24,20},{28,32},{32,28... | collective-permute-start | bytes 393224 | tf_op jit(solution)/shard_map/ppermute | solution.py:478
  48.4 1.4 %collective-permute-start.7 = (f32[16,384]{1,0:T(8,128)S(1)}, f32[16,384]{1,0:T(8,128)S(1)}, u32[]{:S(2)}, u32[]{:S(2)}) collective-permute-start(f32[16,384]{1,0:T(8,128)S(1)} %get-tuple-element.117), channel_id=1, source_target_pairs={{0,4},{4,0},{8,12},{12,8},{16,20},{20,16},{24,28},{28,24},{32,36},... | collective-permute-start | bytes 73736 | tf_op jit(solution)/shard_map/ppermute | solution.py:478
  49.8 2.7 %collective-permute-start.8 = (f32[16,384]{1,0:T(8,128)S(1)}, f32[16,384]{1,0:T(8,128)S(1)}, u32[]{:S(2)}, u32[]{:S(2)}) collective-permute-start(f32[16,384]{1,0:T(8,128)S(1)} %shard_map.76.left), channel_id=1, source_target_pairs={{0,8},{4,12},{8,0},{12,4},{16,24},{20,28},{24,16},{28,20},{32,40},... | collective-permute-start | bytes 73736 | tf_op jit(solution)/shard_map/ppermute | solution.py:478
  52.5 3.4 %collective-permute-start.11 = (f32[16,384]{1,0:T(8,128)S(1)}, f32[16,384]{1,0:T(8,128)S(1)}, u32[]{:S(2)}, u32[]{:S(2)}) collective-permute-start(f32[16,384]{1,0:T(8,128)S(1)} %shard_map.77.left), channel_id=1, source_target_pairs={{0,64},{4,68},{8,72},{12,76},{16,80},{20,84},{24,88},{28,92},{32,9... | collective-permute-start | bytes 73736 | tf_op jit(solution)/shard_map/ppermute | solution.py:478
  55.9 4.1 %collective-permute-start.12 = (f32[16,384]{1,0:T(8,128)S(1)}, f32[16,384]{1,0:T(8,128)S(1)}, u32[]{:S(2)}, u32[]{:S(2)}) collective-permute-start(f32[16,384]{1,0:T(8,128)S(1)} %shard_map.79.early), channel_id=1, source_target_pairs={{0,16},{4,20},{8,24},{12,28},{16,0},{20,4},{24,8},{28,12},{32,48},... | collective-permute-start | bytes 73736 | tf_op jit(solution)/shard_map/ppermute | solution.py:478
  56.0 4.0 %collective-permute-start.13 = (f32[16,128]{1,0:T(8,128)S(1)}, f32[16,128]{1,0:T(8,128)S(1)}, u32[]{:S(2)}, u32[]{:S(2)}) collective-permute-start(f32[16,128]{1,0:T(8,128)S(1)} %get-tuple-element.131), channel_id=1, source_target_pairs={{0,4},{4,0},{8,12},{12,8},{16,20},{20,16},{24,28},{28,24},{32,36},... | collective-permute-start | bytes 24584 | tf_op jit(solution)/shard_map/ppermute | solution.py:478
  60.0 5.0 %collective-permute-start.14 = (f32[16,512]{1,0:T(8,128)S(1)}, f32[16,512]{1,0:T(8,128)S(1)}, u32[]{:S(2)}, u32[]{:S(2)}) collective-permute-start(f32[16,512]{1,0:T(8,128)S(1)} %shard_map.80.left), channel_id=1, source_target_pairs={{0,48},{4,52},{8,56},{12,60},{16,32},{20,36},{24,40},{28,44},{32,1... | collective-permute-start | bytes 98312 | tf_op jit(solution)/shard_map/ppermute | solution.py:478
  65.1 4.3 %collective-permute-start.15 = (f32[16,512]{1,0:T(8,128)S(1)}, f32[16,512]{1,0:T(8,128)S(1)}, u32[]{:S(2)}, u32[]{:S(2)}) collective-permute-start(f32[16,512]{1,0:T(8,128)S(1)} %shard_map.81.left), channel_id=1, source_target_pairs={{0,192},{4,196},{8,200},{12,204},{16,208},{20,212},{24,216},{28,22... | collective-permute-start | bytes 98312 | tf_op jit(solution)/shard_map/ppermute | solution.py:478
  69.3 6.8 %collective-permute-start.16 = (f32[16,384]{1,0:T(8,128)S(1)}, f32[16,384]{1,0:T(8,128)S(1)}, u32[]{:S(2)}, u32[]{:S(2)}) collective-permute-start(f32[16,384]{1,0:T(8,128)S(1)} %slice.8.mine), channel_id=1, source_target_pairs={{0,4},{4,0},{8,12},{12,8},{16,20},{20,16},{24,28},{28,24},{32,36},... | collective-permute-start | bytes 73736 | tf_op jit(solution)/shard_map/ppermute | solution.py:478
  75.3 4.5 %collective-permute-start.17 = (f32[16,128]{1,0:T(8,128)S(1)}, f32[16,128]{1,0:T(8,128)S(1)}, u32[]{:S(2)}, u32[]{:S(2)}) collective-permute-start(f32[16,128]{1,0:T(8,128)S(1)} %slice.9.left), channel_id=1, source_target_pairs={{0,64},{4,68},{8,72},{12,76},{16,80},{20,84},{24,88},{28,92},{32,9... | collective-permute-start | bytes 24584 | tf_op jit(solution)/shard_map/ppermute | solution.py:478
  79.8 4.5 %collective-permute-start.18 = (f32[16,128]{1,0:T(8,128)S(1)}, f32[16,128]{1,0:T(8,128)S(1)}, u32[]{:S(2)}, u32[]{:S(2)}) collective-permute-start(f32[16,128]{1,0:T(8,128)S(1)} %shard_map.84.left), channel_id=1, source_target_pairs={{0,16},{4,20},{8,24},{12,28},{16,0},{20,4},{24,8},{28,12},{32,48},... | collective-permute-start | bytes 24584 | tf_op jit(solution)/shard_map/ppermute | solution.py:478
  84.3 5.2 %copy-start.2 = (f32[2,16,8]{2,1,0:T(8,128)S(1)}, f32[2,16,8]{2,1,0:T(8,128)}, u32[]{:S(2)}) copy-start(f32[2,16,8]{2,1,0:T(8,128)} %constant.11.clone.weights) | copy-start | bytes 3076
  84.3 2.9 %collective-permute-start.19 = (f32[16,128]{1,0:T(8,128)S(1)}, f32[16,128]{1,0:T(8,128)S(1)}, u32[]{:S(2)}, u32[]{:S(2)}) collective-permute-start(f32[16,128]{1,0:T(8,128)S(1)} %shard_map.86.left), channel_id=1, source_target_pairs={{0,8},{4,12},{8,0},{12,4},{16,24},{20,28},{24,16},{28,20},{32,40},... | collective-permute-start | bytes 24584 | tf_op jit(solution)/shard_map/ppermute | solution.py:478
  87.2 2.3 %collective-permute-start.20 = (f32[16,128]{1,0:T(8,128)S(1)}, f32[16,128]{1,0:T(8,128)S(1)}, u32[]{:S(2)}, u32[]{:S(2)}) collective-permute-start(f32[16,128]{1,0:T(8,128)S(1)} %shard_map.88.mine_late), channel_id=1, source_target_pairs={{0,4},{4,0},{8,12},{12,8},{16,20},{20,16},{24,28},{28,24},{32,36},... | collective-permute-start | bytes 24584 | tf_op jit(solution)/shard_map/ppermute | solution.py:478
